TPU v7x, 32 devices: a whole 2x2x4 slice. The times are simulated.
32 devices in a mesh: pipe: 4 (over y, x), dp: 8 (over z, core).
Axes of the slice: x: 2, y: 2, z: 4, core: 2. Of those that a mesh axis runs over, the one named last changes fastest.
Arguments:
- block_input: bfloat16 [2, 3072, 2048], P(None, 'dp', 'pipe'), may hold values from -6 to 6
- cotangent: bfloat16 [2, 3072, 2048], P(None, 'dp', 'pipe'), may hold values from -6 to 6
- weight_wide: bfloat16 [4, 2048, 512], P('pipe'), may hold values from -0.125 to 0.125
- weight_taps: bfloat16 [4, 2304, 512], P('pipe'), may hold values from -0.09375 to 0.09375
- norm_mid: float32 [4, 2, 512], P('pipe'), may hold values from 0.5 to 1.5
- norm_out: float32 [4, 2, 1024], P('pipe'), may hold values from 0.5 to 1.5
- group_counts: int32 [2, 8, 4], replicated, may hold values from 0 to 96, as said below
Outputs:
- mixed: bfloat16 [2, 3072, 2048], P(None, 'dp', 'pipe')
- grad_input: float32 [2, 3072, 2048], P(None, 'dp', 'pipe')
- grad_wide: float32 [4, 2048, 512], P('pipe')
- grad_taps: float32 [4, 2304, 512], P('pipe')
- grad_mid: float32 [4, 2, 512], P('pipe')
- grad_out: float32 [4, 2, 1024], P('pipe')
Inputs may be any that keep to these rules, and one draw needn't show every extreme that they name: group_counts[m, j] are counts of maps of 49, 36 and 25 pixels and of 4-pixel tiles that together fill at most 384 rows; some device holds 96 tiles.
All inputs are finite; a program needn't handle non-finite values.
Results may differ from a plain program's by a relative error of at most 0.023.
Values may be sent and summed in bfloat16 or wider, within the bound.
A program may use at most 320 MiB of HBM per device.

v0:
```python
import jax
import jax.numpy as jnp
from jax import lax
from jax.sharding import PartitionSpec as P

epsilon = 1e-05
float_type = jnp.float32
half_type = jnp.bfloat16


def passed_along(block, axis, distance):
    devices = range(lax.axis_size(axis))
    route = [(i - distance, i) for i in devices if i - distance in devices]
    return lax.ppermute(block, axis, route)


def as_sent(array):

    def short(part):
        return part.astype(jnp.bfloat16) if part.dtype == jnp.float32 else part

    return jax.tree.map(short, array)


def neighbour_table(group_row, row_count):
    row_index = jnp.arange(row_count, dtype=jnp.int32)
    first_end = 49 * group_row[0]
    second_end = first_end + 36 * group_row[1]
    third_end = second_end + 25 * group_row[2]
    fourth_end = third_end + 4 * group_row[3]
    side_length = jnp.where(
        row_index < first_end,
        7,
        jnp.where(
            row_index < second_end,
            6,
            jnp.where(row_index < third_end, 5, jnp.where(row_index < fourth_end, 2, 1)),
        ),
    ).astype(jnp.int32)
    group_start = jnp.where(
        row_index < first_end,
        0,
        jnp.where(
            row_index < second_end,
            first_end,
            jnp.where(
                row_index < third_end,
                second_end,
                jnp.where(row_index < fourth_end, third_end, row_index),
            ),
        ),
    )
    within = (row_index - group_start) % (side_length * side_length)
    image_start = row_index - within
    map_row = within // side_length
    map_column = within % side_length
    inside = row_index < fourth_end
    neighbours = []
    usable_list = []
    for shift_row in (-1, 0, 1):
        for shift_column in (-1, 0, 1):
            new_row = map_row + shift_row
            new_column = map_column + shift_column
            usable = (
                inside
                & (new_row >= 0)
                & (new_row < side_length)
                & (new_column >= 0)
                & (new_column < side_length)
            )
            neighbours.append(
                jnp.where(usable, image_start + new_row * side_length + new_column, 0)
            )
            usable_list.append(usable)
    return (
        jnp.stack(neighbours, 1),
        jnp.stack(usable_list, 1).astype(float_type),
        inside.astype(float_type),
    )


def gather_taps(hidden, neighbour, usable, tap_list):
    blocks = [
        jnp.take(hidden, neighbour[:, tap_id], axis=0)
        * usable[:, tap_id, None].astype(hidden.dtype)
        for tap_id in tap_list
    ]
    return jnp.concatenate(blocks, 1)


def return_taps(blocks, neighbour, usable, tap_list, channels):
    summed = jnp.zeros((blocks.shape[0], channels), float_type)
    for position, tap_id in enumerate(tap_list):
        mirror = 8 - tap_id
        block_part = blocks[:, position * channels : (position + 1) * channels]
        summed = (
            summed + jnp.take(block_part, neighbour[:, mirror], axis=0) * usable[:, mirror, None]
        )
    return summed


def silu_slope(values):
    logistic = jax.nn.sigmoid(values)
    return logistic * (1.0 + values * (1.0 - logistic))


def store_at(buffer, value, index_now, active):
    return jnp.where(active, lax.dynamic_update_index_in_dim(buffer, value, index_now, 0), buffer)


def take_at(buffer, index_now):
    return lax.dynamic_index_in_dim(buffer, index_now, 0, keepdims=False)


def moments(values, inside, pixel_total):
    masked = values * inside[:, None]
    mean_value = lax.psum(jnp.sum(masked, 0), "dp") / pixel_total
    centred = (values - mean_value) * inside[:, None]
    variance = lax.psum(jnp.sum(centred * centred, 0), "dp") / pixel_total
    return jnp.stack([mean_value, lax.rsqrt(variance + epsilon)])


def norm_sums(upstream, normed):
    return lax.psum(jnp.stack([jnp.sum(upstream * normed, 0), jnp.sum(upstream, 0)]), "dp")


def norm_back(upstream, normed, sums, gain_row, inverse, inside, pixel_total):
    return (
        inside[:, None]
        * gain_row
        * inverse
        * (upstream - sums[1] / pixel_total - normed * sums[0] / pixel_total)
    )


def forward_send(fields):
    return (
        passed_along(fields[0], "pipe", 1),
        passed_along(fields[1].astype(jnp.bfloat16), "pipe", 1).astype(jnp.float32),
        passed_along(fields[2], "pipe", 1),
        passed_along(fields[3].astype(jnp.bfloat16), "pipe", 1).astype(jnp.float32),
    )


def backward_send(fields):
    return (
        passed_along(fields[0], "pipe", -1),
        passed_along(as_sent(fields[1]), "pipe", -1),
        passed_along(fields[2], "pipe", -1),
        passed_along(fields[3].astype(jnp.bfloat16), "pipe", -1).astype(jnp.float32),
    )


def local(block_input, cotangent, weight_wide, weight_taps, norm_mid, norm_out, group_counts):
    micro_total = block_input.shape[0]
    row_count = block_input.shape[1]
    wide_weight = weight_wide[0]
    tap_weight = weight_taps[0]
    mid_gains = norm_mid[0]
    own_out_gains = norm_out[0]
    model_width = wide_weight.shape[0]
    channels = wide_weight.shape[1]
    tap_rows = tap_weight.shape[0]
    half_width = model_width // 2
    split_at = channels // 2
    sections = lax.axis_size("pipe")
    section = lax.axis_index("pipe")
    is_front = section % 2 == 0
    first_layer = section < 2
    data_index = lax.axis_index("dp")
    pixel_sizes = jnp.array([49, 36, 25, 4], jnp.int32)
    pixel_totals = jnp.sum(group_counts * pixel_sizes, axis=(1, 2)).astype(float_type)
    own_counts = lax.dynamic_index_in_dim(group_counts, data_index, 1, keepdims=False)
    tables, usables, insides = jax.vmap(lambda counts_row: neighbour_table(counts_row, row_count))(
        own_counts
    )
    front_taps = list(range(5))
    back_taps = list(range(4, 9))
    zero_mid = jnp.zeros((row_count, channels), float_type)
    zero_wide = jnp.zeros((row_count, model_width), float_type)
    zero_patch = jnp.zeros((row_count, tap_rows), half_type)
    gathered = lax.all_gather(block_input, "pipe", axis=2, tiled=True)

    def section_forward(
        input_rows,
        recv_hidden,
        recv_partial,
        neighbour,
        usable,
        inside,
        residual,
        wide_gains,
        mid_stat_fn,
        wide_stat_fn,
    ):

        def front_first():
            return (jnp.dot(input_rows, wide_weight, preferred_element_type=float_type), zero_patch)

        def back_first():
            patches = gather_taps(recv_hidden, neighbour, usable, back_taps)[:, split_at:]
            return (
                recv_partial + jnp.dot(patches, tap_weight, preferred_element_type=float_type),
                patches,
            )

        mid_pre, back_patches = lax.cond(is_front, front_first, back_first)
        mid_stats = mid_stat_fn(mid_pre)
        mid_normed = (mid_pre - mid_stats[0]) * mid_stats[1]
        hidden_mid = (
            inside[:, None] * jax.nn.silu(mid_gains[0] * mid_normed + mid_gains[1])
        ).astype(half_type)

        def front_second():
            patches = gather_taps(hidden_mid, neighbour, usable, front_taps)[:, :tap_rows]
            return (
                patches,
                jnp.dot(patches, tap_weight, preferred_element_type=float_type),
                zero_wide,
            )

        def back_second():
            wide_pre = lax.dot_general(
                hidden_mid, wide_weight, (((1,), (1,)), ((), ())), preferred_element_type=float_type
            )
            return (back_patches, zero_mid, wide_pre)

        patches, partial_value, wide_pre = lax.cond(is_front, front_second, back_second)
        wide_stats = wide_stat_fn(wide_pre)
        wide_normed = (wide_pre - wide_stats[0]) * wide_stats[1]
        branch = wide_gains[0] * wide_normed + wide_gains[1]
        summed = branch + residual
        return (
            hidden_mid,
            partial_value,
            patches,
            mid_normed,
            wide_normed,
            branch,
            summed,
            mid_stats,
            wide_stats,
        )

    message = (
        jnp.zeros((row_count, channels), half_type),
        zero_mid,
        jnp.zeros((row_count, model_width), half_type),
        jnp.zeros((2, half_width), float_type),
    )
    input_store = jnp.zeros((micro_total, row_count, model_width), half_type)
    hidden_store = jnp.zeros((micro_total, row_count, channels), half_type)
    partial_store = jnp.zeros((micro_total, row_count, channels), float_type)
    mid_stat_store = jnp.zeros((micro_total, 2, channels), float_type)
    wide_stat_store = jnp.zeros((micro_total, 2, model_width), float_type)
    branch_store = jnp.zeros((micro_total, row_count, model_width), float_type)
    wide_gains = jnp.zeros((2, model_width), float_type)
    for tick_step in range(micro_total + sections - 1):
        micro_index = tick_step - section
        active = (micro_index >= 0) & (micro_index < micro_total)
        micro_slot = jnp.clip(micro_index, 0, micro_total - 1)
        recv_hidden = message[0]
        recv_partial = message[1].astype(float_type)
        recv_out = message[2]
        recv_gain = message[3].astype(float_type)
        own_input = take_at(gathered, micro_slot)
        input_rows = jnp.where(section == 0, own_input, recv_out)
        neighbour = take_at(tables, micro_slot)
        usable = take_at(usables, micro_slot)
        inside = take_at(insides, micro_slot)
        pixel_total = take_at(pixel_totals, micro_slot)
        residual = jnp.where(first_layer, own_input.astype(float_type), 0.0)
        wide_gains = jnp.concatenate([recv_gain, own_out_gains], 1)
        results = section_forward(
            input_rows,
            recv_hidden,
            recv_partial,
            neighbour,
            usable,
            inside,
            residual,
            wide_gains,
            lambda values: moments(values, inside, pixel_total),
            lambda values: moments(values, inside, pixel_total),
        )
        (
            hidden_mid,
            partial_value,
            patches,
            mid_normed,
            wide_normed,
            branch,
            summed,
            mid_stats,
            wide_stats,
        ) = results
        out_rows = (inside[:, None] * jax.nn.silu(summed)).astype(half_type)
        input_store = store_at(input_store, input_rows, micro_slot, active)
        hidden_store = store_at(hidden_store, recv_hidden, micro_slot, active)
        partial_store = store_at(partial_store, recv_partial, micro_slot, active)
        mid_stat_store = store_at(mid_stat_store, mid_stats, micro_slot, active)
        wide_stat_store = store_at(wide_stat_store, wide_stats, micro_slot, active)
        branch_store = store_at(branch_store, branch, micro_slot, active)
        message = forward_send((hidden_mid, partial_value, out_rows, own_out_gains))
    outer_term = jnp.where(
        section == sections - 1,
        branch_store,
        jnp.where(section == sections - 2, input_store.astype(float_type), 0.0),
    )
    summed_two = lax.psum_scatter(
        outer_term.astype(jnp.bfloat16), "pipe", scatter_dimension=2, tiled=True
    ).astype(jnp.float32)
    mixed = (insides[:, :, None] * jax.nn.silu(summed_two)).astype(half_type)
    grad_last = (
        cotangent.astype(float_type) * insides[:, :, None] * silu_slope(summed_two)
    ).astype(half_type)
    grad_full = lax.all_gather(grad_last, "pipe", axis=2, tiled=True)
    back_message = (
        jnp.zeros((row_count, channels), half_type),
        zero_mid,
        jnp.zeros((row_count, model_width), half_type),
        jnp.zeros((2, half_width), float_type),
    )
    sum_wide = jnp.zeros((model_width, channels), float_type)
    sum_taps = jnp.zeros((tap_rows, channels), float_type)
    sum_mid = jnp.zeros((2, channels), float_type)
    sum_out = jnp.zeros((2, half_width), float_type)
    conv_store = jnp.zeros((micro_total, row_count, model_width), half_type)
    for tick_step in range(micro_total + sections - 1):
        micro_index = tick_step - (sections - 1 - section)
        active = (micro_index >= 0) & (micro_index < micro_total)
        micro_slot = jnp.clip(micro_index, 0, micro_total - 1)
        recv_second = back_message[0]
        recv_hidden_grad = back_message[1].astype(float_type)
        recv_conv = back_message[2]
        recv_gain_grad = back_message[3].astype(float_type)
        neighbour = take_at(tables, micro_slot)
        usable = take_at(usables, micro_slot)
        inside = take_at(insides, micro_slot)
        pixel_total = take_at(pixel_totals, micro_slot)
        input_rows = take_at(input_store, micro_slot)
        mid_stats = take_at(mid_stat_store, micro_slot)
        wide_stats = take_at(wide_stat_store, micro_slot)
        residual = jnp.where(first_layer, take_at(gathered, micro_slot).astype(float_type), 0.0)
        rebuilt = section_forward(
            input_rows,
            take_at(hidden_store, micro_slot),
            take_at(partial_store, micro_slot),
            neighbour,
            usable,
            inside,
            residual,
            wide_gains,
            lambda values: mid_stats,
            lambda values: wide_stats,
        )
        hidden_mid = rebuilt[0]
        patches = rebuilt[2]
        mid_normed = rebuilt[3]
        wide_normed = rebuilt[4]
        summed = rebuilt[6]
        grad_pre = take_at(grad_full, micro_slot).astype(float_type)
        grad_carry = (
            (grad_pre + recv_conv.astype(float_type)) * inside[:, None] * silu_slope(summed)
        ).astype(half_type)
        grad_wide_pre = jnp.where(first_layer, grad_carry.astype(float_type), grad_pre)
        wide_sums = norm_sums(grad_wide_pre, wide_normed)

        def back_middle():
            grad_third = norm_back(
                grad_wide_pre,
                wide_normed,
                wide_sums,
                wide_gains[0],
                wide_stats[1],
                inside,
                pixel_total,
            ).astype(half_type)
            wide_part = lax.dot_general(
                grad_third, hidden_mid, (((0,), (0,)), ((), ())), preferred_element_type=float_type
            )
            grad_hidden = jnp.dot(grad_third, wide_weight, preferred_element_type=float_type)
            return (grad_hidden, wide_part, jnp.zeros((tap_rows, channels), float_type))

        def front_middle():
            grad_patch = lax.dot_general(
                recv_second, tap_weight, (((1,), (1,)), ((), ())), preferred_element_type=float_type
            )
            padded = jnp.pad(grad_patch, ((0, 0), (0, split_at)))
            grad_hidden = (
                return_taps(padded, neighbour, usable, front_taps, channels) + recv_hidden_grad
            )
            taps_part = lax.dot_general(
                patches, recv_second, (((0,), (0,)), ((), ())), preferred_element_type=float_type
            )
            return (grad_hidden, jnp.zeros((model_width, channels), float_type), taps_part)

        grad_hidden, wide_part, taps_part = lax.cond(is_front, front_middle, back_middle)
        grad_mid_pre = (
            grad_hidden * inside[:, None] * silu_slope(mid_gains[0] * mid_normed + mid_gains[1])
        )
        mid_sums = norm_sums(grad_mid_pre, mid_normed)
        grad_second = norm_back(
            grad_mid_pre, mid_normed, mid_sums, mid_gains[0], mid_stats[1], inside, pixel_total
        ).astype(half_type)

        def front_last():
            wide_more = lax.dot_general(
                input_rows, grad_second, (((0,), (0,)), ((), ())), preferred_element_type=float_type
            )
            conv_grad = lax.dot_general(
                grad_second,
                wide_weight,
                (((1,), (1,)), ((), ())),
                preferred_element_type=float_type,
            ).astype(half_type)
            return (wide_more, jnp.zeros((tap_rows, channels), float_type), zero_mid, conv_grad)

        def back_last():
            taps_more = lax.dot_general(
                patches, grad_second, (((0,), (0,)), ((), ())), preferred_element_type=float_type
            )
            grad_patch = lax.dot_general(
                grad_second, tap_weight, (((1,), (1,)), ((), ())), preferred_element_type=float_type
            )
            padded = jnp.pad(grad_patch, ((0, 0), (split_at, 0)))
            hidden_back = return_taps(padded, neighbour, usable, back_taps, channels)
            return (
                jnp.zeros((model_width, channels), float_type),
                taps_more,
                hidden_back,
                jnp.zeros((row_count, model_width), half_type),
            )

        wide_more, taps_more, hidden_back, conv_grad = lax.cond(is_front, front_last, back_last)
        sum_wide = sum_wide + jnp.where(active, wide_part + wide_more, 0.0)
        sum_taps = sum_taps + jnp.where(active, taps_part + taps_more, 0.0)
        sum_mid = sum_mid + jnp.where(active, mid_sums, 0.0)
        sum_out = sum_out + jnp.where(
            is_front, recv_gain_grad, jnp.where(active, wide_sums[:, half_width:], 0.0)
        )
        conv_store = store_at(
            conv_store, jnp.where(section == 0, conv_grad, grad_carry), micro_slot, active
        )
        gain_send = jnp.where(active, wide_sums[:, :half_width], 0.0)
        back_message = backward_send((grad_second, hidden_back, conv_grad, gain_send))
    inner_term = jnp.where(section < 2, conv_store.astype(float_type), 0.0)
    grad_input = lax.psum_scatter(
        inner_term.astype(jnp.bfloat16), "pipe", scatter_dimension=2, tiled=True
    ).astype(jnp.float32)
    wide_total, taps_total = lax.psum((sum_wide, sum_taps), "dp")
    return (mixed, grad_input, wide_total[None], taps_total[None], sum_mid[None], sum_out[None])


def solution(mesh):
    return jax.shard_map(
        local,
        mesh=mesh,
        in_specs=(
            P(None, "dp", "pipe"),
            P(None, "dp", "pipe"),
            P("pipe", None, None),
            P("pipe", None, None),
            P("pipe", None, None),
            P("pipe", None, None),
            P(),
        ),
        out_specs=(
            P(None, "dp", "pipe"),
            P(None, "dp", "pipe"),
            P("pipe", None, None),
            P("pipe", None, None),
            P("pipe", None, None),
            P("pipe", None, None),
        ),
        check_vma=False,
    )
```

profile of v0, /device:TPU:0, one launch (start us, length us, event | category | flops | bytes accessed | tf_op | source)
XLA Modules:
  0.0 1930.7 jit_solution(15252695898260999061)
XLA Ops:
  21.2 35.2 %all-gather.3.cloned.1.call-done = bf16[2,384,2048]{2,1,0:T(8,128)(2,1)} async-done(((bf16[2,384,512]{2,1,0:T(8,128)(2,1)}), bf16[2,384,2048]{2,1,0:T(8,128)(2,1)}) %all-gather.3.cloned.1.call-update) | async-done | bytes 3145744 | tf_op jit(solution)/shard_map/all_gather | solution.py:182
  64.2 16.4 psum.224
  97.0 17.8 conditional.31
  116.8 13.9 psum.226
  133.7 13.9 psum.227
  161.4 37.4 %collective-permute-done.2 = bf16[384,512]{1,0:T(8,128)(2,1)S(1)} collective-permute-done((bf16[384,512]{1,0:T(8,128)(2,1)}, bf16[384,512]{1,0:T(8,128)(2,1)S(1)}, u32[]{:S(2)}, u32[]{:S(2)}) %collective-permute-start.2) | collective-permute-done | bytes 393248 | tf_op jit(solution)/shard_map/ppermute | solution.py:14
  243.9 18.3 conditional.33
  264.2 13.9 psum.230
  281.2 13.9 psum.231
  316.0 36.7 %collective-permute-done.5 = bf16[384,512]{1,0:T(8,128)(2,1)S(1)} collective-permute-done((bf16[384,512]{1,0:T(8,128)(2,1)S(1)}, bf16[384,512]{1,0:T(8,128)(2,1)S(1)}, u32[]{:S(2)}, u32[]{:S(2)}) %collective-permute-start.5) | collective-permute-done | bytes 393248 | tf_op jit(solution)/shard_map/ppermute | solution.py:14
  394.1 26.0 %conditional.35 = (bf16[384,512]{1,0:T(8,128)(2,1)}, f32[384,2048]{1,0:T(8,128)S(1)}) conditional(s32[]{:T(128)} %convert_element_type.516, (bf16[384,512]{1,0:T(8,128)(2,1)S(1)}, bf16[2048,512]{1,0:T(8,128)(2,1)S(1)}) %tuple.938, (s32[384,9]{0,1:T(8,128)}, bf16[384,512]{1,0:T(8,128)(2,1)S(1)}, bf16[384,9]{0,1:T(8,128)(2,1)S(1)}, ...), branch_computations={%region_31.33_spmd, %region_32.34_spmd} | conditional | flops 910907264 | bytes 26636804 | solution.py:228
  422.0 13.9 psum.234
  439.0 13.9 psum.235
  478.8 31.4 %collective-permute-done.8 = bf16[384,512]{1,0:T(8,128)(2,1)S(1)} collective-permute-done((bf16[384,512]{1,0:T(8,128)(2,1)}, bf16[384,512]{1,0:T(8,128)(2,1)S(1)}, u32[]{:S(2)}, u32[]{:S(2)}) %collective-permute-start.8) | collective-permute-done | bytes 393248 | tf_op jit(solution)/shard_map/ppermute | solution.py:14
  518.3 14.2 psum.236
  534.6 14.3 psum.237
  551.7 25.9 %conditional.37 = (bf16[384,512]{1,0:T(8,128)(2,1)S(1)}, f32[384,2048]{1,0:T(8,128)S(1)}) conditional(s32[]{:T(128)} %convert_element_type.516, (bf16[384,512]{1,0:T(8,128)(2,1)S(1)}, bf16[2048,512]{1,0:T(8,128)(2,1)S(1)}) %tuple.940, (s32[384,9]{0,1:T(8,128)}, bf16[384,512]{1,0:T(8,128)(2,1)S(1)}, bf16[384,9]{0,1:T(8,128)(2,1)}, ...), branch_computations={%region_43.45_spmd, %region_44.46_spmd} | conditional | flops 910907264 | bytes 26636804 | solution.py:228
  580.1 14.6 psum.238
  599.1 14.6 psum.239
  640.1 26.9 %collective-permute-done.10 = bf16[384,512]{1,0:T(8,128)(2,1)S(1)} collective-permute-done((bf16[384,512]{1,0:T(8,128)(2,1)S(1)}, bf16[384,512]{1,0:T(8,128)(2,1)S(1)}, u32[]{:S(2)}, u32[]{:S(2)}) %collective-permute-start.10) | collective-permute-done | bytes 393248 | tf_op jit(solution)/shard_map/ppermute | solution.py:14
  744.6 13.9 psum.242
  761.5 13.9 psum.243
  783.7 118.6 %reduce-scatter.3.cloned.1.call-done = bf16[2,384,512]{2,1,0:T(8,128)(2,1)} async-done(((bf16[2,384,2048]{2,1,0:T(8,128)(2,1)}), bf16[2,384,512]{2,1,0:T(8,128)(2,1)}) %reduce-scatter.3.cloned.1.call-update) | async-done | bytes 786448 | tf_op jit(solution)/shard_map/reduce_scatter | solution.py:310
  905.9 20.3 %conditional.41 = (bf16[384,2304]{1,0:T(8,128)(2,1)}, f32[384,2048]{1,0:T(8,128)S(1)}) conditional(s32[]{:T(128)} %convert_element_type.516, (bf16[384,512]{1,0:T(8,128)(2,1)S(1)}, bf16[2048,512]{1,0:T(8,128)(2,1)S(1)}, bf16[384,2304]{1,0:T(8,128)(2,1)}) %tuple.994, (s32[384,9]{0,1:T(8,128)}, bf16[384,512]{1,0:T(8,128)(2,1)S(1)}, ...), branch_computations={%region_64.66_spmd, %region_65.67_spmd} | conditional | flops 805306368 | bytes 16238468 | solution.py:228
  956.1 29.1 %psum.244 = f32[2,2048]{1,0:T(2,128)} all-reduce(f32[2,2048]{1,0:T(2,128)S(1)} %pad_maximum_fusion.1), channel_id=1, replica_groups=mesh['pipe'=4,'dp'=8] {'dp'}, use_global_device_ids=true, to_apply=%region_68.70 | all-reduce | flops 4096 | bytes 32768 | tf_op jit(solution)/shard_map/psum | solution.py:124
  985.3 37.9 %conditional.42 = (f32[384,512]{1,0:T(8,128)S(1)}, f32[2048,512]{1,0:T(8,128)S(1)}, f32[2304,512]{1,0:T(8,128)}) conditional(s32[]{:T(128)} %convert_element_type.516, (f32[384]{0:T(512)S(1)}, f32[2,2048]{1,0:T(2,128)S(1)}, f32[1,2,2048]{2,1,0:T(2,128)S(1)}, f32[2,2048]{1,0:T(2,128)}, f32[]{:T(128)}, /*index=5*/f32[384,2048]{1,0:T(8,128)}, ...), branch_computations={%region_69.71_spmd, %region_70.73_spmd} | conditional | flops 1814714240 | bytes 59548612 | solution.py:398
  1028.8 13.6 psum.245
  1056.7 20.7 %conditional.45 = (bf16[384,2304]{1,0:T(8,128)(2,1)}, f32[384,2048]{1,0:T(8,128)}) conditional(s32[]{:T(128)} %convert_element_type.516, (bf16[384,512]{1,0:T(8,128)(2,1)S(1)}, bf16[2048,512]{1,0:T(8,128)(2,1)S(1)}, bf16[384,2304]{1,0:T(8,128)(2,1)}) %tuple.991, (s32[384,9]{0,1:T(8,128)S(1)}, bf16[384,512]{1,0:T(8,128)(2,1)S(1)}, ...), branch_computations={%region_78.81_spmd, %region_79.82_spmd} | conditional | flops 805306368 | bytes 17806668 | solution.py:228
  1077.4 30.6 %collective-permute-done.15 = bf16[384,512]{1,0:T(8,128)(2,1)} collective-permute-done((bf16[384,512]{1,0:T(8,128)(2,1)}, bf16[384,512]{1,0:T(8,128)(2,1)}, u32[]{:S(2)}, u32[]{:S(2)}) %collective-permute-start.15) | collective-permute-done | bytes 393248 | tf_op jit(solution)/shard_map/ppermute | solution.py:14
  1122.8 26.5 %psum.246 = f32[2,2048]{1,0:T(2,128)} all-reduce(f32[2,2048]{1,0:T(2,128)S(1)} %pad_maximum_fusion.2), channel_id=1, replica_groups=mesh['pipe'=4,'dp'=8] {'dp'}, use_global_device_ids=true, to_apply=%region_82.85 | all-reduce | flops 4096 | bytes 32768 | tf_op jit(solution)/shard_map/psum | solution.py:124
  1149.4 34.9 %conditional.46 = (f32[384,512]{1,0:T(8,128)S(1)}, f32[2048,512]{1,0:T(8,128)}, f32[2304,512]{1,0:T(8,128)}) conditional(s32[]{:T(128)} %convert_element_type.516, (f32[384]{0:T(512)S(1)}, f32[2,2048]{1,0:T(2,128)S(1)}, f32[1,2,2048]{2,1,0:T(2,128)S(1)}, f32[2,2048]{1,0:T(2,128)}, f32[]{:T(128)}, /*index=5*/f32[384,2048]{1,0:T(8,128)}, ...), branch_computations={%region_83.86_spmd, %region_84.87_spmd} | conditional | flops 1814910848 | bytes 51678036 | solution.py:398
  1186.8 13.6 psum.247
  1214.6 20.7 %conditional.49 = (bf16[384,2304]{1,0:T(8,128)(2,1)}, f32[384,2048]{1,0:T(8,128)}) conditional(s32[]{:T(128)} %convert_element_type.516, (bf16[384,512]{1,0:T(8,128)(2,1)S(1)}, bf16[2048,512]{1,0:T(8,128)(2,1)S(1)}, bf16[384,2304]{1,0:T(8,128)(2,1)}) %tuple.993, (s32[384,9]{0,1:T(8,128)S(1)}, bf16[384,512]{1,0:T(8,128)(2,1)S(1)}, ...), branch_computations={%region_92.95_spmd, %region_93.96_spmd} | conditional | flops 805306368 | bytes 17806668 | solution.py:228
  1235.2 27.6 %collective-permute-done.18 = bf16[384,512]{1,0:T(8,128)(2,1)} collective-permute-done((bf16[384,512]{1,0:T(8,128)(2,1)}, bf16[384,512]{1,0:T(8,128)(2,1)}, u32[]{:S(2)}, u32[]{:S(2)}) %collective-permute-start.18) | collective-permute-done | bytes 393248 | tf_op jit(solution)/shard_map/ppermute | solution.py:14
  1277.4 26.5 %psum.248 = f32[2,2048]{1,0:T(2,128)} all-reduce(f32[2,2048]{1,0:T(2,128)S(1)} %pad_maximum_fusion.3), channel_id=1, replica_groups=mesh['pipe'=4,'dp'=8] {'dp'}, use_global_device_ids=true, to_apply=%region_96.99 | all-reduce | flops 4096 | bytes 32768 | tf_op jit(solution)/shard_map/psum | solution.py:124
  1303.9 32.2 %conditional.50 = (f32[384,512]{1,0:T(8,128)S(1)}, f32[2048,512]{1,0:T(8,128)}, f32[2304,512]{1,0:T(8,128)}) conditional(s32[]{:T(128)} %convert_element_type.516, (f32[384]{0:T(512)S(1)}, f32[2,2048]{1,0:T(2,128)S(1)}, f32[1,2,2048]{2,1,0:T(2,128)S(1)}, f32[2,2048]{1,0:T(2,128)}, f32[]{:T(128)}, /*index=5*/f32[384,2048]{1,0:T(8,128)}, ...), branch_computations={%region_97.100_spmd, %region_98.101_spmd} | conditional | flops 1814910848 | bytes 51678036 | solution.py:398
  1338.7 13.6 psum.249
  1368.0 18.4 conditional.57
  1388.1 18.2 conditional.53
  1435.6 25.9 %psum.250 = f32[2,2048]{1,0:T(2,128)S(1)} all-reduce(f32[2,2048]{1,0:T(2,128)S(1)} %pad_maximum_fusion.4), channel_id=1, replica_groups=mesh['pipe'=4,'dp'=8] {'dp'}, use_global_device_ids=true, to_apply=%region_110.113 | all-reduce | flops 4096 | bytes 32768 | tf_op jit(solution)/shard_map/psum | solution.py:124
  1461.5 33.1 %conditional.54 = (f32[384,512]{1,0:T(8,128)S(1)}, f32[2048,512]{1,0:T(8,128)}, f32[2304,512]{1,0:T(8,128)}) conditional(s32[]{:T(128)} %convert_element_type.516, (f32[384]{0:T(512)S(1)}, f32[2,2048]{1,0:T(2,128)S(1)}, f32[1,2,2048]{2,1,0:T(2,128)S(1)}, f32[2,2048]{1,0:T(2,128)S(1)}, f32[]{:T(128)}, /*index=5*/f32[384,2048]{1,0:T(8,128)}, ...), branch_computations={%region_111.114_spmd, %region_112.115_spmd} | conditional | flops 1814910848 | bytes 44600148 | solution.py:398
  1496.3 13.6 psum.251
  1540.7 47.2 %collective-permute-done.24 = bf16[384,512]{1,0:T(8,128)(2,1)S(1)} collective-permute-done((bf16[384,512]{1,0:T(8,128)(2,1)S(1)}, bf16[384,512]{1,0:T(8,128)(2,1)S(1)}, u32[]{:S(2)}, u32[]{:S(2)}) %collective-permute-start.24) | collective-permute-done | bytes 393248 | tf_op jit(solution)/shard_map/ppermute | solution.py:14
  1594.0 25.9 %psum.252 = f32[2,2048]{1,0:T(2,128)S(1)} all-reduce(f32[2,2048]{1,0:T(2,128)S(1)} %pad_maximum_fusion.5), channel_id=1, replica_groups=mesh['pipe'=4,'dp'=8] {'dp'}, use_global_device_ids=true, to_apply=%region_124.127 | all-reduce | flops 4096 | bytes 32768 | tf_op jit(solution)/shard_map/psum | solution.py:124
  1619.9 31.9 %conditional.58 = (f32[384,512]{1,0:T(8,128)S(1)}, f32[2048,512]{1,0:T(8,128)}, f32[2304,512]{1,0:T(8,128)}) conditional(s32[]{:T(128)} %convert_element_type.516, (f32[384]{0:T(512)S(1)}, f32[2,2048]{1,0:T(2,128)S(1)}, f32[1,2,2048]{2,1,0:T(2,128)S(1)}, f32[2,2048]{1,0:T(2,128)S(1)}, f32[]{:T(128)}, /*index=5*/f32[384,2048]{1,0:T(8,128)}, ...), branch_computations={%region_125.128_spmd, %region_126.129_spmd} | conditional | flops 1814910848 | bytes 51678036 | solution.py:398
  1687.6 18.8 add_bitcast_fusion.1
  1706.4 20.5 %add_bitcast_fusion = f32[1,2304,512]{2,1,0:T(8,128)} fusion(f32[2304,512]{1,0:T(8,128)} %get-tuple-element.1090, f32[2304,512]{1,0:T(8,128)} %get-tuple-element.1091, f32[2304,512]{1,0:T(8,128)} %get-tuple-element.1088, f32[2304,512]{1,0:T(8,128)} %get-tuple-element.1089, f32[2304,512]{1,0:T(8,128)} %get-tuple-element.1086, ...), kind=kLoop, calls=%fused_computation.1187 | loop fusion | flops 16515072 | bytes 51904516 | tf_op jit(solution)/shard_map/broadcast_in_dim | solution.py:452
  1744.2 172.6 %all-reduce.13.cloned.1.call-done = (f32[1,2048,512]{2,1,0:T(8,128)}, f32[1,2304,512]{2,1,0:T(8,128)}) async-done(((f32[1,2048,512]{2,1,0:T(8,128)}, f32[1,2304,512]{2,1,0:T(8,128)}), (f32[1,2048,512]{2,1,0:T(8,128)}, f32[1,2304,512]{2,1,0:T(8,128)})) %all-reduce.13.cloned.1.call-update) | async-done | bytes 8912912 | tf_op jit(solution)/shard_map/psum | solution.py:451
  (1063 shorter events, 1005.2 us)
Async XLA Ops:
  7.2 49.2 %all-gather.3.cloned.1.call-start = ((), (), s32[]{:S(2)}) async-start(), calls=%async_computation.2 | async-start | bytes 3932160 | tf_op jit(solution)/shard_map/all_gather | solution.py:182
  7.9 894.4 %reduce-scatter.3.cloned.1.call-start = ((), (), s32[]{:S(2)}) async-start(), calls=%async_computation.3 | async-start | bytes 3932160 | tf_op jit(solution)/shard_map/reduce_scatter | solution.py:310
  8.6 11.6 collective-permute-start
  21.2 127.0 %copy-start.164 = (f32[1,2048]{1,0:T(1,128)}, f32[1,2048]{1,0:T(1,128)S(1)}, u32[]{:S(2)}) copy-start(f32[1,2048]{1,0:T(1,128)S(1)} %get-tuple-element.1814) | copy-start | bytes 24580
  21.2 127.0 %copy-start.166 = (f32[1,2048]{1,0:T(1,128)}, f32[1,2048]{1,0:T(1,128)S(1)}, u32[]{:S(2)}) copy-start(f32[1,2048]{1,0:T(1,128)S(1)} %get-tuple-element.1815) | copy-start | bytes 24580
  131.3 173.4 %copy-start.143 = (f32[2048]{0:T(1024)}, f32[2048]{0:T(1024)S(1)}, u32[]{:S(2)}) copy-start(f32[2048]{0:T(1024)S(1)} %broadcast_divide_fusion.4) | copy-start | bytes 24580
  153.2 52.9 %collective-permute-start.3 = (bf16[384,2048]{1,0:T(8,128)(2,1)}, bf16[384,2048]{1,0:T(8,128)(2,1)}, u32[]{:S(2)}, u32[]{:S(2)}) collective-permute-start(bf16[384,2048]{1,0:T(8,128)(2,1)} %multiply_convert_fusion.8), channel_id=1, source_target_pairs={{0,8},{8,16},{16,24},{1,9},{9,17},{17,25},{2,10},{10,18},{18,26},{... | collective-permute-start | bytes 4718600 | tf_op jit(solution)/shard_map/ppermute | solution.py:14
  156.5 42.4 %collective-permute-start.2 = (bf16[384,512]{1,0:T(8,128)(2,1)}, bf16[384,512]{1,0:T(8,128)(2,1)S(1)}, u32[]{:S(2)}, u32[]{:S(2)}) collective-permute-start(bf16[384,512]{1,0:T(8,128)(2,1)} %copy-done.131), channel_id=1, source_target_pairs={{0,8},{8,16},{16,24},{1,9},{9,17},{17,25},{2,10},{10,18},{18,26},{... | collective-permute-start | bytes 1179656 | tf_op jit(solution)/shard_map/ppermute | solution.py:14
  158.6 47.5 %collective-permute-start.1 = (bf16[384,512]{1,0:T(8,128)(2,1)S(1)}, bf16[384,512]{1,0:T(8,128)(2,1)S(1)}, u32[]{:S(2)}, u32[]{:S(2)}) collective-permute-start(bf16[384,512]{1,0:T(8,128)(2,1)S(1)} %multiply_convert_fusion.23), channel_id=1, source_target_pairs={{0,8},{8,16},{16,24},{1,9},{9,17},{17,25},{2,10},{10,18},{18,26},{... | collective-permute-start | bytes 1179656 | tf_op jit(solution)/shard_map/ppermute | solution.py:14
  295.7 164.0 %copy-start.147 = (f32[2048]{0:T(1024)}, f32[2048]{0:T(1024)S(1)}, u32[]{:S(2)}) copy-start(f32[2048]{0:T(1024)S(1)} %add_rsqrt_fusion.3) | copy-start | bytes 24580
  299.6 54.1 %collective-permute-start.6 = (bf16[384,2048]{1,0:T(8,128)(2,1)S(1)}, bf16[384,2048]{1,0:T(8,128)(2,1)S(1)}, u32[]{:S(2)}, u32[]{:S(2)}) collective-permute-start(bf16[384,2048]{1,0:T(8,128)(2,1)S(1)} %multiply_convert_fusion.7), channel_id=1, source_target_pairs={{0,8},{8,16},{16,24},{1,9},{9,17},{17,25},{2,10},{10,18},{18,26},{... | collective-permute-start | bytes 4718600 | tf_op jit(solution)/shard_map/ppermute | solution.py:14
  302.3 424.8 %copy-start.141 = (f32[384,9]{0,1:T(8,128)}, f32[384,9]{0,1:T(8,128)S(1)}, u32[]{:S(2)}) copy-start(f32[384,9]{0,1:T(8,128)S(1)} %get-tuple-element.1759) | copy-start | bytes 41476
  302.3 628.2 %copy-start.139 = (f32[384,9]{0,1:T(8,128)}, f32[384,9]{0,1:T(8,128)S(1)}, u32[]{:S(2)}) copy-start(f32[384,9]{0,1:T(8,128)S(1)} %get-tuple-element.1760) | copy-start | bytes 41476
  307.2 46.5 %collective-permute-start.4 = (bf16[384,512]{1,0:T(8,128)(2,1)S(1)}, bf16[384,512]{1,0:T(8,128)(2,1)S(1)}, u32[]{:S(2)}, u32[]{:S(2)}) collective-permute-start(bf16[384,512]{1,0:T(8,128)(2,1)S(1)} %multiply_convert_fusion.22), channel_id=1, source_target_pairs={{0,8},{8,16},{16,24},{1,9},{9,17},{17,25},{2,10},{10,18},{18,26},{... | collective-permute-start | bytes 1179656 | tf_op jit(solution)/shard_map/ppermute | solution.py:14
  313.7 39.0 %collective-permute-start.5 = (bf16[384,512]{1,0:T(8,128)(2,1)S(1)}, bf16[384,512]{1,0:T(8,128)(2,1)S(1)}, u32[]{:S(2)}, u32[]{:S(2)}) collective-permute-start(bf16[384,512]{1,0:T(8,128)(2,1)S(1)} %copy-done.133), channel_id=1, source_target_pairs={{0,8},{8,16},{16,24},{1,9},{9,17},{17,25},{2,10},{10,18},{18,26},{... | collective-permute-start | bytes 1179656 | tf_op jit(solution)/shard_map/ppermute | solution.py:14
  457.6 53.7 %collective-permute-start.9 = (bf16[384,2048]{1,0:T(8,128)(2,1)S(1)}, bf16[384,2048]{1,0:T(8,128)(2,1)S(1)}, u32[]{:S(2)}, u32[]{:S(2)}) collective-permute-start(bf16[384,2048]{1,0:T(8,128)(2,1)S(1)} %multiply_convert_fusion.6), channel_id=1, source_target_pairs={{0,8},{8,16},{16,24},{1,9},{9,17},{17,25},{2,10},{10,18},{18,26},{... | collective-permute-start | bytes 4718600 | tf_op jit(solution)/shard_map/ppermute | solution.py:14
  463.4 47.9 %collective-permute-start.7 = (bf16[384,512]{1,0:T(8,128)(2,1)S(1)}, bf16[384,512]{1,0:T(8,128)(2,1)S(1)}, u32[]{:S(2)}, u32[]{:S(2)}) collective-permute-start(bf16[384,512]{1,0:T(8,128)(2,1)S(1)} %multiply_convert_fusion.21), channel_id=1, source_target_pairs={{0,8},{8,16},{16,24},{1,9},{9,17},{17,25},{2,10},{10,18},{18,26},{... | collective-permute-start | bytes 1179656 | tf_op jit(solution)/shard_map/ppermute | solution.py:14
  473.4 36.9 %collective-permute-start.8 = (bf16[384,512]{1,0:T(8,128)(2,1)}, bf16[384,512]{1,0:T(8,128)(2,1)S(1)}, u32[]{:S(2)}, u32[]{:S(2)}) collective-permute-start(bf16[384,512]{1,0:T(8,128)(2,1)} %get-tuple-element.1035), channel_id=1, source_target_pairs={{0,8},{8,16},{16,24},{1,9},{9,17},{17,25},{2,10},{10,18},{18,26},{... | collective-permute-start | bytes 1179656 | tf_op jit(solution)/shard_map/ppermute | solution.py:14
  619.0 56.5 %collective-permute-start.12 = (bf16[384,2048]{1,0:T(8,128)(2,1)S(1)}, bf16[384,2048]{1,0:T(8,128)(2,1)S(1)}, u32[]{:S(2)}, u32[]{:S(2)}) collective-permute-start(bf16[384,2048]{1,0:T(8,128)(2,1)S(1)} %multiply_convert_fusion.5), channel_id=1, source_target_pairs={{0,8},{8,16},{16,24},{1,9},{9,17},{17,25},{2,10},{10,18},{18,26},{... | collective-permute-start | bytes 4718600 | tf_op jit(solution)/shard_map/ppermute | solution.py:14
  624.2 42.8 %collective-permute-start.10 = (bf16[384,512]{1,0:T(8,128)(2,1)S(1)}, bf16[384,512]{1,0:T(8,128)(2,1)S(1)}, u32[]{:S(2)}, u32[]{:S(2)}) collective-permute-start(bf16[384,512]{1,0:T(8,128)(2,1)S(1)} %multiply_convert_fusion.20), channel_id=1, source_target_pairs={{0,8},{8,16},{16,24},{1,9},{9,17},{17,25},{2,10},{10,18},{18,26},{... | collective-permute-start | bytes 1179656 | tf_op jit(solution)/shard_map/ppermute | solution.py:14
  634.7 39.6 %collective-permute-start.11 = (bf16[384,512]{1,0:T(8,128)(2,1)S(1)}, bf16[384,512]{1,0:T(8,128)(2,1)S(1)}, u32[]{:S(2)}, u32[]{:S(2)}) collective-permute-start(bf16[384,512]{1,0:T(8,128)(2,1)S(1)} %copy-done.135), channel_id=1, source_target_pairs={{0,8},{8,16},{16,24},{1,9},{9,17},{17,25},{2,10},{10,18},{18,26},{... | collective-permute-start | bytes 1179656 | tf_op jit(solution)/shard_map/ppermute | solution.py:14
  783.6 118.7 %copy-start.146 = (f32[2,384]{1,0:T(2,128)S(1)}, f32[2,384]{1,0:T(2,128)}, u32[]{:S(2)}) copy-start(f32[2,384]{1,0:T(2,128)} %copy-done.145) | copy-start | bytes 9220
  783.6 122.0 %copy-start.168 = (f32[1,2,1024]{2,1,0:T(2,128)S(1)}, f32[1,2,1024]{2,1,0:T(2,128)}, u32[]{:S(2)}) copy-start(f32[1,2,1024]{2,1,0:T(2,128)} %param.77) | copy-start | bytes 24580
  783.6 122.0 %copy-start.170 = (f32[2,1024]{1,0:T(2,128)S(1)}, f32[2,1024]{1,0:T(2,128)}, u32[]{:S(2)}) copy-start(f32[2,1024]{1,0:T(2,128)} %copy-done.169) | copy-start | bytes 24580
  783.6 122.1 %copy-start.144 = (f32[2048]{0:T(1024)S(1)}, f32[2048]{0:T(1024)}, u32[]{:S(2)}) copy-start(f32[2048]{0:T(1024)} %copy-done.143) | copy-start | bytes 24580
  783.6 122.1 %copy-start.155 = (f32[2048]{0:T(1024)S(1)}, f32[2048]{0:T(1024)}, u32[]{:S(2)}) copy-start(f32[2048]{0:T(1024)} %copy-done.153) | copy-start | bytes 24580
  783.6 122.1 %copy-start.148 = (f32[2048]{0:T(1024)S(1)}, f32[2048]{0:T(1024)}, u32[]{:S(2)}) copy-start(f32[2048]{0:T(1024)} %copy-done.147) | copy-start | bytes 24580
  783.6 122.2 %copy-start.150 = (f32[2048]{0:T(1024)S(1)}, f32[2048]{0:T(1024)}, u32[]{:S(2)}) copy-start(f32[2048]{0:T(1024)} %copy-done.149) | copy-start | bytes 24580
  783.7 122.2 %copy-start.152 = (f32[2048]{0:T(1024)S(1)}, f32[2048]{0:T(1024)}, u32[]{:S(2)}) copy-start(f32[2048]{0:T(1024)} %copy-done.151) | copy-start | bytes 24580
  783.7 165.9 %all-gather.5.cloned.1.call-start = ((), (), s32[]{:S(2)}) async-start(), calls=%async_computation.4 | async-start | bytes 3932160 | tf_op jit(solution)/shard_map/all_gather | solution.py:317
  905.6 836.1 %reduce-scatter.5.cloned.1.call-start = ((), (), s32[]{:S(2)}) async-start(), calls=%async_computation.5 | async-start | bytes 3932160 | tf_op jit(solution)/shard_map/reduce_scatter | solution.py:448
  1052.7 62.9 %collective-permute-start.13 = (bf16[384,2048]{1,0:T(8,128)(2,1)}, bf16[384,2048]{1,0:T(8,128)(2,1)}, u32[]{:S(2)}, u32[]{:S(2)}) collective-permute-start(bf16[384,2048]{1,0:T(8,128)(2,1)} %get-tuple-element.1043), channel_id=1, source_target_pairs={{8,0},{16,8},{24,16},{9,1},{17,9},{25,17},{10,2},{18,10},{26,18},{... | collective-permute-start | bytes 4718600 | tf_op jit(solution)/shard_map/ppermute | solution.py:14
  1054.0 54.0 %collective-permute-start.15 = (bf16[384,512]{1,0:T(8,128)(2,1)}, bf16[384,512]{1,0:T(8,128)(2,1)}, u32[]{:S(2)}, u32[]{:S(2)}) collective-permute-start(bf16[384,512]{1,0:T(8,128)(2,1)} %get-tuple-element.1048), channel_id=1, source_target_pairs={{8,0},{16,8},{24,16},{9,1},{17,9},{25,17},{10,2},{18,10},{26,18},{... | collective-permute-start | bytes 1179656 | tf_op jit(solution)/shard_map/ppermute | solution.py:14
  1055.3 60.4 %collective-permute-start.14 = (bf16[384,512]{1,0:T(8,128)(2,1)S(1)}, bf16[384,512]{1,0:T(8,128)(2,1)}, u32[]{:S(2)}, u32[]{:S(2)}) collective-permute-start(bf16[384,512]{1,0:T(8,128)(2,1)S(1)} %multiply_convert_fusion.17), channel_id=1, source_target_pairs={{8,0},{16,8},{24,16},{9,1},{17,9},{25,17},{10,2},{18,10},{26,18},{... | collective-permute-start | bytes 1179656 | tf_op jit(solution)/shard_map/ppermute | solution.py:14
  1210.7 59.7 %collective-permute-start.16 = (bf16[384,2048]{1,0:T(8,128)(2,1)}, bf16[384,2048]{1,0:T(8,128)(2,1)}, u32[]{:S(2)}, u32[]{:S(2)}) collective-permute-start(bf16[384,2048]{1,0:T(8,128)(2,1)} %get-tuple-element.1050), channel_id=1, source_target_pairs={{8,0},{16,8},{24,16},{9,1},{17,9},{25,17},{10,2},{18,10},{26,18},{... | collective-permute-start | bytes 4718600 | tf_op jit(solution)/shard_map/ppermute | solution.py:14
  1211.9 50.8 %collective-permute-start.18 = (bf16[384,512]{1,0:T(8,128)(2,1)}, bf16[384,512]{1,0:T(8,128)(2,1)}, u32[]{:S(2)}, u32[]{:S(2)}) collective-permute-start(bf16[384,512]{1,0:T(8,128)(2,1)} %get-tuple-element.1055), channel_id=1, source_target_pairs={{8,0},{16,8},{24,16},{9,1},{17,9},{25,17},{10,2},{18,10},{26,18},{... | collective-permute-start | bytes 1179656 | tf_op jit(solution)/shard_map/ppermute | solution.py:14
  1213.2 57.1 %collective-permute-start.17 = (bf16[384,512]{1,0:T(8,128)(2,1)S(1)}, bf16[384,512]{1,0:T(8,128)(2,1)S(1)}, u32[]{:S(2)}, u32[]{:S(2)}) collective-permute-start(bf16[384,512]{1,0:T(8,128)(2,1)S(1)} %multiply_convert_fusion.15), channel_id=1, source_target_pairs={{8,0},{16,8},{24,16},{9,1},{17,9},{25,17},{10,2},{18,10},{26,18},{... | collective-permute-start | bytes 1179656 | tf_op jit(solution)/shard_map/ppermute | solution.py:14
  1366.6 62.4 %collective-permute-start.19 = (bf16[384,2048]{1,0:T(8,128)(2,1)}, bf16[384,2048]{1,0:T(8,128)(2,1)}, u32[]{:S(2)}, u32[]{:S(2)}) collective-permute-start(bf16[384,2048]{1,0:T(8,128)(2,1)} %get-tuple-element.1057), channel_id=1, source_target_pairs={{8,0},{16,8},{24,16},{9,1},{17,9},{25,17},{10,2},{18,10},{26,18},{... | collective-permute-start | bytes 4718600 | tf_op jit(solution)/shard_map/ppermute | solution.py:14
  1406.3 22.7 %collective-permute-start.20 = (bf16[384,512]{1,0:T(8,128)(2,1)}, bf16[384,512]{1,0:T(8,128)(2,1)S(1)}, u32[]{:S(2)}, u32[]{:S(2)}) collective-permute-start(bf16[384,512]{1,0:T(8,128)(2,1)} %multiply_convert_fusion.13), channel_id=1, source_target_pairs={{8,0},{16,8},{24,16},{9,1},{17,9},{25,17},{10,2},{18,10},{26,18},{... | collective-permute-start | bytes 1179656 | tf_op jit(solution)/shard_map/ppermute | solution.py:14
  1407.9 20.1 %collective-permute-start.21 = (bf16[384,512]{1,0:T(8,128)(2,1)}, bf16[384,512]{1,0:T(8,128)(2,1)S(1)}, u32[]{:S(2)}, u32[]{:S(2)}) collective-permute-start(bf16[384,512]{1,0:T(8,128)(2,1)} %copy-done.136), channel_id=1, source_target_pairs={{8,0},{16,8},{24,16},{9,1},{17,9},{25,17},{10,2},{18,10},{26,18},{... | collective-permute-start | bytes 1179656 | tf_op jit(solution)/shard_map/ppermute | solution.py:14
  1524.3 64.5 %collective-permute-start.22 = (bf16[384,2048]{1,0:T(8,128)(2,1)}, bf16[384,2048]{1,0:T(8,128)(2,1)S(1)}, u32[]{:S(2)}, u32[]{:S(2)}) collective-permute-start(bf16[384,2048]{1,0:T(8,128)(2,1)} %get-tuple-element.1064), channel_id=1, source_target_pairs={{8,0},{16,8},{24,16},{9,1},{17,9},{25,17},{10,2},{18,10},{26,18},{... | collective-permute-start | bytes 4718600 | tf_op jit(solution)/shard_map/ppermute | solution.py:14
  1533.8 55.0 %collective-permute-start.23 = (bf16[384,512]{1,0:T(8,128)(2,1)}, bf16[384,512]{1,0:T(8,128)(2,1)S(1)}, u32[]{:S(2)}, u32[]{:S(2)}) collective-permute-start(bf16[384,512]{1,0:T(8,128)(2,1)} %multiply_convert_fusion.11), channel_id=1, source_target_pairs={{8,0},{16,8},{24,16},{9,1},{17,9},{25,17},{10,2},{18,10},{26,18},{... | collective-permute-start | bytes 1179656 | tf_op jit(solution)/shard_map/ppermute | solution.py:14
  1535.1 52.8 %collective-permute-start.24 = (bf16[384,512]{1,0:T(8,128)(2,1)S(1)}, bf16[384,512]{1,0:T(8,128)(2,1)S(1)}, u32[]{:S(2)}, u32[]{:S(2)}) collective-permute-start(bf16[384,512]{1,0:T(8,128)(2,1)S(1)} %copy-done.138), channel_id=1, source_target_pairs={{8,0},{16,8},{24,16},{9,1},{17,9},{25,17},{10,2},{18,10},{26,18},{... | collective-permute-start | bytes 1179656 | tf_op jit(solution)/shard_map/ppermute | solution.py:14
  1687.5 229.3 %all-reduce.13.cloned.1.call-start = ((), (), s32[]{:S(2)}) async-start(), calls=%async_computation.6 | async-start | bytes 17825792 | tf_op jit(solution)/shard_map/psum | solution.py:451
  1727.7 7.2 collective-permute-start.25
  1729.7 6.1 collective-permute-start.26
  1731.6 6.7 collective-permute-start.27
  1732.9 7.4 collective-permute-start.28
  (200 other events, 2868.4 us)
Sparse Core Ops, SparseCore 0:
  9.8 46.5 all-gather.2
  783.7 118.5 reduce-scatter.2
  905.7 43.8 all-gather.4
  1687.7 40.4 reduce-scatter.4
  1731.0 185.7 all-reduce.12
where the time goes:
time: 1940 us; the launch traced here: 1930 us
  waiting for transfers between devices  619 us (32%)
  blocking collectives  482 us (25%)
  local copies, waits for them, and re-layouts  319 us (16%)
  other arithmetic  312 us (16%)
  matrix products  92.7 us (5%)
  starting transfers between devices  76.8 us (4%)
    ppermute x29, waiting for transfers between devices, passed_along(): return lax.ppermute(block, axis, route)  281 us
    psum x10, blocking collectives, norm_sums(): lax.psum(jnp.stack([jnp.sum(upstream * normed, 0), jnp.sum(upstream, 0)])...  202 us
    psum x1, waiting for transfers between devices, local(): wide_total, taps_total = lax.psum((sum_wide, sum_taps), 'dp')  173 us
    psum x10, blocking collectives, moments(): mean_value = lax.psum(jnp.sum(masked, 0), 'dp') / pixel_total  142 us
    psum x10, blocking collectives, moments(): variance = lax.psum(jnp.sum(centred * centred, 0), 'dp') / pixel_total  139 us
    reduce_scatter x1, waiting for transfers between devices, local(): lax.psum_scatter(outer_term.astype(jnp.bfloat16), 'pipe', scatter_dimensi...  119 us
    gather x45, local copies, waits for them, and re-layouts, gather_taps(): jnp.take(hidden, neighbour[:, tap_id], axis=0)  113 us
    gather x25, local copies, waits for them, and re-layouts, return_taps(): jnp.take(block_part, neighbour[:, mirror], axis=0) * usable[:, mirror, None]  88.1 us
  transfers between devices with their start and end apart: 34, of which 19 were waited for; matrix products, arithmetic and copies ran while one was open for 11% of the time, Pallas kernels for 0%

commit v1 on v0

v1 whole, which is shorter than its diff:
```python
import functools
from types import SimpleNamespace

import jax
import jax.numpy as jnp
from jax import lax
from jax.experimental import pallas as pl
from jax.experimental.pallas import tpu as pltpu
from jax.sharding import PartitionSpec as P

MESH = pl.DeviceIdType.MESH
F32 = jnp.float32
BF16 = jnp.bfloat16
EPS = 1e-05
LANES = 128
N_PIPE = 4
NEAR = [k for k in range(9) if k != 4]


def slot_of(tap):
    return tap if tap < 4 else tap - 1


def dot_nn(a, b):
    return jnp.dot(a, b, preferred_element_type=F32)


def dot_nt(a, b):
    return lax.dot_general(a, b, (((1,), (1,)), ((), ())), preferred_element_type=F32)


def sigmoid(v):
    return jax.nn.sigmoid(v)


def sizes(n_dp, rows):
    n_z = n_dp // 2
    n_own = min(n_z, 16)
    return n_z, n_own, 256 // n_own, 2304 // n_own


def scratch_list(n_dp, rows):
    n_z, n_own, wr, kr = sizes(n_dp, rows)
    dma = pltpu.SemaphoreType.DMA

    def half(*shape):
        return pltpu.VMEM(shape, BF16)

    def full(*shape):
        return pltpu.VMEM(shape, F32)

    return dict(
        wt=half(4, 512, 512),
        k2=half(2, 512, 1152),
        gm=full(4, 2, 128),
        go=full(4, 2, 2, 512),
        msk=full(2, rows, 128),
        pm=half(2, 8, rows, rows),
        part=half(2, 2, 4, rows, 128),
        rsr=half(6, 2, 3, rows, 128),
        ag=half(6, 2, 4, rows, 128),
        stm=full(8, 2, n_dp, 2, 128),
        stw=full(4, 2, n_dp, 2, 512),
        midv=full(4, 2, rows, 128),
        dzm=full(2, rows, 128),
        inv_mid=full(4, 2, 1, 128),
        inv_wide=full(2, 2, 1, 512),
        widv=full(2, 2, rows, 512),
        pre0=full(2, rows, 512),
        s1=half(2, rows, 512),
        mix=half(2, rows, 512),
        gp=half(2, 2, rows, 512),
        cv=half(2, rows, 512),
        gt=half(2, rows, 512),
        gb=half(2, rows, 1152),
        yb=half(8, rows, 128),
        tb=half(512, 2 * rows),
        dw=half(4, 2, 256, 512),
        prw=half(4, 256, 512),
        zsw=half(4, 256, 512),
        zrw=half(4, n_z - 1, wr, 512),
        fiw=half(4, wr, 512),
        ow=half(4, 2, n_own, wr, 512),
        dk=half(2, 4608, 128),
        prk=half(2, 2304, 128),
        zsk=half(2, 2304, 128),
        zrk=half(2, n_z - 1, kr, 128),
        fik=half(2, kr, 128),
        ok=half(2304, 512),
        gsm=full(4, 4, 2, 128),
        gsw=full(2, 4, 2, 512),
        cnt=pltpu.SMEM((2, n_dp), F32),
        w_s=dma((3,)),
        w_r=dma((4,)),
        w_f=dma((4,)),
        k_s=dma((3, 5)),
        k_r=dma((4, 5)),
        k_f=dma((4, 5)),
        n_s=dma((3, 3)),
        n_r=dma((3, 3)),
        loc=dma((8,)),
        rs_s=dma((6, 2, 3)),
        rs_r=dma((6, 2, 3)),
        ag_s=dma((6, 2, 3)),
        ag_r=dma((6, 2, 3)),
        stm_s=dma((8, 2)),
        stm_r=dma((8, 2)),
        stw_s=dma((4, 2)),
        stw_r=dma((4, 2)),
        pw_s=dma((6,)),
        pw_r=dma((6,)),
        zw_s=dma((6,)),
        zw_r=dma((6,)),
        fw_s=dma((6,)),
        fw_r=dma((2, 4)),
        aw_s=dma((2,)),
        aw_r=dma((2,)),
        bw_s=dma((2,)),
        bw_r=dma((2,)),
        g_s=dma((3, 2)),
        g_r=dma((3, 2)),
        out=dma((8,)),
    )


def kernel(names, n, *refs):
    (x_ref, cot_ref, wide_ref, taps_ref, nmid_ref, nout_ref, counts_ref) = refs[:7]
    (mixed_ref, gpre_ref, conv_ref, gwide_ref, gtaps_ref, gmid_ref, gout_ref) = refs[7:14]
    sc = SimpleNamespace(**dict(zip(names, refs[14:])))
    rows = x_ref.shape[1]
    n_z, n_own, wr, kr = sizes(n, rows)
    p = lax.axis_index("pipe")
    d = lax.axis_index("dp")
    z = lax.div(d, 2)
    c = lax.rem(d, 2)
    parity = lax.rem(p, 2)
    sibling = (p, 2 * z + 1 - c)
    finish = []

    def pipe_at(off):
        return lax.rem(p + off, N_PIPE)

    def remote(src, dst, ss, rs, dev):
        return pltpu.make_async_remote_copy(
            src_ref=src, dst_ref=dst, send_sem=ss, recv_sem=rs, device_id=dev, device_id_type=MESH
        )

    def each(count, first, body):
        if count - first <= 8:
            for k in range(first, count):
                body(k)
        else:

            def step(k, carry):
                body(k)
                return carry

            lax.fori_loop(first, count, step, 0)

    def bytes_wait(view, sem):
        pltpu.make_async_copy(view, view, sem).wait()

    barrier = pltpu.get_barrier_semaphore()
    for off in range(1, N_PIPE):
        pl.semaphore_signal(barrier, inc=1, device_id=(pipe_at(off), d), device_id_type=MESH)

    def greet(k):
        pl.semaphore_signal(
            barrier, inc=1, device_id=(p, lax.rem(d + k, n)), device_id_type=MESH
        )

    each(n, 1, greet)

    own_w = pltpu.make_async_copy(
        wide_ref.at[0, pl.ds(pl.multiple_of(512 * p, 512), 512), :], sc.wt.at[p], sc.loc.at[0]
    )
    own_w.start()

    def tap_parts(h, column):
        layer = h // 2
        odd = h % 2
        listed = [
            (
                taps_ref.at[0, pl.ds(512 * i + 256 * odd, 512), column],
                (layer, pl.ds(0, 512), pl.ds(128 * (i + 5 * odd), 128)),
            )
            for i in range(4)
        ]
        listed.append(
            (
                taps_ref.at[0, pl.ds(2048 * (1 - odd), 256), column],
                (layer, pl.ds(256 * odd, 256), pl.ds(512, 128)),
            )
        )
        return listed

    def columns_of(q):
        return pl.ds(pl.multiple_of(128 * q, 128), 128)

    for s in range(4):

        @pl.when(p == s)
        def _(s=s):
            for i, (src, dst) in enumerate(tap_parts(s, columns_of(p))):
                pltpu.make_async_copy(src, sc.k2.at[dst], sc.loc.at[1 + i]).start()

    own_n = pltpu.make_async_copy(
        nmid_ref.at[0, :, columns_of(p)], sc.gm.at[p], sc.loc.at[6]
    )
    own_n.start()
    for e in range(2):
        sc.go[p, e] = nout_ref[0, :, 512 * e : 512 * e + 512]

    def used_rows(m, j):
        return (
            49 * counts_ref[m, j, 0]
            + 36 * counts_ref[m, j, 1]
            + 25 * counts_ref[m, j, 2]
            + 4 * counts_ref[m, j, 3]
        )

    totals = []
    for m in range(2):

        def count_up(j, acc, m=m):
            used = used_rows(m, j)
            sc.cnt[m, j] = used.astype(F32)
            return acc + used

        totals.append(lax.fori_loop(0, n, count_up, jnp.int32(0)).astype(F32))

    pl.semaphore_wait(barrier, N_PIPE - 1 + n - 1)

    def send_wide(off):
        q = pipe_at(off)
        return remote(
            wide_ref.at[0, pl.ds(pl.multiple_of(512 * q, 512), 512), :],
            sc.wt.at[p],
            sc.w_s.at[off - 1],
            sc.w_r.at[p],
            (q, d),
        )

    def send_taps(s, off):
        q = pipe_at(off)
        return [
            remote(
                src, sc.k2.at[dst], sc.k_s.at[off - 1, i], sc.k_r.at[p, i], (q, d)
            )
            for i, (src, dst) in enumerate(tap_parts(s, columns_of(q)))
        ]

    def send_norm(off):
        q = pipe_at(off)
        listed = [
            remote(
                nmid_ref.at[0, :, columns_of(q)],
                sc.gm.at[p],
                sc.n_s.at[off - 1, 0],
                sc.n_r.at[off - 1, 0],
                (q, d),
            )
        ]
        for e in range(2):
            listed.append(
                remote(
                    nout_ref.at[0, :, pl.ds(512 * e, 512)],
                    sc.go.at[p, e],
                    sc.n_s.at[off - 1, 1 + e],
                    sc.n_r.at[off - 1, 1 + e],
                    (q, d),
                )
            )
        return listed

    def start_wide(s):
        @pl.when((p == s) & (c == s % 2))
        def _():
            for off in range(1, 4):
                send_wide(off).start()

    def start_taps(s):
        @pl.when((p == s) & (c == s % 2))
        def _():
            for off in range(1, 4):
                for copy in send_taps(s, off):
                    copy.start()

    def finish_weights():
        for s in range(4):

            @pl.when((p == s) & (c == s % 2))
            def _(s=s):
                for off in range(1, 4):
                    send_wide(off).wait_send()
                    for copy in send_taps(s, off):
                        copy.wait_send()

            @pl.when((p != s) & (c == s % 2))
            def _(s=s):
                pass_wide(s).wait_send()
                for copy in pass_taps(s):
                    copy.wait_send()

    finish.append(finish_weights)

    def pass_wide(s):
        return remote(sc.wt.at[s], sc.wt.at[s], sc.w_f.at[s], sc.w_r.at[s], sibling)

    def pass_taps(s):
        return [
            remote(
                sc.k2.at[dst], sc.k2.at[dst], sc.k_f.at[s, i], sc.k_r.at[s, i], sibling
            )
            for i, (_, dst) in enumerate(tap_parts(s, pl.ds(0, 128)))
        ]

    def relay_wide(s):
        @pl.when((p != s) & (c == s % 2))
        def _():
            copy = pass_wide(s)
            copy.wait_recv()
            copy.start()

    def ready_wide(s):
        @pl.when((p != s) & (c != s % 2))
        def _():
            pass_wide(s).wait_recv()

        if s == 0:
            own_w.wait()

    def relay_taps(s):
        @pl.when((p != s) & (c == s % 2))
        def _():
            for copy in pass_taps(s):
                copy.wait_recv()
                copy.start()

    def ready_taps(s):
        @pl.when((p != s) & (c != s % 2))
        def _():
            for copy in pass_taps(s):
                copy.wait_recv()

        @pl.when(p == s)
        def _():
            for i, (src, dst) in enumerate(tap_parts(s, columns_of(p))):
                pltpu.make_async_copy(src, sc.k2.at[dst], sc.loc.at[1 + i]).wait()

    start_wide(0)
    for off in range(1, 4):
        for copy in send_norm(off):
            copy.start()
    start_taps(0)
    start_taps(1)
    start_wide(1)

    def finish_norm():
        for off in range(1, 4):
            for copy in send_norm(off):
                copy.wait_send()

    finish.append(finish_norm)

    row_id = lax.broadcasted_iota(jnp.int32, (rows, LANES), 0).astype(F32)
    lane_id = lax.broadcasted_iota(jnp.int32, (rows, LANES), 1).astype(F32)

    def build(m):
        ends = []
        total = jnp.int32(0)
        for g, area in enumerate((49, 36, 25, 4)):
            total = total + area * counts_ref[m, d, g]
            ends.append(total.astype(F32))
        sc.msk[m] = jnp.where(row_id < ends[3], 1.0, 0.0)

        def pick(values):
            out = values[4]
            for g in (3, 2, 1, 0):
                out = jnp.where(row_id < ends[g], values[g], out)
            return out

        zero = jnp.zeros((rows, LANES), F32)
        side = pick([zero + 7.0, zero + 6.0, zero + 5.0, zero + 2.0, zero + 1.0])
        begin = pick([zero, zero + ends[0], zero + ends[1], zero + ends[2], row_id])
        one_over = pick(
            [zero + 1.0 / 7.0, zero + 1.0 / 6.0, zero + 1.0 / 5.0, zero + 0.5, zero + 1.0]
        )
        within = row_id - begin
        within = within - side * side * jnp.floor((within + 0.5) * one_over * one_over)
        map_row = jnp.floor((within + 0.5) * one_over)
        map_col = within - side * map_row
        for k in NEAR:
            du, dv = k // 3 - 1, k % 3 - 1
            usable = row_id < ends[3]
            if du == -1:
                usable = usable & (map_row > 0.5)
            if du == 1:
                usable = usable & (map_row < side - 1.5)
            if dv == -1:
                usable = usable & (map_col > 0.5)
            if dv == 1:
                usable = usable & (map_col < side - 1.5)
            target = jnp.where(usable, row_id + du * side + dv, -1000.0)
            for t in range(rows // LANES):
                hit = jnp.where(target == lane_id + float(LANES * t), 1.0, 0.0)
                sc.pm[m, slot_of(k), :, LANES * t : LANES * (t + 1)] = hit.astype(BF16)

    for m in range(2):
        build(m)

    rs_last = {0: None, 1: None}
    rs_turn = [0]

    def rs_copies(rid, m, par):
        listed = []
        for off in range(1, 4):
            q = pipe_at(off)
            listed.append(
                remote(
                    sc.part.at[par, m, q],
                    sc.rsr.at[rid, m, off - 1],
                    sc.rs_s.at[rid, m, off - 1],
                    sc.rs_r.at[rid, m, off - 1],
                    (q, d),
                )
            )
        return listed

    def rs_open(rid, m, par):
        if rs_last[par] is not None:
            for copy in rs_copies(rs_last[par], m, par):
                copy.wait_send()

    def rs_start(rid, m, par):
        for copy in rs_copies(rid, m, par):
            copy.start()

    def rs_sum(rid, m, par):
        for copy in rs_copies(rid, m, par):
            copy.wait_recv()
        total = sc.part[par, m, p].astype(F32)
        for k in range(3):
            total = total + sc.rsr[rid, m, k].astype(F32)
        return total

    def ag_copies(aid, m):
        listed = []
        for off in range(1, 4):
            listed.append(
                remote(
                    sc.ag.at[aid, m, p],
                    sc.ag.at[aid, m, p],
                    sc.ag_s.at[aid, m, off - 1],
                    sc.ag_r.at[aid, m, off - 1],
                    (pipe_at(off), d),
                )
            )
        return listed

    def ag_start(aid, m, value):
        sc.ag[aid, m, p] = value
        for copy in ag_copies(aid, m):
            copy.start()

    def ag_wait(aid, m):
        for copy in ag_copies(aid, m):
            copy.wait_recv()

    def ag_value(aid, m):
        return jnp.concatenate([sc.ag[aid, m, q] for q in range(4)], axis=1)

    def finish_ag():
        for aid in range(6):
            for m in range(2):
                for copy in ag_copies(aid, m):
                    copy.wait_send()

    finish.append(finish_ag)

    def st_refs(wide, i, m):
        if wide:
            return sc.stw.at[i, m], sc.stw_s.at[i, m], sc.stw_r.at[i, m]
        return sc.stm.at[i, m], sc.stm_s.at[i, m], sc.stm_r.at[i, m]

    def st_start(wide, i, m):
        buf, ss, rs = st_refs(wide, i, m)

        def go(k):
            remote(buf.at[d], buf.at[d], ss, rs, (p, lax.rem(d + k, n))).start()

        each(n, 1, go)

    def st_wait(wide, i, m):
        buf, ss, rs = st_refs(wide, i, m)
        bytes_wait(buf.at[pl.ds(0, n - 1)], rs)

    def finish_st():
        for wide, count in ((True, 4), (False, 8)):
            for i in range(count):
                for m in range(2):
                    buf, ss, rs = st_refs(wide, i, m)
                    bytes_wait(buf.at[pl.ds(0, n - 1)], ss)

    finish.append(finish_st)

    def over_devices(body, init):
        if n <= 8:
            for j in range(n):
                init = body(j, init)
            return init
        return lax.fori_loop(0, n, body, init)

    def combine(wide, i, m):
        st_wait(wide, i, m)
        ref = sc.stw if wide else sc.stm
        blank = jnp.zeros((1, ref.shape[-1]), F32)
        mean = over_devices(
            lambda j, acc: acc + sc.cnt[m, j] * ref[i, m, j, 0:1, :], blank
        )
        mean = mean / totals[m]

        def spread(j, acc):
            gap = ref[i, m, j, 0:1, :] - mean
            return acc + ref[i, m, j, 1:2, :] + sc.cnt[m, j] * (gap * gap)

        var = over_devices(spread, blank) / totals[m]
        return mean, lax.rsqrt(var + EPS)

    def back_sums(wide, i, m):
        st_wait(wide, i, m)
        ref = sc.stw if wide else sc.stm
        return over_devices(
            lambda j, acc: acc + ref[i, m, j], jnp.zeros((2, ref.shape[-1]), F32)
        )

    def local_moments(v, m):
        mask = sc.msk[m]
        own = jnp.maximum(sc.cnt[m, d], 1.0)
        mean = jnp.sum(v * mask, 0, keepdims=True) / own
        gap = (v - mean) * mask
        return jnp.concatenate([mean, jnp.sum(gap * gap, 0, keepdims=True)], 0)

    def local_sums(dz, vhat):
        return jnp.concatenate(
            [jnp.sum(dz * vhat, 0, keepdims=True), jnp.sum(dz, 0, keepdims=True)], 0
        )

    def lanes(j):
        return slice(LANES * j, LANES * (j + 1))

    def stream(layer, m):
        return x_ref[m] if layer == 0 else sc.s1[m]

    def stream_part(layer, m, j):
        return (x_ref[m, :, lanes(j)] if layer == 0 else sc.s1[m, :, lanes(j)]).astype(F32)

    rs_par = {0: 0, 1: 1, 3: 0, 5: 1, 2: 0, 4: 1}
    rs_before = {0: None, 1: None, 3: 0, 5: 1, 2: 3, 4: 5}

    def rs_send(rid, m, values):
        par = rs_par[rid]
        if rs_before[rid] is not None:
            for copy in rs_copies(rs_before[rid], m, par):
                copy.wait_send()
        for j, value in enumerate(values):
            half = value.astype(BF16)
            sc.part[par, m, 2 * j] = half[:, :LANES]
            sc.part[par, m, 2 * j + 1] = half[:, LANES:]
        rs_start(rid, m, par)

    def finish_rs():
        for rid in (2, 4):
            for m in range(2):
                for copy in rs_copies(rid, m, rs_par[rid]):
                    copy.wait_send()

    finish.append(finish_rs)

    def first_part(layer, m):
        s = stream(layer, m)
        rs_send(
            layer,
            m,
            [dot_nn(s, sc.wt[2 * layer, :, 256 * j : 256 * j + 256]) for j in range(2)],
        )

    def mid_moments(i, m, v):
        sc.midv[i, m] = v
        sc.stm[i, m, d] = local_moments(v, m)
        st_start(False, i, m)

    def first_norm(layer, m):
        mid_moments(2 * layer, m, rs_sum(layer, m, rs_par[layer]))

    def mid_hidden(i, m):
        mean, inv = combine(False, i, m)
        sc.inv_mid[i, m] = inv
        vhat = (sc.midv[i, m] - mean) * inv
        sc.midv[i, m] = vhat
        u = sc.gm[i, 0:1, :] * vhat + sc.gm[i, 1:2, :]
        return (sc.msk[m] * (u * sigmoid(u))).astype(BF16)

    def hidden_one(layer, m):
        ag_start(layer, m, mid_hidden(2 * layer, m))

    def second_part(layer, m):
        ag_wait(layer, m)
        h = ag_value(layer, m)
        centre = None
        for j in range(5):
            width = 256 if j < 4 else 128
            y = dot_nn(h, sc.k2[layer, :, 256 * j : 256 * j + width])
            for e in range(width // LANES):
                tap = 2 * j + e
                if tap == 4:
                    centre = y[:, lanes(e)]
                    sc.midv[2 * layer + 1, m] = centre
                else:
                    sc.yb[slot_of(tap)] = y[:, lanes(e)].astype(BF16)
        total = sc.midv[2 * layer + 1, m]
        for k in range(8):
            total = total + dot_nn(sc.pm[m, k], sc.yb[k])
        mid_moments(2 * layer + 1, m, total)

    def hidden_two(layer, m):
        ag_start(2 + layer, m, mid_hidden(2 * layer + 1, m))

    def third_part(layer, m):
        ag_wait(2 + layer, m)
        h = ag_value(2 + layer, m)
        for j in range(2):
            sc.widv[layer, m, :, 256 * j : 256 * j + 256] = dot_nt(
                h, sc.wt[2 * layer + 1, 256 * j : 256 * j + 256, :]
            )
        for j in range(4):
            sc.stw[layer, m, d, :, lanes(j)] = local_moments(sc.widv[layer, m, :, lanes(j)], m)
        st_start(True, layer, m)

    def out_gain(layer, j):
        both = sc.go[2 * layer + lax.div(p, 2), lax.rem(p, 2)]
        return both[0:1, lanes(j)], both[1:2, lanes(j)]

    def pre_values(layer, m):
        mean, inv = combine(True, layer, m)
        sc.inv_wide[layer, m] = inv
        mask = sc.msk[m]
        for j in range(4):
            gain, bias = out_gain(layer, j)
            vhat = (sc.widv[layer, m, :, lanes(j)] - mean[:, lanes(j)]) * inv[:, lanes(j)]
            sc.widv[layer, m, :, lanes(j)] = vhat
            pre = gain * vhat + bias + stream_part(layer, m, j)
            sig = sigmoid(pre)
            out = (mask * (pre * sig)).astype(BF16)
            if layer == 0:
                sc.pre0[m, :, lanes(j)] = pre
                sc.s1[m, :, lanes(j)] = out
            else:
                sc.mix[m, :, lanes(j)] = out
                slope = sig * (1.0 + pre * (1.0 - sig))
                grad = (cot_ref[m, :, lanes(j)].astype(F32) * mask * slope).astype(BF16)
                sc.gp[1, m, :, lanes(j)] = grad
                sc.stw[3, m, d, :, lanes(j)] = local_sums(grad.astype(F32), vhat)
        if layer == 1:
            st_start(True, 3, m)

    def put_out(k, src, dst):
        copy = pltpu.make_async_copy(src, dst, sc.out.at[k])
        copy.start()
        return copy

    def grad_out_norm(layer, m):
        sums = back_sums(True, 2 + layer, m)
        if m == 0:
            sc.gsw[layer, p] = sums
        else:
            sc.gsw[layer, p] = sc.gsw[layer, p] + sums
        mask = sc.msk[m]
        inv = sc.inv_wide[layer, m]
        for j in range(4):
            gain, _ = out_gain(layer, j)
            dz = sc.gp[layer, m, :, lanes(j)].astype(F32)
            vhat = sc.widv[layer, m, :, lanes(j)]
            s1 = sums[0:1, lanes(j)] / totals[m]
            s0 = sums[1:2, lanes(j)] / totals[m]
            dv = mask * (gain * inv[:, lanes(j)]) * (dz - s0 - vhat * s1)
            sc.gt[m, :, lanes(j)] = dv.astype(BF16)
        g = sc.gt[m]
        rs_send(
            2 + layer,
            m,
            [dot_nn(g, sc.wt[2 * layer + 1, :, 256 * j : 256 * j + 256]) for j in range(2)],
        )

    def mid_grad(i, m, upstream):
        vhat = sc.midv[i, m]
        u = sc.gm[i, 0:1, :] * vhat + sc.gm[i, 1:2, :]
        sig = sigmoid(u)
        dz = upstream * sc.msk[m] * (sig * (1.0 + u * (1.0 - sig)))
        sc.dzm[m] = dz
        sc.stm[4 + i, m, d] = local_sums(dz, vhat)
        st_start(False, 4 + i, m)

    def mid_back(i, m):
        sums = back_sums(False, 4 + i, m)
        if m == 0:
            sc.gsm[i, p] = sums
        else:
            sc.gsm[i, p] = sc.gsm[i, p] + sums
        s1 = sums[0:1, :] / totals[m]
        s0 = sums[1:2, :] / totals[m]
        scale = sc.gm[i, 0:1, :] * sc.inv_mid[i, m]
        return (sc.msk[m] * scale * (sc.dzm[m] - s0 - sc.midv[i, m] * s1)).astype(BF16)

    def grad_two(layer, m):
        mid_grad(2 * layer + 1, m, rs_sum(2 + layer, m, rs_par[2 + layer]))

    def grad_second(layer, m):
        gs = mid_back(2 * layer + 1, m)
        for k in range(9):
            if k == 4:
                sc.gb[m, :, lanes(k)] = gs
            else:
                sc.gb[m, :, lanes(k)] = dot_nn(sc.pm[m, slot_of(8 - k)], gs).astype(BF16)
        g = sc.gb[m]
        rs_send(
            4 + layer,
            m,
            [dot_nt(g, sc.k2[layer, 256 * j : 256 * j + 256, :]) for j in range(2)],
        )

    def grad_one(layer, m):
        mid_grad(2 * layer, m, rs_sum(4 + layer, m, rs_par[4 + layer]))

    def grad_first(layer, m):
        ag_start(4 + layer, m, mid_back(2 * layer, m))

    def conv_grad(layer, m):
        ag_wait(4 + layer, m)
        g = ag_value(4 + layer, m)
        mask = sc.msk[m]
        for j in range(2):
            r = dot_nt(g, sc.wt[2 * layer, 256 * j : 256 * j + 256, :]).astype(BF16)
            if layer == 0:
                sc.cv[m, :, 256 * j : 256 * j + 256] = r
                continue
            for e in range(2):
                i = 2 * j + e
                pre = sc.pre0[m, :, lanes(i)]
                sig = sigmoid(pre)
                slope = sig * (1.0 + pre * (1.0 - sig))
                up = sc.gp[1, m, :, lanes(i)].astype(F32) + r[:, lanes(e)].astype(F32)
                grad = (up * mask * slope).astype(BF16)
                sc.gp[0, m, :, lanes(i)] = grad
                sc.stw[2, m, d, :, lanes(i)] = local_sums(
                    grad.astype(F32), sc.widv[0, m, :, lanes(i)]
                )
        if layer == 1:
            st_start(True, 2, m)

    def turned(blocks):
        for m, block in enumerate(blocks):
            sc.tb[:, rows * m : rows * (m + 1)] = block.T

    def both(get):
        return jnp.concatenate([get(0), get(1)], axis=0)

    def wide_grad(s, left, right):
        turned([left(0), left(1)])
        for j in range(2):
            cols = slice(256 * j, 256 * j + 256)
            rhs = both(lambda m: right(m)[:, cols])
            for h in range(2):
                r = dot_nn(sc.tb[256 * h : 256 * h + 256, :], rhs)
                sc.dw[s, h, :, cols] = r.astype(BF16)
        pair_w(s).start()

    def taps_grad(layer):
        turned([ag_value(layer, 0), ag_value(layer, 1)])
        for j in range(5):
            width = 256 if j < 4 else 128
            rhs = both(lambda m: sc.gb[m, :, 256 * j : 256 * j + width])
            r = dot_nn(sc.tb[...], rhs).astype(BF16)
            for e in range(width // LANES):
                tap = 2 * j + e
                sc.dk[layer, 512 * tap : 512 * tap + 512, :] = r[:, lanes(e)]
        pair_k(layer).start()

    def pair_w(s):
        return remote(
            sc.dw.at[s, 1 - c], sc.prw.at[s], sc.pw_s.at[s], sc.pw_r.at[s], sibling
        )

    def other_half():
        return pl.ds(pl.multiple_of(2304 * (1 - c), 2304), 2304)

    def own_half():
        return pl.ds(pl.multiple_of(2304 * c, 2304), 2304)

    def pair_k(layer):
        return remote(
            sc.dk.at[layer, other_half()],
            sc.prk.at[layer],
            sc.pw_s.at[4 + layer],
            sc.pw_r.at[4 + layer],
            sibling,
        )

    def owner(index, body):
        if n_own == n_z:
            body()
        else:
            pl.when(index < n_own)(body)

    def z_copy(wide, s, k):
        j = lax.rem(z + k, n_z)
        if wide:
            src = sc.zsw.at[s, pl.ds(pl.multiple_of(wr * j, wr), wr)]
            dst, sem = sc.zrw.at[s, k - 1], s
        else:
            src = sc.zsk.at[s, pl.ds(pl.multiple_of(kr * j, kr), kr)]
            dst, sem = sc.zrk.at[s, k - 1], 4 + s
        return j, remote(src, dst, sc.zw_s.at[sem], sc.zw_r.at[sem], (p, 2 * j + c))

    def z_start(wide, s):
        def go(k):
            j, copy = z_copy(wide, s, k)
            owner(j, lambda: copy.start())

        each(n_z, 1, go)

    def wide_z(s):
        pair_w(s).wait_recv()
        sc.zsw[s] = (sc.dw[s, c].astype(F32) + sc.prw[s].astype(F32)).astype(BF16)
        z_start(True, s)

    def taps_z(layer):
        pair_k(layer).wait_recv()
        for i in range(4):
            part = slice(576 * i, 576 * i + 576)
            mine = pl.ds(pl.multiple_of(2304 * c + 576 * i, 576), 576)
            sc.zsk[layer, part] = (
                sc.dk[layer, mine].astype(F32) + sc.prk[layer, part].astype(F32)
            ).astype(BF16)
        z_start(False, layer)

    def wide_fin_copy(s):
        return remote(
            sc.fiw.at[s], sc.ow.at[p, c, z], sc.fw_s.at[s], sc.fw_r.at[0, p], (s, d)
        )

    def wide_pipe(s):
        def go():
            bytes_wait(sc.zrw.at[s], sc.zw_r.at[s])
            total = sc.zsw[s, pl.ds(pl.multiple_of(wr * z, wr), wr)].astype(F32)
            for k in range(n_z - 1):
                total = total + sc.zrw[s, k].astype(F32)
            sc.fiw[s] = total.astype(BF16)

            @pl.when(p == s)
            def _():
                sc.ow[p, c, z] = sc.fiw[s]

            @pl.when(p != s)
            def _():
                wide_fin_copy(s).start()

        owner(z, go)

    def wide_ag_copy(k):
        j = lax.rem(z + k, n_z)
        view = sc.ow.at[:, c, lax.rem(z, n_own)]
        return remote(view, view, sc.aw_s.at[0], sc.aw_r.at[0], (p, 2 * j + c))

    def wide_ag(s):
        def go():
            for q in range(4):
                if q != s:
                    copy = remote(
                        sc.fiw.at[s],
                        sc.ow.at[q, c, z],
                        sc.fw_s.at[s],
                        sc.fw_r.at[0, q],
                        (s, d),
                    )
                    copy.wait_recv()
            each(n_z, 1, lambda k: wide_ag_copy(k).start())

        @pl.when(p == s)
        def _():
            owner(z, go)

    def wait_pieces(view_of, sem):
        if n_own == n_z:
            bytes_wait(view_of(n_own - 1), sem)
        else:

            @pl.when(z < n_own)
            def _():
                bytes_wait(view_of(n_own - 1), sem)

            @pl.when(z >= n_own)
            def _():
                bytes_wait(view_of(n_own), sem)

    def wide_pair_copy():
        return remote(sc.ow.at[:, c], sc.ow.at[:, c], sc.bw_s.at[0], sc.bw_r.at[0], sibling)

    def wide_pair(s):
        @pl.when(p == s)
        def _():
            wait_pieces(lambda count: sc.ow.at[:, 0, pl.ds(0, count)], sc.aw_r.at[0])
            wide_pair_copy().start()

    def wide_done():
        wide_pair_copy().wait_recv()
        return [
            put_out(
                0,
                sc.ow.at[...],
                gwide_ref.at[...],
            )
        ]

    def taps_fin_copy(layer, q):
        return remote(
            sc.fik.at[layer],
            sc.ok.at[pl.ds(pl.multiple_of(kr * z, kr), kr), pl.ds(128 * q, 128)],
            sc.fw_s.at[4 + layer],
            sc.fw_r.at[1, q],
            (2 * layer + c, d),
        )

    def taps_pipe(layer):
        def go():
            bytes_wait(sc.zrk.at[layer], sc.zw_r.at[4 + layer])
            total = sc.zsk[layer, pl.ds(pl.multiple_of(kr * z, kr), kr)].astype(F32)
            for k in range(n_z - 1):
                total = total + sc.zrk[layer, k].astype(F32)
            sc.fik[layer] = total.astype(BF16)
            for q in range(4):
                if q // 2 == layer:

                    @pl.when((p == q) & (c == q % 2))
                    def _(q=q):
                        sc.ok[pl.ds(pl.multiple_of(kr * z, kr), kr), 128 * q : 128 * q + 128] = (
                            sc.fik[layer]
                        )

                    @pl.when((p == q) & (c != q % 2))
                    def _(q=q):
                        taps_fin_copy(layer, q).start()

                else:

                    @pl.when(p == q)
                    def _(q=q):
                        taps_fin_copy(layer, q).start()

        owner(z, go)

    def taps_ag_copy(k):
        j = lax.rem(z + k, n_z)
        view = sc.ok.at[pl.ds(pl.multiple_of(kr * lax.rem(z, n_own), kr), kr)]
        return remote(view, view, sc.aw_s.at[1], sc.aw_r.at[1], (p, 2 * j + c))

    def taps_ag(layer):
        for h in range(2):
            s = 2 * layer + h

            def go(s=s):
                for q in range(4):
                    if q != s:
                        taps_fin_copy(layer, q).wait_recv()
                each(n_z, 1, lambda k: taps_ag_copy(k).start())

            @pl.when((p == s) & (c == h))
            def _(go=go):
                owner(z, go)

    def taps_pair_copy():
        return remote(sc.ok.at[...], sc.ok.at[...], sc.bw_s.at[1], sc.bw_r.at[1], sibling)

    def taps_pair(layer):
        @pl.when((lax.div(p, 2) == layer) & (c == parity))
        def _():
            wait_pieces(lambda count: sc.ok.at[pl.ds(0, kr * count)], sc.aw_r.at[1])
            taps_pair_copy().start()

    def taps_done():
        @pl.when(c != parity)
        def _():
            taps_pair_copy().wait_recv()

        return [put_out(1, sc.ok.at[...], gtaps_ref.at[...])]

    def finish_grads():
        for wide, s in [(True, s) for s in range(4)] + [(False, layer) for layer in range(2)]:
            (pair_w if wide else pair_k)(s).wait_send()

            def sent(k, wide=wide, s=s):
                j, copy = z_copy(wide, s, k)
                owner(j, lambda: copy.wait_send())

            each(n_z, 1, sent)

        def pieces():
            for s in range(4):

                @pl.when(p != s)
                def _(s=s):
                    wide_fin_copy(s).wait_send()

            for layer in range(2):

                @pl.when(p != 2 * layer + c)
                def _(layer=layer):
                    taps_fin_copy(layer, 0).wait_send()

            each(n_z, 1, lambda k: wide_ag_copy(k).wait_send())

            @pl.when(c == parity)
            def _():
                each(n_z, 1, lambda k: taps_ag_copy(k).wait_send())

        owner(z, pieces)
        wide_pair_copy().wait_send()

        @pl.when(c == parity)
        def _():
            taps_pair_copy().wait_send()

    finish.append(finish_grads)

    def gain_copies(off):
        dev = (pipe_at(off), d)
        return [
            remote(
                sc.gsm.at[:, p], sc.gsm.at[:, p], sc.g_s.at[off - 1, 0], sc.g_r.at[off - 1, 0], dev
            ),
            remote(
                sc.gsw.at[:, p], sc.gsw.at[:, p], sc.g_s.at[off - 1, 1], sc.g_r.at[off - 1, 1], dev
            ),
        ]

    def gains_start():
        for off in range(1, 4):
            for copy in gain_copies(off):
                copy.start()

    def gains_done():
        for off in range(1, 4):
            for copy in gain_copies(off):
                copy.wait_recv()
        for q in range(4):
            gmid_ref[0, :, lanes(q)] = sc.gsm[p, q]
        layer = lax.div(p, 2)
        for e in range(2):
            gout_ref[0, :, 512 * e : 512 * e + 512] = sc.gsw[layer, 2 * parity + e]

    def finish_gains():
        for off in range(1, 4):
            for copy in gain_copies(off):
                copy.wait_send()

    finish.append(finish_gains)

    def phase(body, layer):
        for m in range(2):
            body(layer, m)

    relay_wide(0)
    ready_wide(0)
    phase(first_part, 0)
    own_n.wait()
    for off in range(1, 4):
        for copy in send_norm(off):
            copy.wait_recv()
    phase(first_norm, 0)
    phase(hidden_one, 0)
    start_wide(2)
    start_taps(2)
    start_taps(3)
    start_wide(3)
    relay_taps(0)
    relay_taps(1)
    ready_taps(0)
    ready_taps(1)
    phase(second_part, 0)
    relay_wide(1)
    phase(hidden_two, 0)
    ready_wide(1)
    phase(third_part, 0)
    relay_wide(2)
    ready_wide(2)

    def turn(layer, m):
        pre_values(0, m)
        first_part(1, m)

    phase(turn, 0)
    phase(first_norm, 1)
    relay_taps(2)
    relay_taps(3)
    phase(hidden_one, 1)
    ready_taps(2)
    ready_taps(3)
    phase(second_part, 1)
    relay_wide(3)
    phase(hidden_two, 1)
    ready_wide(3)
    phase(third_part, 1)
    phase(pre_values, 1)
    outs = [put_out(2, sc.mix.at[...], mixed_ref.at[...])]

    phase(grad_out_norm, 1)
    wide_grad(3, lambda m: sc.gt[m], lambda m: ag_value(3, m))
    phase(grad_two, 1)
    wide_z(3)
    phase(grad_second, 1)
    taps_grad(1)
    phase(grad_one, 1)
    wide_pipe(3)
    taps_z(1)
    phase(grad_first, 1)
    wide_ag(3)
    phase(conv_grad, 1)
    outs.append(put_out(3, sc.gp.at[0], gpre_ref.at[...]))
    wide_grad(2, lambda m: sc.s1[m], lambda m: ag_value(5, m))
    phase(grad_out_norm, 0)
    wide_grad(1, lambda m: sc.gt[m], lambda m: ag_value(2, m))
    wide_z(2)
    phase(grad_two, 0)
    wide_z(1)
    taps_pipe(1)
    phase(grad_second, 0)
    taps_grad(0)
    wide_pipe(2)
    phase(grad_one, 0)
    taps_z(0)
    wide_pipe(1)
    taps_ag(1)
    phase(grad_first, 0)
    gains_start()
    wide_ag(2)
    wide_ag(1)
    phase(conv_grad, 0)
    outs.append(put_out(4, sc.cv.at[...], conv_ref.at[...]))
    wide_grad(0, lambda m: x_ref[m], lambda m: ag_value(4, m))
    taps_pipe(0)
    wide_z(0)
    gains_done()
    taps_ag(0)
    wide_pipe(0)
    taps_pair(1)
    wide_pair(3)
    wide_ag(0)
    wide_pair(2)
    wide_pair(1)
    taps_pair(0)
    outs.extend(taps_done())
    wide_pair(0)
    outs.extend(wide_done())
    for copy in outs:
        copy.wait()
    for body in finish:
        body()


def local(block_input, cotangent, weight_wide, weight_taps, norm_mid, norm_out, group_counts):
    n_dp = group_counts.shape[1]
    micro, rows, width = block_input.shape
    n_z, n_own, wr, kr = sizes(n_dp, rows)
    scratch = scratch_list(n_dp, rows)
    vmem = pl.BlockSpec(memory_space=pltpu.VMEM)
    smem = pl.BlockSpec(memory_space=pltpu.SMEM)
    anywhere = pl.BlockSpec(memory_space=pl.ANY)

    def shape(dims, dtype):
        return jax.ShapeDtypeStruct(dims, dtype)

    stream = (micro, rows, width)
    mixed, gpre, conv, gwide, gtaps, gmid, gout = pl.pallas_call(
        functools.partial(kernel, list(scratch), n_dp),
        out_shape=[
            shape(stream, BF16),
            shape(stream, BF16),
            shape(stream, BF16),
            shape((4, 2, n_own, wr, 512), BF16),
            shape((2304, 512), BF16),
            shape(norm_mid.shape, F32),
            shape(norm_out.shape, F32),
        ],
        in_specs=[vmem, vmem, anywhere, anywhere, vmem, vmem, smem],
        out_specs=[anywhere] * 5 + [vmem] * 2,
        scratch_shapes=list(scratch.values()),
        compiler_params=pltpu.CompilerParams(
            collective_id=0, has_side_effects=True, vmem_limit_bytes=62 * 2**20
        ),
        name="layers",
    )(block_input, cotangent, weight_wide, weight_taps, norm_mid, norm_out, group_counts)
    grad_input = gpre.astype(F32) + conv.astype(F32)
    return (
        mixed,
        grad_input,
        gwide.astype(F32).reshape(weight_wide.shape),
        gtaps.astype(F32).reshape(weight_taps.shape),
        gmid,
        gout,
    )


def solution(mesh):
    split = P(None, "dp", "pipe")
    section = P("pipe", None, None)
    return jax.shard_map(
        local,
        mesh=mesh,
        in_specs=(split, split, section, section, section, section, P()),
        out_specs=(split, split, section, section, section, section),
        check_vma=False,
    )
```

time: 1940 us -> 318 us (0.16)
  waiting for transfers between devices: 619 us -> 0 us
  blocking collectives: 482 us -> 0 us
  local copies, waits for them, and re-layouts: 319 us -> 3.45 us
  other arithmetic: 312 us -> 8.36 us
  Pallas kernels: 0 us -> 303 us
  matrix products: 92.7 us -> 0 us
  starting transfers between devices: 76.8 us -> 0 us
    psum x30 -> x0, blocking collectives: 482 us -> none  [the longest x10 202 us: norm_sums(): lax.psum(jnp.stack([jnp.sum(upstream * normed, 0), jnp.sum(upstream, 0)])...]
    pallas_call x0 -> x1, Pallas kernels: none -> 303 us  [local(): pl.pallas_call(functools.partial(kernel, list(scratch), n_dp), out_shape=...]
    ppermute x29 -> x0, waiting for transfers between devices: 281 us -> none  [passed_along(): return lax.ppermute(block, axis, route)]
    gather x70 -> x0, local copies, waits for them, and re-layouts: 201 us -> none  [the longest x45 113 us: gather_taps(): jnp.take(hidden, neighbour[:, tap_id], axis=0)]
    psum x1 -> x0, waiting for transfers between devices: 173 us -> none  [local(): wide_total, taps_total = lax.psum((sum_wide, sum_taps), 'dp')]
    reduce_scatter x2 -> x0, waiting for transfers between devices: 119 us -> none  [the longest x1 119 us: local(): lax.psum_scatter(outer_term.astype(jnp.bfloat16), 'pipe', scatter_dimensi...]
    dot_general x34 -> x0, matrix products: 92.7 us -> none  [the longest x10 25.7 us: front_first(): jnp.dot(input_rows, wide_weight, preferred_element_type=float_type)]
    ppermute x29 -> x0, starting transfers between devices: 76.6 us -> none  [passed_along(): return lax.ppermute(block, axis, route)]
  transfers between devices with their start and end apart: 34 -> 0, of which waited for: 19 -> 0; matrix products, arithmetic and copies ran while one was open for 11% -> 0% of each run, Pallas kernels for 0% -> 0%
where the time goes in v1:
time: 318 us; the launch traced here: 315 us
  Pallas kernels  303 us (95%)
  other arithmetic  8.36 us (3%)
  local copies, waits for them, and re-layouts  3.45 us (1%)
    pallas_call x1, Pallas kernels, local(): pl.pallas_call(functools.partial(kernel, list(scratch), n_dp), out_shape=...  303 us

profile of v1, /device:TPU:0, one launch (start us, length us, event | category | flops | bytes accessed | tf_op | source)
XLA Modules:
  0.0 315.0 jit_solution(13259002890255973726)
XLA Ops:
  0.6 1.4 copy.13.refs_6_
  2.0 302.6 %layers.1 = (bf16[2,384,512]{2,1,0:T(8,128)(2,1)}, bf16[2,384,512]{2,1,0:T(8,128)(2,1)}, bf16[2,384,512]{2,1,0:T(8,128)(2,1)}, bf16[4,2,4,64,512]{4,3,2,1,0:T(8,...) custom-call(bf16[2,384,512]{2,1,0:T(8,128)(2,1)} %refs_0_.1, ...), custom_call_target="tpu_custom_call" | custom-call | tf_op jit(solution)/shard_map/layers/pallas_call | solution.py:1183
  304.6 0.0 copy-start
  304.6 2.9 convert_add_fusion
  307.5 0.0 copy-done
  307.5 0.0 copy-start.1
  307.5 2.9 bitcast_convert_fusion
  310.4 0.0 copy-done.1
  310.4 0.0 copy-start.2
  310.4 0.0 copy-start.4
  310.4 0.0 copy-start.3
  310.4 2.6 convert.2
  313.0 0.0 copy-done.2
  313.0 0.9 copy.17
  313.9 0.0 copy-done.4
  313.9 0.6 copy.18
  314.4 0.0 copy-done.3
  314.4 0.6 copy.19
Async XLA Ops:
  304.6 2.9 copy-start
  307.5 2.9 copy-start.1
  310.4 2.6 copy-start.2
  310.4 3.5 %copy-start.4 = (f32[1,2,512]{2,1,0:T(2,128)S(1)}, f32[1,2,512]{2,1,0:T(2,128)}, u32[]{:S(2)}) copy-start(f32[1,2,512]{2,1,0:T(2,128)} %get-tuple-element.30) | copy-start | bytes 12292
  310.4 4.1 %copy-start.3 = (f32[1,2,1024]{2,1,0:T(2,128)S(1)}, f32[1,2,1024]{2,1,0:T(2,128)}, u32[]{:S(2)}) copy-start(f32[1,2,1024]{2,1,0:T(2,128)} %get-tuple-element.31) | copy-start | bytes 24580

commit v2 on v1

--- a/solution.py
+++ b/solution.py
@@ -33,14 +33,41 @@
     return jax.nn.sigmoid(v)
 
 
-def sizes(n_dp, rows):
+def sizes(n_dp):
     n_z = n_dp // 2
     n_own = min(n_z, 16)
-    return n_z, n_own, 256 // n_own, 2304 // n_own
+    return n_z, n_own
+
+
+def gradient_items(n_dp):
+    line = n_dp // 2 == 4
+    listed = []
+    for kind, index, chunks in (
+        ("w", 3, 1),
+        ("k", 1, 2 if line else 1),
+        ("w", 2, 1),
+        ("w", 1, 1),
+        ("k", 0, 4 if line else 1),
+        ("w", 0, 2 if line else 1),
+    ):
+        total = 256 if kind == "w" else 2304
+        for part in range(chunks):
+            listed.append(
+                SimpleNamespace(
+                    kind=kind,
+                    t=index,
+                    r0=total // chunks * part,
+                    nr=total // chunks,
+                    i=len(listed),
+                )
+            )
+    return listed
 
 
 def scratch_list(n_dp, rows):
-    n_z, n_own, wr, kr = sizes(n_dp, rows)
+    n_z, n_own = sizes(n_dp)
+    items = len(gradient_items(n_dp))
+    line = n_z == 4
     dma = pltpu.SemaphoreType.DMA
 
     def half(*shape):
@@ -51,7 +78,7 @@
 
     return dict(
         wt=half(4, 512, 512),
-        k2=half(2, 512, 1152),
+        k2=half(2, 18, 256, 128),
         gm=full(4, 2, 128),
         go=full(4, 2, 2, 512),
         msk=full(2, rows, 128),
@@ -78,24 +105,26 @@
         dw=half(4, 2, 256, 512),
         prw=half(4, 256, 512),
         zsw=half(4, 256, 512),
-        zrw=half(4, n_z - 1, wr, 512),
-        fiw=half(4, wr, 512),
-        ow=half(4, 2, n_own, wr, 512),
+        fzw=half(4, 256, 512),
+        ow=half(4, 2, 256, 512),
         dk=half(2, 4608, 128),
         prk=half(2, 2304, 128),
         zsk=half(2, 2304, 128),
-        zrk=half(2, n_z - 1, kr, 128),
-        fik=half(2, kr, 128),
+        fzk=half(2, 2304, 128),
         ok=half(2304, 512),
+        zow=half(4, 256, 512) if line else half(4, n_z - 1, 256 // n_own, 512),
+        ziw=half(4, 128, 512),
+        zok=half(2, 2304, 128) if line else half(2, n_z - 1, 2304 // n_own, 128),
+        zik=half(2, 1152, 128),
         gsm=full(4, 4, 2, 128),
         gsw=full(2, 4, 2, 512),
         cnt=pltpu.SMEM((2, n_dp), F32),
-        w_s=dma((3,)),
-        w_r=dma((4,)),
-        w_f=dma((4,)),
-        k_s=dma((3, 5)),
-        k_r=dma((4, 5)),
-        k_f=dma((4, 5)),
+        f_s=dma((2, 3)),
+        f_r=dma((2, 4)),
+        z_s=dma((2, 4)),
+        z_r=dma((2, 4)),
+        b_s=dma((2, 4, 2)),
+        b_r=dma((2, 4, 2)),
         n_s=dma((3, 3)),
         n_r=dma((3, 3)),
         loc=dma((8,)),
@@ -109,14 +138,18 @@
         stw_r=dma((4, 2)),
         pw_s=dma((6,)),
         pw_r=dma((6,)),
-        zw_s=dma((6,)),
-        zw_r=dma((6,)),
-        fw_s=dma((6,)),
-        fw_r=dma((2, 4)),
-        aw_s=dma((2,)),
-        aw_r=dma((2,)),
-        bw_s=dma((2,)),
-        bw_r=dma((2,)),
+        up_s=dma((items,)),
+        up_r=dma((items,)),
+        mid_s=dma((items,)),
+        mid_r=dma((items,)),
+        inn_s=dma((items,)),
+        inn_r=dma((items,)),
+        dn_s=dma((items, 2)),
+        dn_r=dma((items, 2)),
+        to_s=dma((items,)),
+        to_r=dma((items, 4)),
+        sib_s=dma((items, 4)),
+        sib_r=dma((items, 4)),
         g_s=dma((3, 2)),
         g_r=dma((3, 2)),
         out=dma((8,)),
@@ -128,13 +161,17 @@
     (mixed_ref, gpre_ref, conv_ref, gwide_ref, gtaps_ref, gmid_ref, gout_ref) = refs[7:14]
     sc = SimpleNamespace(**dict(zip(names, refs[14:])))
     rows = x_ref.shape[1]
-    n_z, n_own, wr, kr = sizes(n, rows)
+    n_z, n_own = sizes(n)
     p = lax.axis_index("pipe")
     d = lax.axis_index("dp")
     z = lax.div(d, 2)
     c = lax.rem(d, 2)
     parity = lax.rem(p, 2)
     sibling = (p, 2 * z + 1 - c)
+    z_odd = lax.rem(z, 2)
+    z_pair = (p, 2 * (z + 1 - 2 * z_odd) + c)
+    quarter = 2 * z_odd + c
+    quarter_z = 2 * (1 - z_odd) + c
     finish = []
 
     def pipe_at(off):
@@ -171,39 +208,19 @@
 
     each(n, 1, greet)
 
+    def columns_of(q):
+        return pl.ds(pl.multiple_of(128 * q, 128), 128)
+
     own_w = pltpu.make_async_copy(
         wide_ref.at[0, pl.ds(pl.multiple_of(512 * p, 512), 512), :], sc.wt.at[p], sc.loc.at[0]
     )
+    own_k = pltpu.make_async_copy(
+        taps_ref.at[:, :, columns_of(p)],
+        sc.k2.at[lax.div(p, 2), pl.ds(9 * parity, 9)],
+        sc.loc.at[1],
+    )
     own_w.start()
-
-    def tap_parts(h, column):
-        layer = h // 2
-        odd = h % 2
-        listed = [
-            (
-                taps_ref.at[0, pl.ds(512 * i + 256 * odd, 512), column],
-                (layer, pl.ds(0, 512), pl.ds(128 * (i + 5 * odd), 128)),
-            )
-            for i in range(4)
-        ]
-        listed.append(
-            (
-                taps_ref.at[0, pl.ds(2048 * (1 - odd), 256), column],
-                (layer, pl.ds(256 * odd, 256), pl.ds(512, 128)),
-            )
-        )
-        return listed
-
-    def columns_of(q):
-        return pl.ds(pl.multiple_of(128 * q, 128), 128)
-
-    for s in range(4):
-
-        @pl.when(p == s)
-        def _(s=s):
-            for i, (src, dst) in enumerate(tap_parts(s, columns_of(p))):
-                pltpu.make_async_copy(src, sc.k2.at[dst], sc.loc.at[1 + i]).start()
-
+    own_k.start()
     own_n = pltpu.make_async_copy(
         nmid_ref.at[0, :, columns_of(p)], sc.gm.at[p], sc.loc.at[6]
     )
@@ -231,24 +248,23 @@
 
     pl.semaphore_wait(barrier, N_PIPE - 1 + n - 1)
 
-    def send_wide(off):
+    def held(kind, s, part):
+        if kind == 0:
+            return sc.wt.at[s, pl.ds(pl.multiple_of(128 * part, 128), 128)]
+        layer, odd = (s // 2, s % 2) if isinstance(s, int) else (lax.div(s, 2), lax.rem(s, 2))
+        return sc.k2.at[
+            layer, pl.ds(9 * odd, 9), pl.ds(pl.multiple_of(64 * part, 64), 64)
+        ]
+
+    def fetch(kind, off):
         q = pipe_at(off)
+        if kind == 0:
+            src = wide_ref.at[0, pl.ds(pl.multiple_of(512 * q + 128 * quarter, 128), 128), :]
+        else:
+            src = taps_ref.at[:, pl.ds(pl.multiple_of(64 * quarter, 64), 64), columns_of(q)]
         return remote(
-            wide_ref.at[0, pl.ds(pl.multiple_of(512 * q, 512), 512), :],
-            sc.wt.at[p],
-            sc.w_s.at[off - 1],
-            sc.w_r.at[p],
-            (q, d),
-        )
-
-    def send_taps(s, off):
-        q = pipe_at(off)
-        return [
-            remote(
-                src, sc.k2.at[dst], sc.k_s.at[off - 1, i], sc.k_r.at[p, i], (q, d)
-            )
-            for i, (src, dst) in enumerate(tap_parts(s, columns_of(q)))
-        ]
+            src, held(kind, p, quarter), sc.f_s.at[kind, off - 1], sc.f_r.at[kind, p], (q, d)
+        )
 
     def send_norm(off):
         q = pipe_at(off)
@@ -273,88 +289,63 @@
             )
         return listed
 
-    def start_wide(s):
-        @pl.when((p == s) & (c == s % 2))
+    def pass_z(kind, s):
+        view = held(kind, s, quarter)
+        return remote(view, view, sc.z_s.at[kind, s], sc.z_r.at[kind, s], z_pair)
+
+    def pass_sibling(kind, s, e):
+        view = held(kind, s, quarter if e == 0 else quarter_z)
+        return remote(view, view, sc.b_s.at[kind, s, e], sc.b_r.at[kind, s, e], sibling)
+
+    def spread_first(kind, s):
+        @pl.when(p != s)
         def _():
-            for off in range(1, 4):
-                send_wide(off).start()
-
-    def start_taps(s):
-        @pl.when((p == s) & (c == s % 2))
+            view = held(kind, s, quarter)
+            bytes_wait(view, sc.f_r.at[kind, s])
+            pass_z(kind, s).start()
+            pass_sibling(kind, s, 0).start()
+
+    def spread_second(kind, s):
+        @pl.when(p != s)
         def _():
-            for off in range(1, 4):
-                for copy in send_taps(s, off):
-                    copy.start()
-
-    def finish_weights():
-        for s in range(4):
-
-            @pl.when((p == s) & (c == s % 2))
-            def _(s=s):
-                for off in range(1, 4):
-                    send_wide(off).wait_send()
-                    for copy in send_taps(s, off):
-                        copy.wait_send()
-
-            @pl.when((p != s) & (c == s % 2))
-            def _(s=s):
-                pass_wide(s).wait_send()
-                for copy in pass_taps(s):
-                    copy.wait_send()
-
-    finish.append(finish_weights)
-
-    def pass_wide(s):
-        return remote(sc.wt.at[s], sc.wt.at[s], sc.w_f.at[s], sc.w_r.at[s], sibling)
-
-    def pass_taps(s):
-        return [
-            remote(
-                sc.k2.at[dst], sc.k2.at[dst], sc.k_f.at[s, i], sc.k_r.at[s, i], sibling
-            )
-            for i, (_, dst) in enumerate(tap_parts(s, pl.ds(0, 128)))
-        ]
-
-    def relay_wide(s):
-        @pl.when((p != s) & (c == s % 2))
+            pass_z(kind, s).wait_recv()
+            pass_sibling(kind, s, 1).start()
+
+    def ready(kind, s):
+        @pl.when(p != s)
         def _():
-            copy = pass_wide(s)
-            copy.wait_recv()
-            copy.start()
-
-    def ready_wide(s):
-        @pl.when((p != s) & (c != s % 2))
-        def _():
-            pass_wide(s).wait_recv()
-
-        if s == 0:
-            own_w.wait()
-
-    def relay_taps(s):
-        @pl.when((p != s) & (c == s % 2))
-        def _():
-            for copy in pass_taps(s):
-                copy.wait_recv()
-                copy.start()
-
-    def ready_taps(s):
-        @pl.when((p != s) & (c != s % 2))
-        def _():
-            for copy in pass_taps(s):
-                copy.wait_recv()
+            for e in range(2):
+                pass_sibling(kind, s, e).wait_recv()
 
         @pl.when(p == s)
         def _():
-            for i, (src, dst) in enumerate(tap_parts(s, columns_of(p))):
-                pltpu.make_async_copy(src, sc.k2.at[dst], sc.loc.at[1 + i]).wait()
-
-    start_wide(0)
-    for off in range(1, 4):
-        for copy in send_norm(off):
-            copy.start()
-    start_taps(0)
-    start_taps(1)
-    start_wide(1)
+            (own_w if kind == 0 else own_k).wait()
+
+    def finish_weights():
+        for kind in range(2):
+            for off in range(1, 4):
+                fetch(kind, off).wait_send()
+            for s in range(4):
+
+                @pl.when(p != s)
+                def _(kind=kind, s=s):
+                    pass_z(kind, s).wait_send()
+                    for e in range(2):
+                        pass_sibling(kind, s, e).wait_send()
+
+    finish.append(finish_weights)
+
+    for even in range(2):
+
+        @pl.when(parity == even)
+        def _(even=even):
+            for kind in (even, 1 - even):
+                for off in range(1, 4):
+                    fetch(kind, off).start()
+                if kind == even:
+                    for off in range(1, 4):
+                        for copy in send_norm(off):
+                            copy.start()
 
     def finish_norm():
         for off in range(1, 4):
@@ -409,8 +400,6 @@
     for m in range(2):
         build(m)
 
-    rs_last = {0: None, 1: None}
-    rs_turn = [0]
 
     def rs_copies(rid, m, par):
         listed = []
@@ -427,11 +416,6 @@
             )
         return listed
 
-    def rs_open(rid, m, par):
-        if rs_last[par] is not None:
-            for copy in rs_copies(rs_last[par], m, par):
-                copy.wait_send()
-
     def rs_start(rid, m, par):
         for copy in rs_copies(rid, m, par):
             copy.start()
@@ -604,13 +588,22 @@
     def hidden_one(layer, m):
         ag_start(layer, m, mid_hidden(2 * layer, m))
 
+    def taps_of(layer, taps):
+        return jnp.concatenate(
+            [
+                jnp.concatenate([sc.k2[layer, 2 * k], sc.k2[layer, 2 * k + 1]], axis=0)
+                for k in taps
+            ],
+            axis=1,
+        )
+
     def second_part(layer, m):
         ag_wait(layer, m)
         h = ag_value(layer, m)
         centre = None
         for j in range(5):
             width = 256 if j < 4 else 128
-            y = dot_nn(h, sc.k2[layer, :, 256 * j : 256 * j + width])
+            y = dot_nn(h, taps_of(layer, [2 * j + e for e in range(width // LANES)]))
             for e in range(width // LANES):
                 tap = 2 * j + e
                 if tap == 4:
@@ -726,7 +719,12 @@
         rs_send(
             4 + layer,
             m,
-            [dot_nt(g, sc.k2[layer, 256 * j : 256 * j + 256, :]) for j in range(2)],
+            [
+                dot_nt(
+                    g, jnp.concatenate([sc.k2[layer, 2 * k + j] for k in range(9)], axis=1)
+                )
+                for j in range(2)
+            ],
         )
 
     def grad_one(layer, m):
@@ -773,7 +771,7 @@
             for h in range(2):
                 r = dot_nn(sc.tb[256 * h : 256 * h + 256, :], rhs)
                 sc.dw[s, h, :, cols] = r.astype(BF16)
-        pair_w(s).start()
+        pair_copy("w", s).start()
 
     def taps_grad(layer):
         turned([ag_value(layer, 0), ag_value(layer, 1)])
@@ -784,27 +782,78 @@
             for e in range(width // LANES):
                 tap = 2 * j + e
                 sc.dk[layer, 512 * tap : 512 * tap + 512, :] = r[:, lanes(e)]
-        pair_k(layer).start()
-
-    def pair_w(s):
+        pair_copy("k", layer).start()
+
+    def half_rows(which):
+        return pl.ds(pl.multiple_of(2304 * which, 2304), 2304)
+
+    def pair_copy(kind, t):
+        if kind == "w":
+            src, dst, i = sc.dw.at[t, 1 - c], sc.prw.at[t], t
+        else:
+            src, dst, i = sc.dk.at[t, half_rows(1 - c)], sc.prk.at[t], 4 + t
+        return remote(src, dst, sc.pw_s.at[i], sc.pw_r.at[i], sibling)
+
+    def pair_sum(kind, t):
+        pair_copy(kind, t).wait_recv()
+        if kind == "w":
+            sc.zsw[t] = (sc.dw[t, c].astype(F32) + sc.prw[t].astype(F32)).astype(BF16)
+            return
+        for i in range(4):
+            part = slice(576 * i, 576 * i + 576)
+            mine = pl.ds(pl.multiple_of(2304 * c + 576 * i, 576), 576)
+            sc.zsk[t, part] = (
+                sc.dk[t, mine].astype(F32) + sc.prk[t, part].astype(F32)
+            ).astype(BF16)
+
+    items = gradient_items(n)
+    line = n_z == 4
+    inner = (z == 1) | (z == 2)
+
+    def tile(it, name):
+        return getattr(sc, name + it.kind)
+
+    def some(it, name, start, count):
+        return tile(it, name).at[it.t, pl.ds(start, count)]
+
+    def part_rows(it, which):
+        half = it.nr // 2
+        return pl.ds(pl.multiple_of(it.r0 + half * which, half), half)
+
+    def up_copy(it):
+        rows_of = pl.ds(it.r0, it.nr)
         return remote(
-            sc.dw.at[s, 1 - c], sc.prw.at[s], sc.pw_s.at[s], sc.pw_r.at[s], sibling
-        )
-
-    def other_half():
-        return pl.ds(pl.multiple_of(2304 * (1 - c), 2304), 2304)
-
-    def own_half():
-        return pl.ds(pl.multiple_of(2304 * c, 2304), 2304)
-
-    def pair_k(layer):
+            tile(it, "zs").at[it.t, rows_of],
+            tile(it, "zo").at[it.t, rows_of],
+            sc.up_s.at[it.i],
+            sc.up_r.at[it.i],
+            (p, 2 * (1 + lax.div(z, 3)) + c),
+        )
+
+    def mid_copy(it):
         return remote(
-            sc.dk.at[layer, other_half()],
-            sc.prk.at[layer],
-            sc.pw_s.at[4 + layer],
-            sc.pw_r.at[4 + layer],
-            sibling,
-        )
+            tile(it, "zs").at[it.t, part_rows(it, 2 - z)],
+            tile(it, "zi").at[it.t, pl.ds(it.r0 // 2, it.nr // 2)],
+            sc.mid_s.at[it.i],
+            sc.mid_r.at[it.i],
+            (p, 2 * (3 - z) + c),
+        )
+
+    def inn_copy(it):
+        view = tile(it, "fz").at[it.t, part_rows(it, z - 1)]
+        return remote(
+            view, view, sc.inn_s.at[it.i], sc.inn_r.at[it.i], (p, 2 * (3 - z) + c)
+        )
+
+    def down_copy(it, e):
+        view = tile(it, "fz").at[it.t, part_rows(it, z - 1 if e == 0 else 2 - z)]
+        return remote(
+            view, view, sc.dn_s.at[it.i, e], sc.dn_r.at[it.i, e], (p, 2 * (3 * (z - 1)) + c)
+        )
+
+    def direct_rows(it, j):
+        count = it.nr // n_own
+        return pl.ds(pl.multiple_of(it.r0 + count * j, count), count)
 
     def owner(index, body):
         if n_own == n_z:
@@ -812,223 +861,211 @@
         else:
             pl.when(index < n_own)(body)
 
-    def z_copy(wide, s, k):
+    def scatter_copy(it, k):
         j = lax.rem(z + k, n_z)
-        if wide:
-            src = sc.zsw.at[s, pl.ds(pl.multiple_of(wr * j, wr), wr)]
-            dst, sem = sc.zrw.at[s, k - 1], s
+        return j, remote(
+            tile(it, "zs").at[it.t, direct_rows(it, lax.rem(j, n_own))],
+            tile(it, "zo").at[it.t, k - 1],
+            sc.up_s.at[it.i],
+            sc.up_r.at[it.i],
+            (p, 2 * j + c),
+        )
+
+    def gather_copy(it, k):
+        j = lax.rem(z + k, n_z)
+        view = tile(it, "fz").at[it.t, direct_rows(it, lax.rem(z, n_own))]
+        return remote(view, view, sc.dn_s.at[it.i, 0], sc.dn_r.at[it.i, 0], (p, 2 * j + c))
+
+    def add_rows(target, first, second):
+        target[...] = (first[...].astype(F32) + second[...].astype(F32)).astype(BF16)
+
+    def step_up(it):
+        if line:
+
+            @pl.when((z == 0) | (z == 3))
+            def _():
+                up_copy(it).start()
+
         else:
-            src = sc.zsk.at[s, pl.ds(pl.multiple_of(kr * j, kr), kr)]
-            dst, sem = sc.zrk.at[s, k - 1], 4 + s
-        return j, remote(src, dst, sc.zw_s.at[sem], sc.zw_r.at[sem], (p, 2 * j + c))
-
-    def z_start(wide, s):
-        def go(k):
-            j, copy = z_copy(wide, s, k)
-            owner(j, lambda: copy.start())
-
-        each(n_z, 1, go)
-
-    def wide_z(s):
-        pair_w(s).wait_recv()
-        sc.zsw[s] = (sc.dw[s, c].astype(F32) + sc.prw[s].astype(F32)).astype(BF16)
-        z_start(True, s)
-
-    def taps_z(layer):
-        pair_k(layer).wait_recv()
-        for i in range(4):
-            part = slice(576 * i, 576 * i + 576)
-            mine = pl.ds(pl.multiple_of(2304 * c + 576 * i, 576), 576)
-            sc.zsk[layer, part] = (
-                sc.dk[layer, mine].astype(F32) + sc.prk[layer, part].astype(F32)
-            ).astype(BF16)
-        z_start(False, layer)
-
-    def wide_fin_copy(s):
+
+            def go(k):
+                j, copy = scatter_copy(it, k)
+                owner(j, lambda: copy.start())
+
+            each(n_z, 1, go)
+
+    def step_mid(it):
+        if not line:
+            return
+
+        @pl.when(inner)
+        def _():
+            up_copy(it).wait_recv()
+            mine = some(it, "zs", it.r0, it.nr)
+            add_rows(mine, mine, some(it, "zo", it.r0, it.nr))
+            mid_copy(it).start()
+
+    def step_down(it):
+        if line:
+
+            @pl.when(inner)
+            def _():
+                mid_copy(it).wait_recv()
+                keep = part_rows(it, z - 1)
+                add_rows(
+                    tile(it, "fz").at[it.t, keep],
+                    tile(it, "zs").at[it.t, keep],
+                    some(it, "zi", it.r0 // 2, it.nr // 2),
+                )
+                inn_copy(it).start()
+                down_copy(it, 0).start()
+
+            return
+
+        def go():
+            bytes_wait(tile(it, "zo").at[it.t], sc.up_r.at[it.i])
+            mine = direct_rows(it, z)
+            total = tile(it, "zs")[it.t, mine].astype(F32)
+            total = lax.fori_loop(
+                0, n_z - 1, lambda k, acc: acc + tile(it, "zo")[it.t, k].astype(F32), total
+            )
+            tile(it, "fz")[it.t, mine] = total.astype(BF16)
+            each(n_z, 1, lambda k: gather_copy(it, k).start())
+
+        owner(z, go)
+
+    def step_last(it):
+        if not line:
+            return
+
+        @pl.when(inner)
+        def _():
+            inn_copy(it).wait_recv()
+            down_copy(it, 1).start()
+
+    def owner_of(it):
+        return it.t if it.kind == "w" else 2 * it.t + c
+
+    def landing(it, q, core):
+        if it.kind == "w":
+            return sc.ow.at[q, core, pl.ds(it.r0, it.nr)]
+        lane = pl.ds(128 * q, 128) if isinstance(q, int) else columns_of(q)
+        return sc.ok.at[pl.ds(it.r0, it.nr), lane]
+
+    def to_copy(it):
         return remote(
-            sc.fiw.at[s], sc.ow.at[p, c, z], sc.fw_s.at[s], sc.fw_r.at[0, p], (s, d)
-        )
-
-    def wide_pipe(s):
-        def go():
-            bytes_wait(sc.zrw.at[s], sc.zw_r.at[s])
-            total = sc.zsw[s, pl.ds(pl.multiple_of(wr * z, wr), wr)].astype(F32)
-            for k in range(n_z - 1):
-                total = total + sc.zrw[s, k].astype(F32)
-            sc.fiw[s] = total.astype(BF16)
-
-            @pl.when(p == s)
+            some(it, "fz", it.r0, it.nr),
+            landing(it, p, c),
+            sc.to_s.at[it.i],
+            sc.to_r.at[it.i, p],
+            (owner_of(it), d),
+        )
+
+    def step_out(it):
+        if line:
+
+            @pl.when((z == 0) | (z == 3))
             def _():
-                sc.ow[p, c, z] = sc.fiw[s]
-
-            @pl.when(p != s)
-            def _():
-                wide_fin_copy(s).start()
-
-        owner(z, go)
-
-    def wide_ag_copy(k):
-        j = lax.rem(z + k, n_z)
-        view = sc.ow.at[:, c, lax.rem(z, n_own)]
-        return remote(view, view, sc.aw_s.at[0], sc.aw_r.at[0], (p, 2 * j + c))
-
-    def wide_ag(s):
+                for e in range(2):
+                    bytes_wait(some(it, "fz", it.r0, it.nr // 2), sc.dn_r.at[it.i, e])
+
+        else:
+            count = it.nr // n_own
+            if n_own == n_z:
+                bytes_wait(some(it, "fz", it.r0, count * (n_own - 1)), sc.dn_r.at[it.i, 0])
+            else:
+
+                @pl.when(z < n_own)
+                def _():
+                    bytes_wait(some(it, "fz", it.r0, count * (n_own - 1)), sc.dn_r.at[it.i, 0])
+
+                @pl.when(z >= n_own)
+                def _():
+                    bytes_wait(some(it, "fz", it.r0, count * n_own), sc.dn_r.at[it.i, 0])
+
+        @pl.when(p != owner_of(it))
+        def _():
+            to_copy(it).start()
+
+        def place(q):
+            landing(it, q, c)[...] = some(it, "fz", it.r0, it.nr)[...]
+
+        if it.kind == "w":
+            pl.when(p == it.t)(lambda: place(it.t))
+        else:
+            for core in range(2):
+                pl.when((p == 2 * it.t + core) & (c == core))(
+                    functools.partial(place, 2 * it.t + core)
+                )
+
+    def sibling_copy(it, q):
+        view = landing(it, q, c)
+        return remote(view, view, sc.sib_s.at[it.i, q], sc.sib_r.at[it.i, q], sibling)
+
+    def step_sibling(it):
+        def go(own):
+            for q in range(4):
+                if q != own:
+                    bytes_wait(landing(it, q, 0), sc.to_r.at[it.i, q])
+                sibling_copy(it, q).start()
+
+        if it.kind == "w":
+            pl.when(p == it.t)(lambda: go(it.t))
+        else:
+            for core in range(2):
+                pl.when((p == 2 * it.t + core) & (c == core))(
+                    functools.partial(go, 2 * it.t + core)
+                )
+
+    def step_done(it):
         def go():
             for q in range(4):
-                if q != s:
-                    copy = remote(
-                        sc.fiw.at[s],
-                        sc.ow.at[q, c, z],
-                        sc.fw_s.at[s],
-                        sc.fw_r.at[0, q],
-                        (s, d),
-                    )
-                    copy.wait_recv()
-            each(n_z, 1, lambda k: wide_ag_copy(k).start())
-
-        @pl.when(p == s)
-        def _():
-            owner(z, go)
-
-    def wait_pieces(view_of, sem):
-        if n_own == n_z:
-            bytes_wait(view_of(n_own - 1), sem)
+                bytes_wait(landing(it, q, 0), sc.sib_r.at[it.i, q])
+
+        if it.kind == "w":
+            pl.when(p == it.t)(go)
         else:
-
-            @pl.when(z < n_own)
-            def _():
-                bytes_wait(view_of(n_own - 1), sem)
-
-            @pl.when(z >= n_own)
-            def _():
-                bytes_wait(view_of(n_own), sem)
-
-    def wide_pair_copy():
-        return remote(sc.ow.at[:, c], sc.ow.at[:, c], sc.bw_s.at[0], sc.bw_r.at[0], sibling)
-
-    def wide_pair(s):
-        @pl.when(p == s)
-        def _():
-            wait_pieces(lambda count: sc.ow.at[:, 0, pl.ds(0, count)], sc.aw_r.at[0])
-            wide_pair_copy().start()
-
-    def wide_done():
-        wide_pair_copy().wait_recv()
-        return [
-            put_out(
-                0,
-                sc.ow.at[...],
-                gwide_ref.at[...],
-            )
-        ]
-
-    def taps_fin_copy(layer, q):
-        return remote(
-            sc.fik.at[layer],
-            sc.ok.at[pl.ds(pl.multiple_of(kr * z, kr), kr), pl.ds(128 * q, 128)],
-            sc.fw_s.at[4 + layer],
-            sc.fw_r.at[1, q],
-            (2 * layer + c, d),
-        )
-
-    def taps_pipe(layer):
-        def go():
-            bytes_wait(sc.zrk.at[layer], sc.zw_r.at[4 + layer])
-            total = sc.zsk[layer, pl.ds(pl.multiple_of(kr * z, kr), kr)].astype(F32)
-            for k in range(n_z - 1):
-                total = total + sc.zrk[layer, k].astype(F32)
-            sc.fik[layer] = total.astype(BF16)
-            for q in range(4):
-                if q // 2 == layer:
-
-                    @pl.when((p == q) & (c == q % 2))
-                    def _(q=q):
-                        sc.ok[pl.ds(pl.multiple_of(kr * z, kr), kr), 128 * q : 128 * q + 128] = (
-                            sc.fik[layer]
-                        )
-
-                    @pl.when((p == q) & (c != q % 2))
-                    def _(q=q):
-                        taps_fin_copy(layer, q).start()
-
-                else:
-
-                    @pl.when(p == q)
-                    def _(q=q):
-                        taps_fin_copy(layer, q).start()
-
-        owner(z, go)
-
-    def taps_ag_copy(k):
-        j = lax.rem(z + k, n_z)
-        view = sc.ok.at[pl.ds(pl.multiple_of(kr * lax.rem(z, n_own), kr), kr)]
-        return remote(view, view, sc.aw_s.at[1], sc.aw_r.at[1], (p, 2 * j + c))
-
-    def taps_ag(layer):
-        for h in range(2):
-            s = 2 * layer + h
-
-            def go(s=s):
+            for core in range(2):
+                pl.when((p == 2 * it.t + core) & (c != core))(go)
+
+    def finish_grads():
+        for kind, t in [("w", s) for s in range(4)] + [("k", layer) for layer in range(2)]:
+            pair_copy(kind, t).wait_send()
+        for it in items:
+            if line:
+
+                @pl.when(inner)
+                def _(it=it):
+                    mid_copy(it).wait_send()
+                    inn_copy(it).wait_send()
+                    for e in range(2):
+                        down_copy(it, e).wait_send()
+
+                @pl.when((z == 0) | (z == 3))
+                def _(it=it):
+                    up_copy(it).wait_send()
+
+            else:
+
+                def sent(k, it=it):
+                    j, copy = scatter_copy(it, k)
+                    owner(j, lambda: copy.wait_send())
+
+                each(n_z, 1, sent)
+                owner(z, lambda: each(n_z, 1, lambda k: gather_copy(it, k).wait_send()))
+
+            @pl.when(p != owner_of(it))
+            def _(it=it):
+                to_copy(it).wait_send()
+
+            def passed(it=it):
                 for q in range(4):
-                    if q != s:
-                        taps_fin_copy(layer, q).wait_recv()
-                each(n_z, 1, lambda k: taps_ag_copy(k).start())
-
-            @pl.when((p == s) & (c == h))
-            def _(go=go):
-                owner(z, go)
-
-    def taps_pair_copy():
-        return remote(sc.ok.at[...], sc.ok.at[...], sc.bw_s.at[1], sc.bw_r.at[1], sibling)
-
-    def taps_pair(layer):
-        @pl.when((lax.div(p, 2) == layer) & (c == parity))
-        def _():
-            wait_pieces(lambda count: sc.ok.at[pl.ds(0, kr * count)], sc.aw_r.at[1])
-            taps_pair_copy().start()
-
-    def taps_done():
-        @pl.when(c != parity)
-        def _():
-            taps_pair_copy().wait_recv()
-
-        return [put_out(1, sc.ok.at[...], gtaps_ref.at[...])]
-
-    def finish_grads():
-        for wide, s in [(True, s) for s in range(4)] + [(False, layer) for layer in range(2)]:
-            (pair_w if wide else pair_k)(s).wait_send()
-
-            def sent(k, wide=wide, s=s):
-                j, copy = z_copy(wide, s, k)
-                owner(j, lambda: copy.wait_send())
-
-            each(n_z, 1, sent)
-
-        def pieces():
-            for s in range(4):
-
-                @pl.when(p != s)
-                def _(s=s):
-                    wide_fin_copy(s).wait_send()
-
-            for layer in range(2):
-
-                @pl.when(p != 2 * layer + c)
-                def _(layer=layer):
-                    taps_fin_copy(layer, 0).wait_send()
-
-            each(n_z, 1, lambda k: wide_ag_copy(k).wait_send())
-
-            @pl.when(c == parity)
-            def _():
-                each(n_z, 1, lambda k: taps_ag_copy(k).wait_send())
-
-        owner(z, pieces)
-        wide_pair_copy().wait_send()
-
-        @pl.when(c == parity)
-        def _():
-            taps_pair_copy().wait_send()
+                    sibling_copy(it, q).wait_send()
+
+            if it.kind == "w":
+                pl.when(p == it.t)(passed)
+            else:
+                pl.when(p == 2 * it.t + c)(passed)
 
     finish.append(finish_grads)
 
@@ -1069,46 +1106,59 @@
         for m in range(2):
             body(layer, m)
 
-    relay_wide(0)
-    ready_wide(0)
+    def of(kind, t, part=None):
+        chosen = [it for it in items if it.kind == kind and it.t == t]
+        return chosen
+
+    def run(step, kind, t):
+        for it in of(kind, t):
+            step(it)
+
+    wide, taps = 0, 1
+    spread_first(wide, 0)
+    spread_second(wide, 0)
+    ready(wide, 0)
     phase(first_part, 0)
     own_n.wait()
     for off in range(1, 4):
         for copy in send_norm(off):
             copy.wait_recv()
+    spread_first(taps, 0)
+    spread_first(taps, 1)
     phase(first_norm, 0)
+    spread_second(taps, 0)
+    spread_second(taps, 1)
     phase(hidden_one, 0)
-    start_wide(2)
-    start_taps(2)
-    start_taps(3)
-    start_wide(3)
-    relay_taps(0)
-    relay_taps(1)
-    ready_taps(0)
-    ready_taps(1)
+    spread_first(wide, 1)
+    spread_first(wide, 2)
+    ready(taps, 0)
+    ready(taps, 1)
     phase(second_part, 0)
-    relay_wide(1)
+    spread_second(wide, 1)
+    spread_second(wide, 2)
     phase(hidden_two, 0)
-    ready_wide(1)
+    spread_first(taps, 2)
+    spread_first(taps, 3)
+    ready(wide, 1)
     phase(third_part, 0)
-    relay_wide(2)
-    ready_wide(2)
+    spread_second(taps, 2)
+    spread_second(taps, 3)
+    ready(wide, 2)
 
     def turn(layer, m):
         pre_values(0, m)
         first_part(1, m)
 
     phase(turn, 0)
+    spread_first(wide, 3)
     phase(first_norm, 1)
-    relay_taps(2)
-    relay_taps(3)
+    spread_second(wide, 3)
     phase(hidden_one, 1)
-    ready_taps(2)
-    ready_taps(3)
+    ready(taps, 2)
+    ready(taps, 3)
     phase(second_part, 1)
-    relay_wide(3)
     phase(hidden_two, 1)
-    ready_wide(3)
+    ready(wide, 3)
     phase(third_part, 1)
     phase(pre_values, 1)
     outs = [put_out(2, sc.mix.at[...], mixed_ref.at[...])]
@@ -1116,51 +1166,73 @@
     phase(grad_out_norm, 1)
     wide_grad(3, lambda m: sc.gt[m], lambda m: ag_value(3, m))
     phase(grad_two, 1)
-    wide_z(3)
+    pair_sum("w", 3)
+    run(step_up, "w", 3)
     phase(grad_second, 1)
     taps_grad(1)
+    run(step_mid, "w", 3)
     phase(grad_one, 1)
-    wide_pipe(3)
-    taps_z(1)
+    pair_sum("k", 1)
+    run(step_up, "k", 1)
+    run(step_down, "w", 3)
     phase(grad_first, 1)
-    wide_ag(3)
+    run(step_last, "w", 3)
     phase(conv_grad, 1)
     outs.append(put_out(3, sc.gp.at[0], gpre_ref.at[...]))
     wide_grad(2, lambda m: sc.s1[m], lambda m: ag_value(5, m))
+    run(step_mid, "k", 1)
     phase(grad_out_norm, 0)
     wide_grad(1, lambda m: sc.gt[m], lambda m: ag_value(2, m))
-    wide_z(2)
+    run(step_out, "w", 3)
     phase(grad_two, 0)
-    wide_z(1)
-    taps_pipe(1)
+    pair_sum("w", 2)
+    run(step_up, "w", 2)
+    pair_sum("w", 1)
+    run(step_up, "w", 1)
+    run(step_down, "k", 1)
     phase(grad_second, 0)
     taps_grad(0)
-    wide_pipe(2)
+    run(step_mid, "w", 2)
+    run(step_last, "k", 1)
     phase(grad_one, 0)
-    taps_z(0)
-    wide_pipe(1)
-    taps_ag(1)
+    pair_sum("k", 0)
+    run(step_up, "k", 0)
+    run(step_mid, "w", 1)
+    run(step_down, "w", 2)
     phase(grad_first, 0)
+    run(step_out, "k", 1)
+    run(step_last, "w", 2)
+    run(step_down, "w", 1)
     gains_start()
-    wide_ag(2)
-    wide_ag(1)
     phase(conv_grad, 0)
     outs.append(put_out(4, sc.cv.at[...], conv_ref.at[...]))
     wide_grad(0, lambda m: x_ref[m], lambda m: ag_value(4, m))
-    taps_pipe(0)
-    wide_z(0)
+    run(step_out, "w", 2)
+    run(step_mid, "k", 0)
+    run(step_last, "w", 1)
+    pair_sum("w", 0)
+    run(step_up, "w", 0)
+    run(step_down, "k", 0)
+    run(step_out, "w", 1)
     gains_done()
-    taps_ag(0)
-    wide_pipe(0)
-    taps_pair(1)
-    wide_pair(3)
-    wide_ag(0)
-    wide_pair(2)
-    wide_pair(1)
-    taps_pair(0)
-    outs.extend(taps_done())
-    wide_pair(0)
-    outs.extend(wide_done())
+    run(step_sibling, "w", 3)
+    run(step_sibling, "k", 1)
+    run(step_last, "k", 0)
+    run(step_mid, "w", 0)
+    run(step_sibling, "w", 2)
+    run(step_out, "k", 0)
+    run(step_down, "w", 0)
+    run(step_sibling, "w", 1)
+    run(step_last, "w", 0)
+    run(step_sibling, "k", 0)
+    run(step_out, "w", 0)
+    run(step_done, "k", 1)
+    run(step_done, "k", 0)
+    outs.append(put_out(1, sc.ok.at[...], gtaps_ref.at[...]))
+    run(step_sibling, "w", 0)
+    for s in (3, 2, 1, 0):
+        run(step_done, "w", s)
+    outs.append(put_out(0, sc.ow.at[...], gwide_ref.at[...]))
     for copy in outs:
         copy.wait()
     for body in finish:
@@ -1170,7 +1242,6 @@
 def local(block_input, cotangent, weight_wide, weight_taps, norm_mid, norm_out, group_counts):
     n_dp = group_counts.shape[1]
     micro, rows, width = block_input.shape
-    n_z, n_own, wr, kr = sizes(n_dp, rows)
     scratch = scratch_list(n_dp, rows)
     vmem = pl.BlockSpec(memory_space=pltpu.VMEM)
     smem = pl.BlockSpec(memory_space=pltpu.SMEM)
@@ -1186,7 +1257,7 @@
             shape(stream, BF16),
             shape(stream, BF16),
             shape(stream, BF16),
-            shape((4, 2, n_own, wr, 512), BF16),
+            shape((4, 2, 256, 512), BF16),
             shape((2304, 512), BF16),
             shape(norm_mid.shape, F32),
             shape(norm_out.shape, F32),
@@ -1198,7 +1269,7 @@
             collective_id=0, has_side_effects=True, vmem_limit_bytes=62 * 2**20
         ),
         name="layers",
-    )(block_input, cotangent, weight_wide, weight_taps, norm_mid, norm_out, group_counts)
+    )(block_input, cotangent, weight_wide, weight_taps.reshape(9, 256, 512), norm_mid, norm_out, group_counts)
     grad_input = gpre.astype(F32) + conv.astype(F32)
     return (
         mixed,

time: 318 us -> 242 us (0.76)
  Pallas kernels: 303 us -> 229 us
    pallas_call x1, Pallas kernels: 303 us -> 229 us  [local(): pl.pallas_call(functools.partial(kernel, list(scratch), n_dp), out_shape=...]
where the time goes in v2:
time: 242 us; the launch traced here: 241 us
  Pallas kernels  229 us (95%)
  other arithmetic  8.36 us (3%)
  local copies, waits for them, and re-layouts  3.45 us (1%)
    pallas_call x1, Pallas kernels, local(): pl.pallas_call(functools.partial(kernel, list(scratch), n_dp), out_shape=...  229 us

profile of v2, /device:TPU:0, one launch (start us, length us, event | category | flops | bytes accessed | tf_op | source)
XLA Modules:
  0.0 241.5 jit_solution(4741037856364996444)
XLA Ops:
  0.6 1.4 copy.13.refs_6_
  2.0 229.0 %layers.1 = (bf16[2,384,512]{2,1,0:T(8,128)(2,1)}, bf16[2,384,512]{2,1,0:T(8,128)(2,1)}, bf16[2,384,512]{2,1,0:T(8,128)(2,1)}, bf16[4,2,256,512]{3,2,1,0:T(8,128...) custom-call(bf16[2,384,512]{2,1,0:T(8,128)(2,1)} %refs_0_.1, ...), custom_call_target="tpu_custom_call" | custom-call | tf_op jit(solution)/shard_map/layers/pallas_call | solution.py:1254
  231.0 0.0 copy-start
  231.0 2.9 %convert_add_fusion = f32[2,384,512]{2,1,0:T(8,128)} fusion(bf16[2,384,512]{2,1,0:T(8,128)(2,1)} %get-tuple-element.15, bf16[2,384,512]{2,1,0:T(8,128)(2,1)} %get-tuple-element.14), kind=kLoop, calls=%fused_computation.1 | loop fusion | flops 1179648 | bytes 3145728 | tf_op jit(solution)/shard_map/add | solution.py:1273
  233.9 0.0 copy-done
  233.9 0.0 copy-start.1
  233.9 2.9 %bitcast_convert_fusion = f32[1,2304,512]{2,1,0:T(8,128)} fusion(bf16[2304,512]{1,0:T(8,128)(2,1)S(1)} %copy-done), kind=kLoop, calls=%fused_computation | loop fusion | flops 1179648 | bytes 7077888 | tf_op jit(solution)/shard_map/reshape | solution.py:1278
  236.8 0.0 copy-done.1
  236.8 0.0 copy-start.2
  236.8 0.0 copy-start.4
  236.8 0.0 copy-start.3
  236.8 2.6 %convert.2 = f32[1,2048,512]{2,1,0:T(8,128)} convert(bf16[1,2048,512]{2,1,0:T(8,128)(2,1)S(1)} %bitcast.7) | non-fusion elementwise | flops 1048576 | bytes 6291456 | tf_op jit(solution)/shard_map/reshape | solution.py:1277
  239.4 0.0 copy-done.2
  239.4 0.9 copy.17
  240.3 0.0 copy-done.4
  240.3 0.6 copy.18
  240.9 0.0 copy-done.3
  240.9 0.6 copy.19
Async XLA Ops:
  231.0 2.9 %copy-start = (bf16[2304,512]{1,0:T(8,128)(2,1)S(1)}, bf16[2304,512]{1,0:T(8,128)(2,1)}, u32[]{:S(2)}) copy-start(bf16[2304,512]{1,0:T(8,128)(2,1)} %get-tuple-element.17) | copy-start | bytes 7077892
  233.9 2.9 %copy-start.1 = (bf16[4,2,256,512]{3,2,1,0:T(8,128)(2,1)S(1)}, bf16[4,2,256,512]{3,2,1,0:T(8,128)(2,1)}, u32[]{:S(2)}) copy-start(bf16[4,2,256,512]{3,2,1,0:T(8,128)(2,1)} %get-tuple-element.16) | copy-start | bytes 6291460
  236.8 2.6 %copy-start.2 = (bf16[2,384,512]{2,1,0:T(8,128)(2,1)S(1)}, bf16[2,384,512]{2,1,0:T(8,128)(2,1)}, u32[]{:S(2)}) copy-start(bf16[2,384,512]{2,1,0:T(8,128)(2,1)} %get-tuple-element.26) | copy-start | bytes 2359300
  236.8 3.5 %copy-start.4 = (f32[1,2,512]{2,1,0:T(2,128)S(1)}, f32[1,2,512]{2,1,0:T(2,128)}, u32[]{:S(2)}) copy-start(f32[1,2,512]{2,1,0:T(2,128)} %get-tuple-element.30) | copy-start | bytes 12292
  236.8 4.1 %copy-start.3 = (f32[1,2,1024]{2,1,0:T(2,128)S(1)}, f32[1,2,1024]{2,1,0:T(2,128)}, u32[]{:S(2)}) copy-start(f32[1,2,1024]{2,1,0:T(2,128)} %get-tuple-element.31) | copy-start | bytes 24580

commit v3 on v2

--- a/solution.py
+++ b/solution.py
@@ -42,25 +42,22 @@
 def gradient_items(n_dp):
     line = n_dp // 2 == 4
     listed = []
-    for kind, index, chunks in (
-        ("w", 3, 1),
-        ("k", 1, 2 if line else 1),
-        ("w", 2, 1),
-        ("w", 1, 1),
-        ("k", 0, 4 if line else 1),
-        ("w", 0, 2 if line else 1),
+    for kind, index, parts in (
+        ("w", 3, [256]),
+        ("k", 1, [576] * 4),
+        ("w", 2, [256]),
+        ("w", 1, [256]),
+        ("k", 0, [288, 576, 576, 576, 288]),
+        ("w", 0, [64] * 4),
     ):
-        total = 256 if kind == "w" else 2304
-        for part in range(chunks):
+        start = 0
+        for part, rows in enumerate(parts if line else [sum(parts)]):
             listed.append(
                 SimpleNamespace(
-                    kind=kind,
-                    t=index,
-                    r0=total // chunks * part,
-                    nr=total // chunks,
-                    i=len(listed),
+                    kind=kind, t=index, r0=start, nr=rows, i=len(listed), part=part
                 )
             )
+            start += rows
     return listed
 
 
@@ -119,47 +116,40 @@
         gsm=full(4, 4, 2, 128),
         gsw=full(2, 4, 2, 512),
         cnt=pltpu.SMEM((2, n_dp), F32),
-        f_s=dma((2, 3)),
+        counts=pltpu.SMEM((2, 4, n_dp), jnp.int32),
+        f_s=dma((2,)),
         f_r=dma((2, 4)),
-        z_s=dma((2, 4)),
         z_r=dma((2, 4)),
-        b_s=dma((2, 4, 2)),
-        b_r=dma((2, 4, 2)),
-        n_s=dma((3, 3)),
-        n_r=dma((3, 3)),
-        loc=dma((8,)),
-        rs_s=dma((6, 2, 3)),
-        rs_r=dma((6, 2, 3)),
-        ag_s=dma((6, 2, 3)),
-        ag_r=dma((6, 2, 3)),
-        stm_s=dma((8, 2)),
-        stm_r=dma((8, 2)),
-        stw_s=dma((4, 2)),
-        stw_r=dma((4, 2)),
+        b_s=dma((2, 4)),
+        b_r=dma((2, 4)),
+        n_s=dma((2,)),
+        n_r=dma((2,)),
+        loc=dma((4,)),
+        ex_s=dma((2, 2)),
+        ex_r=dma((2, 2)),
+        st_s=dma((2, 2)),
+        st_r=dma((2, 2)),
         pw_s=dma((6,)),
         pw_r=dma((6,)),
-        up_s=dma((items,)),
-        up_r=dma((items,)),
-        mid_s=dma((items,)),
+        it_s=dma((items,)),
+        one_r=dma((items,)),
         mid_r=dma((items,)),
-        inn_s=dma((items,)),
         inn_r=dma((items,)),
-        dn_s=dma((items, 2)),
-        dn_r=dma((items, 2)),
         to_s=dma((items,)),
-        to_r=dma((items, 4)),
-        sib_s=dma((items, 4)),
-        sib_r=dma((items, 4)),
-        g_s=dma((3, 2)),
-        g_r=dma((3, 2)),
-        out=dma((8,)),
+        to_r=dma((2, 5)),
+        sib_s=dma((2, 5)),
+        sib_r=dma((2, 5)),
+        g_s=dma((2,)),
+        g_r=dma((2,)),
+        out=dma((7,)),
     )
 
 
 def kernel(names, n, *refs):
-    (x_ref, cot_ref, wide_ref, taps_ref, nmid_ref, nout_ref, counts_ref) = refs[:7]
+    (x_ref, cot_ref, wide_ref, taps_ref, nmid_ref, nout_ref, counts_hbm) = refs[:7]
     (mixed_ref, gpre_ref, conv_ref, gwide_ref, gtaps_ref, gmid_ref, gout_ref) = refs[7:14]
     sc = SimpleNamespace(**dict(zip(names, refs[14:])))
+    counts_ref = sc.counts
     rows = x_ref.shape[1]
     n_z, n_own = sizes(n)
     p = lax.axis_index("pipe")
@@ -175,7 +165,7 @@
     finish = []
 
     def pipe_at(off):
-        return lax.rem(p + off, N_PIPE)
+        return lax.rem(p + N_PIPE + (2 * parity - 1) * off, N_PIPE)
 
     def remote(src, dst, ss, rs, dev):
         return pltpu.make_async_remote_copy(
@@ -219,21 +209,25 @@
         sc.k2.at[lax.div(p, 2), pl.ds(9 * parity, 9)],
         sc.loc.at[1],
     )
+    own_c = pltpu.make_async_copy(counts_hbm, counts_ref, sc.loc.at[2])
+    own_c.start()
     own_w.start()
     own_k.start()
     own_n = pltpu.make_async_copy(
-        nmid_ref.at[0, :, columns_of(p)], sc.gm.at[p], sc.loc.at[6]
+        nmid_ref.at[0, :, columns_of(p)], sc.gm.at[p], sc.loc.at[3]
     )
     own_n.start()
     for e in range(2):
         sc.go[p, e] = nout_ref[0, :, 512 * e : 512 * e + 512]
 
+    own_c.wait()
+
     def used_rows(m, j):
         return (
-            49 * counts_ref[m, j, 0]
-            + 36 * counts_ref[m, j, 1]
-            + 25 * counts_ref[m, j, 2]
-            + 4 * counts_ref[m, j, 3]
+            49 * counts_ref[m, 0, j]
+            + 36 * counts_ref[m, 1, j]
+            + 25 * counts_ref[m, 2, j]
+            + 4 * counts_ref[m, 3, j]
         )
 
     totals = []
@@ -263,7 +257,7 @@
         else:
             src = taps_ref.at[:, pl.ds(pl.multiple_of(64 * quarter, 64), 64), columns_of(q)]
         return remote(
-            src, held(kind, p, quarter), sc.f_s.at[kind, off - 1], sc.f_r.at[kind, p], (q, d)
+            src, held(kind, p, quarter), sc.f_s.at[kind], sc.f_r.at[kind, p], (q, d)
         )
 
     def send_norm(off):
@@ -272,8 +266,8 @@
             remote(
                 nmid_ref.at[0, :, columns_of(q)],
                 sc.gm.at[p],
-                sc.n_s.at[off - 1, 0],
-                sc.n_r.at[off - 1, 0],
+                sc.n_s.at[0],
+                sc.n_r.at[0],
                 (q, d),
             )
         ]
@@ -282,20 +276,24 @@
                 remote(
                     nout_ref.at[0, :, pl.ds(512 * e, 512)],
                     sc.go.at[p, e],
-                    sc.n_s.at[off - 1, 1 + e],
-                    sc.n_r.at[off - 1, 1 + e],
+                    sc.n_s.at[1],
+                    sc.n_r.at[1],
                     (q, d),
                 )
             )
         return listed
 
+    def norm_wait(sems):
+        bytes_wait(sc.gm.at[pl.ds(0, 3)], sems.at[0])
+        bytes_wait(sc.go.at[pl.ds(0, 3)], sems.at[1])
+
     def pass_z(kind, s):
         view = held(kind, s, quarter)
-        return remote(view, view, sc.z_s.at[kind, s], sc.z_r.at[kind, s], z_pair)
+        return remote(view, view, sc.b_s.at[kind, s], sc.z_r.at[kind, s], z_pair)
 
     def pass_sibling(kind, s, e):
         view = held(kind, s, quarter if e == 0 else quarter_z)
-        return remote(view, view, sc.b_s.at[kind, s, e], sc.b_r.at[kind, s, e], sibling)
+        return remote(view, view, sc.b_s.at[kind, s], sc.b_r.at[kind, s], sibling)
 
     def spread_first(kind, s):
         @pl.when(p != s)
@@ -311,11 +309,15 @@
             pass_z(kind, s).wait_recv()
             pass_sibling(kind, s, 1).start()
 
+    def quarters(kind, s, count):
+        if kind == 0:
+            return sc.wt.at[s, pl.ds(0, 128 * count)]
+        return sc.k2.at[s // 2, pl.ds(9 * (s % 2), 9), pl.ds(0, 64 * count)]
+
     def ready(kind, s):
         @pl.when(p != s)
         def _():
-            for e in range(2):
-                pass_sibling(kind, s, e).wait_recv()
+            bytes_wait(quarters(kind, s, 2), sc.b_r.at[kind, s])
 
         @pl.when(p == s)
         def _():
@@ -323,15 +325,12 @@
 
     def finish_weights():
         for kind in range(2):
-            for off in range(1, 4):
-                fetch(kind, off).wait_send()
+            bytes_wait(quarters(kind, 0, 3), sc.f_s.at[kind])
             for s in range(4):
 
                 @pl.when(p != s)
                 def _(kind=kind, s=s):
-                    pass_z(kind, s).wait_send()
-                    for e in range(2):
-                        pass_sibling(kind, s, e).wait_send()
+                    bytes_wait(quarters(kind, s, 3), sc.b_s.at[kind, s])
 
     finish.append(finish_weights)
 
@@ -348,9 +347,7 @@
                             copy.start()
 
     def finish_norm():
-        for off in range(1, 4):
-            for copy in send_norm(off):
-                copy.wait_send()
+        norm_wait(sc.n_s)
 
     finish.append(finish_norm)
 
@@ -361,7 +358,7 @@
         ends = []
         total = jnp.int32(0)
         for g, area in enumerate((49, 36, 25, 4)):
-            total = total + area * counts_ref[m, d, g]
+            total = total + area * counts_ref[m, g, d]
             ends.append(total.astype(F32))
         sc.msk[m] = jnp.where(row_id < ends[3], 1.0, 0.0)
 
@@ -401,90 +398,82 @@
         build(m)
 
 
-    def rs_copies(rid, m, par):
-        listed = []
-        for off in range(1, 4):
-            q = pipe_at(off)
-            listed.append(
-                remote(
-                    sc.part.at[par, m, q],
-                    sc.rsr.at[rid, m, off - 1],
-                    sc.rs_s.at[rid, m, off - 1],
-                    sc.rs_r.at[rid, m, off - 1],
-                    (q, d),
-                )
-            )
-        return listed
-
-    def rs_start(rid, m, par):
-        for copy in rs_copies(rid, m, par):
-            copy.start()
+    exchange_order = [
+        ("rs", 0), ("ag", 0), ("ag", 2), ("rs", 1), ("ag", 1), ("ag", 3),
+        ("rs", 3), ("rs", 5), ("ag", 5), ("rs", 2), ("rs", 4), ("ag", 4),
+    ]
+
+    def three(kind, i, m):
+        return sc.rsr.at[i, m] if kind == "rs" else sc.ag.at[i, m, pl.ds(0, 3)]
+
+    def exchange_wait(sems, kind, i, m):
+        turn = exchange_order.index((kind, i))
+        bytes_wait(three(kind, i, m), sems.at[turn % 2, m])
+
+    def exchange_open(kind, i, m):
+        turn = exchange_order.index((kind, i))
+        if turn >= 2:
+            exchange_wait(sc.ex_s, *exchange_order[turn - 2], m)
+        return sc.ex_s.at[turn % 2, m], sc.ex_r.at[turn % 2, m]
 
     def rs_sum(rid, m, par):
-        for copy in rs_copies(rid, m, par):
-            copy.wait_recv()
+        exchange_wait(sc.ex_r, "rs", rid, m)
         total = sc.part[par, m, p].astype(F32)
         for k in range(3):
             total = total + sc.rsr[rid, m, k].astype(F32)
         return total
 
-    def ag_copies(aid, m):
-        listed = []
+    def ag_start(aid, m, value):
+        ss, rs = exchange_open("ag", aid, m)
+        sc.ag[aid, m, p] = value
+        own = sc.ag.at[aid, m, p]
         for off in range(1, 4):
-            listed.append(
-                remote(
-                    sc.ag.at[aid, m, p],
-                    sc.ag.at[aid, m, p],
-                    sc.ag_s.at[aid, m, off - 1],
-                    sc.ag_r.at[aid, m, off - 1],
-                    (pipe_at(off), d),
-                )
-            )
-        return listed
-
-    def ag_start(aid, m, value):
-        sc.ag[aid, m, p] = value
-        for copy in ag_copies(aid, m):
-            copy.start()
+            remote(own, own, ss, rs, (pipe_at(off), d)).start()
 
     def ag_wait(aid, m):
-        for copy in ag_copies(aid, m):
-            copy.wait_recv()
+        exchange_wait(sc.ex_r, "ag", aid, m)
 
     def ag_value(aid, m):
         return jnp.concatenate([sc.ag[aid, m, q] for q in range(4)], axis=1)
 
-    def finish_ag():
-        for aid in range(6):
+    def finish_exchanges():
+        for kind, i in exchange_order[-2:]:
             for m in range(2):
-                for copy in ag_copies(aid, m):
-                    copy.wait_send()
-
-    finish.append(finish_ag)
-
-    def st_refs(wide, i, m):
-        if wide:
-            return sc.stw.at[i, m], sc.stw_s.at[i, m], sc.stw_r.at[i, m]
-        return sc.stm.at[i, m], sc.stm_s.at[i, m], sc.stm_r.at[i, m]
+                exchange_wait(sc.ex_s, kind, i, m)
+
+    finish.append(finish_exchanges)
+
+    sum_order = [
+        (False, 0), (False, 1), (True, 0), (False, 2), (False, 3), (True, 1),
+        (True, 3), (False, 7), (False, 6), (True, 2), (False, 5), (False, 4),
+    ]
+
+    def st_buffer(wide, i, m):
+        return (sc.stw if wide else sc.stm).at[i, m]
+
+    def st_bytes(sems, wide, i, m):
+        turn = sum_order.index((wide, i))
+        bytes_wait(st_buffer(wide, i, m).at[pl.ds(0, n - 1)], sems.at[turn % 2, m])
 
     def st_start(wide, i, m):
-        buf, ss, rs = st_refs(wide, i, m)
+        turn = sum_order.index((wide, i))
+        if turn >= 2:
+            st_bytes(sc.st_s, *sum_order[turn - 2], m)
+        own = st_buffer(wide, i, m).at[d]
+        ss, rs = sc.st_s.at[turn % 2, m], sc.st_r.at[turn % 2, m]
 
         def go(k):
-            remote(buf.at[d], buf.at[d], ss, rs, (p, lax.rem(d + k, n))).start()
+            remote(own, own, ss, rs, (p, lax.rem(d + k, n))).start()
 
         each(n, 1, go)
 
     def st_wait(wide, i, m):
-        buf, ss, rs = st_refs(wide, i, m)
-        bytes_wait(buf.at[pl.ds(0, n - 1)], rs)
+        st_bytes(sc.st_r, wide, i, m)
 
     def finish_st():
-        for wide, count in ((True, 4), (False, 8)):
-            for i in range(count):
-                for m in range(2):
-                    buf, ss, rs = st_refs(wide, i, m)
-                    bytes_wait(buf.at[pl.ds(0, n - 1)], ss)
+        for wide, i in sum_order[-2:]:
+            for m in range(2):
+                st_bytes(sc.st_s, wide, i, m)
 
     finish.append(finish_st)
 
@@ -540,26 +529,17 @@
         return (x_ref[m, :, lanes(j)] if layer == 0 else sc.s1[m, :, lanes(j)]).astype(F32)
 
     rs_par = {0: 0, 1: 1, 3: 0, 5: 1, 2: 0, 4: 1}
-    rs_before = {0: None, 1: None, 3: 0, 5: 1, 2: 3, 4: 5}
 
     def rs_send(rid, m, values):
         par = rs_par[rid]
-        if rs_before[rid] is not None:
-            for copy in rs_copies(rs_before[rid], m, par):
-                copy.wait_send()
+        ss, rs = exchange_open("rs", rid, m)
         for j, value in enumerate(values):
             half = value.astype(BF16)
             sc.part[par, m, 2 * j] = half[:, :LANES]
             sc.part[par, m, 2 * j + 1] = half[:, LANES:]
-        rs_start(rid, m, par)
-
-    def finish_rs():
-        for rid in (2, 4):
-            for m in range(2):
-                for copy in rs_copies(rid, m, rs_par[rid]):
-                    copy.wait_send()
-
-    finish.append(finish_rs)
+        for off in range(1, 4):
+            q = pipe_at(off)
+            remote(sc.part.at[par, m, q], sc.rsr.at[rid, m, off - 1], ss, rs, (q, d)).start()
 
     def first_part(layer, m):
         s = stream(layer, m)
@@ -825,8 +805,8 @@
         return remote(
             tile(it, "zs").at[it.t, rows_of],
             tile(it, "zo").at[it.t, rows_of],
-            sc.up_s.at[it.i],
-            sc.up_r.at[it.i],
+            sc.it_s.at[it.i],
+            sc.one_r.at[it.i],
             (p, 2 * (1 + lax.div(z, 3)) + c),
         )
 
@@ -834,7 +814,7 @@
         return remote(
             tile(it, "zs").at[it.t, part_rows(it, 2 - z)],
             tile(it, "zi").at[it.t, pl.ds(it.r0 // 2, it.nr // 2)],
-            sc.mid_s.at[it.i],
+            sc.it_s.at[it.i],
             sc.mid_r.at[it.i],
             (p, 2 * (3 - z) + c),
         )
@@ -842,13 +822,13 @@
     def inn_copy(it):
         view = tile(it, "fz").at[it.t, part_rows(it, z - 1)]
         return remote(
-            view, view, sc.inn_s.at[it.i], sc.inn_r.at[it.i], (p, 2 * (3 - z) + c)
+            view, view, sc.it_s.at[it.i], sc.inn_r.at[it.i], (p, 2 * (3 - z) + c)
         )
 
     def down_copy(it, e):
         view = tile(it, "fz").at[it.t, part_rows(it, z - 1 if e == 0 else 2 - z)]
         return remote(
-            view, view, sc.dn_s.at[it.i, e], sc.dn_r.at[it.i, e], (p, 2 * (3 * (z - 1)) + c)
+            view, view, sc.it_s.at[it.i], sc.one_r.at[it.i], (p, 2 * (3 * (z - 1)) + c)
         )
 
     def direct_rows(it, j):
@@ -866,15 +846,15 @@
         return j, remote(
             tile(it, "zs").at[it.t, direct_rows(it, lax.rem(j, n_own))],
             tile(it, "zo").at[it.t, k - 1],
-            sc.up_s.at[it.i],
-            sc.up_r.at[it.i],
+            sc.it_s.at[it.i],
+            sc.one_r.at[it.i],
             (p, 2 * j + c),
         )
 
     def gather_copy(it, k):
         j = lax.rem(z + k, n_z)
         view = tile(it, "fz").at[it.t, direct_rows(it, lax.rem(z, n_own))]
-        return remote(view, view, sc.dn_s.at[it.i, 0], sc.dn_r.at[it.i, 0], (p, 2 * j + c))
+        return remote(view, view, sc.to_s.at[it.i], sc.mid_r.at[it.i], (p, 2 * j + c))
 
     def add_rows(target, first, second):
         target[...] = (first[...].astype(F32) + second[...].astype(F32)).astype(BF16)
@@ -923,7 +903,7 @@
             return
 
         def go():
-            bytes_wait(tile(it, "zo").at[it.t], sc.up_r.at[it.i])
+            bytes_wait(tile(it, "zo").at[it.t], sc.one_r.at[it.i])
             mine = direct_rows(it, z)
             total = tile(it, "zs")[it.t, mine].astype(F32)
             total = lax.fori_loop(
@@ -952,12 +932,15 @@
         lane = pl.ds(128 * q, 128) if isinstance(q, int) else columns_of(q)
         return sc.ok.at[pl.ds(it.r0, it.nr), lane]
 
+    def to_sem(it, sems):
+        return sems.at[0 if it.kind == "w" else 1, it.part]
+
     def to_copy(it):
         return remote(
             some(it, "fz", it.r0, it.nr),
             landing(it, p, c),
             sc.to_s.at[it.i],
-            sc.to_r.at[it.i, p],
+            to_sem(it, sc.to_r),
             (owner_of(it), d),
         )
 
@@ -966,22 +949,21 @@
 
             @pl.when((z == 0) | (z == 3))
             def _():
-                for e in range(2):
-                    bytes_wait(some(it, "fz", it.r0, it.nr // 2), sc.dn_r.at[it.i, e])
+                bytes_wait(some(it, "fz", it.r0, it.nr), sc.one_r.at[it.i])
 
         else:
             count = it.nr // n_own
             if n_own == n_z:
-                bytes_wait(some(it, "fz", it.r0, count * (n_own - 1)), sc.dn_r.at[it.i, 0])
+                bytes_wait(some(it, "fz", it.r0, count * (n_own - 1)), sc.mid_r.at[it.i])
             else:
 
                 @pl.when(z < n_own)
                 def _():
-                    bytes_wait(some(it, "fz", it.r0, count * (n_own - 1)), sc.dn_r.at[it.i, 0])
+                    bytes_wait(some(it, "fz", it.r0, count * (n_own - 1)), sc.mid_r.at[it.i])
 
                 @pl.when(z >= n_own)
                 def _():
-                    bytes_wait(some(it, "fz", it.r0, count * n_own), sc.dn_r.at[it.i, 0])
+                    bytes_wait(some(it, "fz", it.r0, count * n_own), sc.mid_r.at[it.i])
 
         @pl.when(p != owner_of(it))
         def _():
@@ -1000,33 +982,33 @@
 
     def sibling_copy(it, q):
         view = landing(it, q, c)
-        return remote(view, view, sc.sib_s.at[it.i, q], sc.sib_r.at[it.i, q], sibling)
+        return remote(
+            view, view, to_sem(it, sc.sib_s), to_sem(it, sc.sib_r), sibling
+        )
+
+    def slices(it, count):
+        if it.kind == "w":
+            return sc.ow.at[pl.ds(0, count), 0, pl.ds(it.r0, it.nr)]
+        return sc.ok.at[pl.ds(it.r0, it.nr), pl.ds(0, 128 * count)]
 
     def step_sibling(it):
-        def go(own):
+        def go():
+            bytes_wait(slices(it, 3), to_sem(it, sc.to_r))
             for q in range(4):
-                if q != own:
-                    bytes_wait(landing(it, q, 0), sc.to_r.at[it.i, q])
                 sibling_copy(it, q).start()
 
-        if it.kind == "w":
-            pl.when(p == it.t)(lambda: go(it.t))
-        else:
-            for core in range(2):
-                pl.when((p == 2 * it.t + core) & (c == core))(
-                    functools.partial(go, 2 * it.t + core)
-                )
+        pl.when(p == owner_of(it))(go)
 
     def step_done(it):
         def go():
-            for q in range(4):
-                bytes_wait(landing(it, q, 0), sc.sib_r.at[it.i, q])
-
+            bytes_wait(slices(it, 4), to_sem(it, sc.sib_r))
+
+        pl.when(p == (it.t if it.kind == "w" else 2 * it.t + 1 - c))(go)
+
+    def twice(it):
         if it.kind == "w":
-            pl.when(p == it.t)(go)
-        else:
-            for core in range(2):
-                pl.when((p == 2 * it.t + core) & (c != core))(go)
+            return sc.dw.at[it.t, :, pl.ds(0, it.nr)]
+        return sc.dk.at[it.t, pl.ds(0, 2 * it.nr)]
 
     def finish_grads():
         for kind, t in [("w", s) for s in range(4)] + [("k", layer) for layer in range(2)]:
@@ -1036,10 +1018,7 @@
 
                 @pl.when(inner)
                 def _(it=it):
-                    mid_copy(it).wait_send()
-                    inn_copy(it).wait_send()
-                    for e in range(2):
-                        down_copy(it, e).wait_send()
+                    bytes_wait(twice(it), sc.it_s.at[it.i])
 
                 @pl.when((z == 0) | (z == 3))
                 def _(it=it):
@@ -1058,27 +1037,22 @@
             def _(it=it):
                 to_copy(it).wait_send()
 
-            def passed(it=it):
-                for q in range(4):
-                    sibling_copy(it, q).wait_send()
-
-            if it.kind == "w":
-                pl.when(p == it.t)(passed)
-            else:
-                pl.when(p == 2 * it.t + c)(passed)
+            @pl.when(p == owner_of(it))
+            def _(it=it):
+                bytes_wait(slices(it, 4), to_sem(it, sc.sib_s))
 
     finish.append(finish_grads)
 
     def gain_copies(off):
         dev = (pipe_at(off), d)
         return [
-            remote(
-                sc.gsm.at[:, p], sc.gsm.at[:, p], sc.g_s.at[off - 1, 0], sc.g_r.at[off - 1, 0], dev
-            ),
-            remote(
-                sc.gsw.at[:, p], sc.gsw.at[:, p], sc.g_s.at[off - 1, 1], sc.g_r.at[off - 1, 1], dev
-            ),
+            remote(sc.gsm.at[:, p], sc.gsm.at[:, p], sc.g_s.at[0], sc.g_r.at[0], dev),
+            remote(sc.gsw.at[:, p], sc.gsw.at[:, p], sc.g_s.at[1], sc.g_r.at[1], dev),
         ]
+
+    def gains_wait(sems):
+        bytes_wait(sc.gsm.at[:, pl.ds(0, 3)], sems.at[0])
+        bytes_wait(sc.gsw.at[:, pl.ds(0, 3)], sems.at[1])
 
     def gains_start():
         for off in range(1, 4):
@@ -1086,9 +1060,7 @@
                 copy.start()
 
     def gains_done():
-        for off in range(1, 4):
-            for copy in gain_copies(off):
-                copy.wait_recv()
+        gains_wait(sc.g_r)
         for q in range(4):
             gmid_ref[0, :, lanes(q)] = sc.gsm[p, q]
         layer = lax.div(p, 2)
@@ -1096,19 +1068,22 @@
             gout_ref[0, :, 512 * e : 512 * e + 512] = sc.gsw[layer, 2 * parity + e]
 
     def finish_gains():
-        for off in range(1, 4):
-            for copy in gain_copies(off):
-                copy.wait_send()
+        gains_wait(sc.g_s)
 
     finish.append(finish_gains)
 
-    def phase(body, layer):
-        for m in range(2):
-            body(layer, m)
-
-    def of(kind, t, part=None):
-        chosen = [it for it in items if it.kind == kind and it.t == t]
-        return chosen
+    def phase(body, layer, between=None):
+        body(layer, 0)
+        if between is not None:
+            between()
+        body(layer, 1)
+
+    def of(kind, t):
+        return [it for it in items if it.kind == kind and it.t == t]
+
+    def one(step, kind, t, part):
+        for it in of(kind, t)[part : part + 1]:
+            step(it)
 
     def run(step, kind, t):
         for it in of(kind, t):
@@ -1120,9 +1095,7 @@
     ready(wide, 0)
     phase(first_part, 0)
     own_n.wait()
-    for off in range(1, 4):
-        for copy in send_norm(off):
-            copy.wait_recv()
+    norm_wait(sc.n_r)
     spread_first(taps, 0)
     spread_first(taps, 1)
     phase(first_norm, 0)
@@ -1170,73 +1143,233 @@
     run(step_up, "w", 3)
     phase(grad_second, 1)
     taps_grad(1)
-    run(step_mid, "w", 3)
-    phase(grad_one, 1)
+    phase(grad_one, 1, lambda: run(step_mid, "w", 3))
     pair_sum("k", 1)
     run(step_up, "k", 1)
     run(step_down, "w", 3)
     phase(grad_first, 1)
     run(step_last, "w", 3)
-    phase(conv_grad, 1)
+    one(step_mid, "k", 1, 0)
+    phase(conv_grad, 1, lambda: one(step_mid, "k", 1, 1))
     outs.append(put_out(3, sc.gp.at[0], gpre_ref.at[...]))
     wide_grad(2, lambda m: sc.s1[m], lambda m: ag_value(5, m))
-    run(step_mid, "k", 1)
-    phase(grad_out_norm, 0)
+    one(step_mid, "k", 1, 2)
+    one(step_down, "k", 1, 0)
+    one(step_down, "k", 1, 1)
+
+    def early_zero():
+        one(step_mid, "k", 1, 3)
+        one(step_down, "k", 1, 2)
+        pair_sum("w", 2)
+        run(step_up, "w", 2)
+
+    phase(grad_out_norm, 0, early_zero)
     wide_grad(1, lambda m: sc.gt[m], lambda m: ag_value(2, m))
-    run(step_out, "w", 3)
-    phase(grad_two, 0)
-    pair_sum("w", 2)
-    run(step_up, "w", 2)
+    one(step_last, "k", 1, 0)
+    one(step_last, "k", 1, 1)
+    def early_two():
+        one(step_down, "k", 1, 3)
+        run(step_mid, "w", 2)
+
+    phase(grad_two, 0, early_two)
     pair_sum("w", 1)
     run(step_up, "w", 1)
-    run(step_down, "k", 1)
-    phase(grad_second, 0)
+    one(step_last, "k", 1, 2)
+    one(step_last, "k", 1, 3)
+    phase(grad_second, 0, lambda: run(step_down, "w", 2))
     taps_grad(0)
-    run(step_mid, "w", 2)
-    run(step_last, "k", 1)
-    phase(grad_one, 0)
-    pair_sum("k", 0)
-    run(step_up, "k", 0)
-    run(step_mid, "w", 1)
-    run(step_down, "w", 2)
+
+    def early_one():
+        run(step_last, "w", 2)
+        run(step_mid, "w", 1)
+        pair_sum("k", 0)
+        one(step_up, "k", 0, 0)
+
+    phase(grad_one, 0, early_one)
+    for part in range(1, 5):
+        one(step_up, "k", 0, part)
+    run(step_down, "w", 1)
     phase(grad_first, 0)
+    gains_start()
+    one(step_mid, "k", 0, 0)
+    run(step_last, "w", 1)
+    one(step_mid, "k", 0, 1)
+    one(step_down, "k", 0, 0)
+    conv_grad(0, 0)
+    one(step_mid, "k", 0, 2)
+    one(step_down, "k", 0, 1)
+    one(step_last, "k", 0, 0)
     run(step_out, "k", 1)
-    run(step_last, "w", 2)
-    run(step_down, "w", 1)
-    gains_start()
-    phase(conv_grad, 0)
+    conv_grad(0, 1)
+    wide_grad(0, lambda m: x_ref[m], lambda m: ag_value(4, m))
+    one(step_mid, "k", 0, 3)
+    one(step_down, "k", 0, 2)
+    one(step_last, "k", 0, 1)
+    one(step_out, "k", 0, 0)
     outs.append(put_out(4, sc.cv.at[...], conv_ref.at[...]))
-    wide_grad(0, lambda m: x_ref[m], lambda m: ag_value(4, m))
-    run(step_out, "w", 2)
-    run(step_mid, "k", 0)
-    run(step_last, "w", 1)
+    one(step_mid, "k", 0, 4)
     pair_sum("w", 0)
     run(step_up, "w", 0)
-    run(step_down, "k", 0)
+    one(step_down, "k", 0, 3)
+    one(step_last, "k", 0, 2)
+    one(step_out, "k", 0, 1)
+    run(step_out, "w", 3)
+    one(step_down, "k", 0, 4)
+    one(step_mid, "w", 0, 0)
+    one(step_last, "k", 0, 3)
+    one(step_out, "k", 0, 2)
+    one(step_mid, "w", 0, 1)
+    one(step_last, "k", 0, 4)
+    one(step_down, "w", 0, 0)
+    one(step_mid, "w", 0, 2)
+    one(step_out, "k", 0, 3)
+    one(step_down, "w", 0, 1)
+    one(step_mid, "w", 0, 3)
+    one(step_last, "w", 0, 0)
+    one(step_out, "k", 0, 4)
+    one(step_down, "w", 0, 2)
+    one(step_last, "w", 0, 1)
+    one(step_out, "w", 0, 0)
+    run(step_out, "w", 2)
+    one(step_down, "w", 0, 3)
+    one(step_last, "w", 0, 2)
+    one(step_out, "w", 0, 1)
+    one(step_last, "w", 0, 3)
     run(step_out, "w", 1)
+    one(step_out, "w", 0, 2)
+    one(step_out, "w", 0, 3)
     gains_done()
     run(step_sibling, "w", 3)
     run(step_sibling, "k", 1)
-    run(step_last, "k", 0)
-    run(step_mid, "w", 0)
+    run(step_sibling, "k", 0)
     run(step_sibling, "w", 2)
-    run(step_out, "k", 0)
-    run(step_down, "w", 0)
     run(step_sibling, "w", 1)
-    run(step_last, "w", 0)
-    run(step_sibling, "k", 0)
-    run(step_out, "w", 0)
+    one(step_sibling, "w", 0, 0)
+    one(step_sibling, "w", 0, 1)
     run(step_done, "k", 1)
     run(step_done, "k", 0)
     outs.append(put_out(1, sc.ok.at[...], gtaps_ref.at[...]))
-    run(step_sibling, "w", 0)
-    for s in (3, 2, 1, 0):
+    for s in (3, 2, 1):
         run(step_done, "w", s)
-    outs.append(put_out(0, sc.ow.at[...], gwide_ref.at[...]))
+    last = of("w", 0)
+    for group, part in enumerate((last[:-1], last[-1:]) if len(last) > 1 else (last,)):
+        first, count = part[0].r0, sum(it.nr for it in part)
+        for it in part:
+            if it.i >= last[0].i + 2:
+                step_sibling(it)
+        for it in part:
+            step_done(it)
+        part_rows_of = pl.ds(first, count)
+        outs.append(
+            put_out(
+                5 + group, sc.ow.at[:, :, part_rows_of], gwide_ref.at[:, :, part_rows_of]
+            )
+        )
     for copy in outs:
         copy.wait()
     for body in finish:
         body()
+
+
+def cast_pieces(rows):
+    pieces = [("taps", pl.ds(576 * i, 576)) for i in range(4)]
+    pieces += [("wide", pl.ds(512 * i, 512)) for i in range(4)]
+    return pieces + [("stream", m) for m in range(2)]
+
+
+def cast_kernel(mixed, gpre, conv, gwide, gtaps, gmid, gout, *refs):
+    o_mixed, o_input, o_wide, o_taps, o_mid, o_out = refs[:6]
+    b_taps, b_wide, b_gpre, b_conv, f_taps, f_wide, f_stream = refs[6:13]
+    b_mixed, b_mid, b_out, r_sem, w_sem, d_sem = refs[13:]
+    pieces = cast_pieces(gpre.shape[1])
+    same = ((mixed, b_mixed, o_mixed), (gmid, b_mid, o_mid), (gout, b_out, o_out))
+    arrive = [pltpu.make_async_copy(a, b, d_sem.at[i]) for i, (a, b, _) in enumerate(same)]
+    leave = [pltpu.make_async_copy(b, o, d_sem.at[i]) for i, (_, b, o) in enumerate(same)]
+    reads, writes = [], []
+    for i, (kind, part) in enumerate(pieces):
+        if kind == "stream":
+            reads.append(
+                [
+                    pltpu.make_async_copy(gpre.at[part], b_gpre.at[part], r_sem.at[i]),
+                    pltpu.make_async_copy(conv.at[part], b_conv.at[part], r_sem.at[i + 2]),
+                ]
+            )
+            writes.append(
+                pltpu.make_async_copy(f_stream.at[part], o_input.at[part], w_sem.at[i])
+            )
+            continue
+        src, low, high, dst = (
+            (gtaps, b_taps, f_taps, o_taps)
+            if kind == "taps"
+            else (gwide, b_wide, f_wide, o_wide)
+        )
+        reads.append([pltpu.make_async_copy(src.at[part], low.at[part], r_sem.at[i])])
+        writes.append(pltpu.make_async_copy(high.at[part], dst.at[part], w_sem.at[i]))
+    for group in reads:
+        for copy in group:
+            copy.start()
+    for copy in arrive:
+        copy.start()
+    for (kind, part), group, write in zip(pieces, reads, writes):
+        for copy in group:
+            copy.wait()
+        size = 64
+
+        def strip(i, carry, kind=kind, part=part):
+            if kind == "stream":
+                at = pl.ds(pl.multiple_of(i * size, size), size)
+                f_stream[part, at] = b_gpre[part, at].astype(F32) + b_conv[part, at].astype(F32)
+                return carry
+            at = pl.ds(pl.multiple_of(part.start + i * size, size), size)
+            if kind == "taps":
+                f_taps[at] = b_taps[at].astype(F32)
+            else:
+                f_wide[at] = b_wide[at].astype(F32)
+            return carry
+
+        lax.fori_loop(0, (gpre.shape[1] if kind == "stream" else part.size) // size, strip, 0)
+        write.start()
+    for first, second in zip(arrive, leave):
+        first.wait()
+        second.start()
+    for copy in writes + leave:
+        copy.wait()
+
+
+def cast_all(mixed, gpre, conv, gwide, gtaps, gmid, gout):
+    anywhere = pl.BlockSpec(memory_space=pl.ANY)
+    shape = jax.ShapeDtypeStruct
+    count = len(cast_pieces(gpre.shape[1]))
+    return pl.pallas_call(
+        cast_kernel,
+        in_specs=[anywhere] * 7,
+        out_specs=[anywhere] * 6,
+        out_shape=[
+            shape(mixed.shape, BF16),
+            shape(mixed.shape, F32),
+            shape(gwide.shape, F32),
+            shape(gtaps.shape, F32),
+            shape(gmid.shape, F32),
+            shape(gout.shape, F32),
+        ],
+        scratch_shapes=[
+            pltpu.VMEM(gtaps.shape, BF16),
+            pltpu.VMEM(gwide.shape, BF16),
+            pltpu.VMEM(gpre.shape, BF16),
+            pltpu.VMEM(gpre.shape, BF16),
+            pltpu.VMEM(gtaps.shape, F32),
+            pltpu.VMEM(gwide.shape, F32),
+            pltpu.VMEM(gpre.shape, F32),
+            pltpu.VMEM(mixed.shape, BF16),
+            pltpu.VMEM(gmid.shape, F32),
+            pltpu.VMEM(gout.shape, F32),
+            pltpu.SemaphoreType.DMA((count + 2,)),
+            pltpu.SemaphoreType.DMA((count,)),
+            pltpu.SemaphoreType.DMA((3,)),
+        ],
+        compiler_params=pltpu.CompilerParams(vmem_limit_bytes=60 * 2**20),
+        name="casts",
+    )(mixed, gpre, conv, gwide, gtaps, gmid, gout)
 
 
 def local(block_input, cotangent, weight_wide, weight_taps, norm_mid, norm_out, group_counts):
@@ -1244,7 +1377,6 @@
     micro, rows, width = block_input.shape
     scratch = scratch_list(n_dp, rows)
     vmem = pl.BlockSpec(memory_space=pltpu.VMEM)
-    smem = pl.BlockSpec(memory_space=pltpu.SMEM)
     anywhere = pl.BlockSpec(memory_space=pl.ANY)
 
     def shape(dims, dtype):
@@ -1262,20 +1394,21 @@
             shape(norm_mid.shape, F32),
             shape(norm_out.shape, F32),
         ],
-        in_specs=[vmem, vmem, anywhere, anywhere, vmem, vmem, smem],
+        in_specs=[vmem, vmem, anywhere, anywhere, vmem, vmem, anywhere],
         out_specs=[anywhere] * 5 + [vmem] * 2,
         scratch_shapes=list(scratch.values()),
         compiler_params=pltpu.CompilerParams(
             collective_id=0, has_side_effects=True, vmem_limit_bytes=62 * 2**20
         ),
         name="layers",
-    )(block_input, cotangent, weight_wide, weight_taps.reshape(9, 256, 512), norm_mid, norm_out, group_counts)
-    grad_input = gpre.astype(F32) + conv.astype(F32)
+    )(block_input, cotangent, weight_wide, weight_taps.reshape(9, 256, 512), norm_mid, norm_out, jnp.swapaxes(group_counts, 1, 2))
+    results = cast_all(mixed, gpre, conv, gwide.reshape(2048, 512), gtaps, gmid, gout)
+    mixed, grad_input, gwide, gtaps, gmid, gout = results
     return (
         mixed,
         grad_input,
-        gwide.astype(F32).reshape(weight_wide.shape),
-        gtaps.astype(F32).reshape(weight_taps.shape),
+        gwide.reshape(weight_wide.shape),
+        gtaps.reshape(weight_taps.shape),
         gmid,
         gout,
     )

time: 242 us -> 212 us (0.88)
  Pallas kernels: 229 us -> 211 us
  other arithmetic: 8.36 us -> 0 us
  local copies, waits for them, and re-layouts: 3.45 us -> 0 us
    pallas_call x1, Pallas kernels: 229 us -> 205 us  [local(): pl.pallas_call(functools.partial(kernel, list(scratch), n_dp), out_shape=...]
    pallas_call x0 -> x1, Pallas kernels: none -> 6.44 us  [cast_all(): pl.pallas_call(cast_kernel, in_specs=[anywhere] * 7, out_specs=[anywhere]...]
    reshape x2 -> x0, other arithmetic: 5.45 us -> none  [the longest x1 2.85 us: local(): gtaps.astype(F32).reshape(weight_taps.shape)]
    unnamed x14 -> x0, local copies, waits for them, and re-layouts: 3.45 us -> none
    add x1 -> x0, other arithmetic: 2.91 us -> none  [local(): grad_input = gpre.astype(F32) + conv.astype(F32)]
where the time goes in v3:
time: 212 us
  Pallas kernels  211 us (100%)
    pallas_call x1, Pallas kernels, local(): pl.pallas_call(functools.partial(kernel, list(scratch), n_dp), out_shape=...  205 us
    pallas_call x1, Pallas kernels, cast_all(): pl.pallas_call(cast_kernel, in_specs=[anywhere] * 7, out_specs=[anywhere]...  6.44 us

profile of v3, /device:TPU:0, one launch (start us, length us, event | category | flops | bytes accessed | tf_op | source)
XLA Modules:
  0.0 211.9 jit_solution(8604584951922090569)
XLA Ops:
  0.6 204.6 %layers.1 = (bf16[2,384,512]{2,1,0:T(8,128)(2,1)}, bf16[2,384,512]{2,1,0:T(8,128)(2,1)}, bf16[2,384,512]{2,1,0:T(8,128)(2,1)}, bf16[4,2,256,512]{3,2,1,0:T(8,128...) custom-call(bf16[2,384,512]{2,1,0:T(8,128)(2,1)} %refs_0_.1, ...), custom_call_target="tpu_custom_call" | custom-call | tf_op jit(solution)/shard_map/layers/pallas_call | solution.py:1386
  205.3 6.4 %casts.1 = (bf16[2,384,512]{2,1,0:T(8,128)(2,1)}, f32[2,384,512]{2,1,0:T(8,128)}, f32[2048,512]{1,0:T(8,128)}, f32[2304,512]{1,0:T(8,128)}, f32[1,2,512]{2,1,0:T(2,128)}, /*index=5*/f32[1,2,1024]{2,1,0:T(2,128)}) custom-call(bf16[2,384,512]{2,1,0:T(8,128)(2,1)} %get-tuple-element.19.mixed, bf16[2,384,512]{2,1,0:T(8,128)(2,1)} %get-tuple-element.20.gpre, ...), custom_call_target="tpu_custom_call" | custom-call | tf_op jit(solution)/shard_map/casts/pallas_call | solution.py:1343

commit v4 on v3

--- a/solution.py
+++ b/solution.py
@@ -43,11 +43,11 @@
     line = n_dp // 2 == 4
     listed = []
     for kind, index, parts in (
-        ("w", 3, [256]),
+        ("w", 3, [128, 128]),
         ("k", 1, [576] * 4),
-        ("w", 2, [256]),
-        ("w", 1, [256]),
-        ("k", 0, [288, 576, 576, 576, 288]),
+        ("w", 2, [128, 128]),
+        ("w", 1, [128, 128]),
+        ("k", 0, [576] * 4),
         ("w", 0, [64] * 4),
     ):
         start = 0
@@ -1072,12 +1072,6 @@
 
     finish.append(finish_gains)
 
-    def phase(body, layer, between=None):
-        body(layer, 0)
-        if between is not None:
-            between()
-        body(layer, 1)
-
     def of(kind, t):
         return [it for it in items if it.kind == kind and it.t == t]
 
@@ -1089,155 +1083,238 @@
         for it in of(kind, t):
             step(it)
 
+    def nothing():
+        return None
+
+    def paired(arrival, reply, layer, hooks=(nothing, nothing)):
+        for m in range(2):
+            arrival(layer, m)
+            hooks[m]()
+            reply(layer, m)
+
+    def steps(*listed):
+        def go():
+            for body, *rest in listed:
+                body(*rest)
+
+        return go
+
+    up, mid, down, last, out = step_up, step_mid, step_down, step_last, step_out
     wide, taps = 0, 1
     spread_first(wide, 0)
     spread_second(wide, 0)
     ready(wide, 0)
-    phase(first_part, 0)
+    first_part(0, 0)
+    first_part(0, 1)
     own_n.wait()
     norm_wait(sc.n_r)
     spread_first(taps, 0)
     spread_first(taps, 1)
-    phase(first_norm, 0)
-    spread_second(taps, 0)
-    spread_second(taps, 1)
-    phase(hidden_one, 0)
-    spread_first(wide, 1)
-    spread_first(wide, 2)
+    paired(
+        first_norm,
+        hidden_one,
+        0,
+        (
+            steps((spread_second, taps, 0), (spread_second, taps, 1)),
+            steps((spread_first, wide, 1)),
+        ),
+    )
     ready(taps, 0)
     ready(taps, 1)
-    phase(second_part, 0)
-    spread_second(wide, 1)
-    spread_second(wide, 2)
-    phase(hidden_two, 0)
-    spread_first(taps, 2)
-    spread_first(taps, 3)
+    paired(
+        second_part,
+        hidden_two,
+        0,
+        (steps((spread_first, wide, 2), (spread_second, wide, 1)), steps((spread_first, taps, 2))),
+    )
     ready(wide, 1)
-    phase(third_part, 0)
-    spread_second(taps, 2)
-    spread_second(taps, 3)
-    ready(wide, 2)
 
     def turn(layer, m):
         pre_values(0, m)
+        if m == 0:
+            ready(wide, 2)
         first_part(1, m)
 
-    phase(turn, 0)
-    spread_first(wide, 3)
-    phase(first_norm, 1)
-    spread_second(wide, 3)
-    phase(hidden_one, 1)
+    paired(
+        third_part,
+        turn,
+        0,
+        (
+            steps((spread_second, wide, 2), (spread_first, taps, 3), (spread_second, taps, 2)),
+            steps((spread_first, wide, 3)),
+        ),
+    )
+    paired(
+        first_norm,
+        hidden_one,
+        1,
+        (steps((spread_second, taps, 3)), steps((spread_second, wide, 3))),
+    )
     ready(taps, 2)
     ready(taps, 3)
-    phase(second_part, 1)
-    phase(hidden_two, 1)
+    paired(second_part, hidden_two, 1)
     ready(wide, 3)
-    phase(third_part, 1)
-    phase(pre_values, 1)
+    third_part(1, 0)
+    pre_values(1, 0)
+    third_part(1, 1)
+    grad_out_norm(1, 0)
+    pre_values(1, 1)
     outs = [put_out(2, sc.mix.at[...], mixed_ref.at[...])]
-
-    phase(grad_out_norm, 1)
+    grad_out_norm(1, 1)
     wide_grad(3, lambda m: sc.gt[m], lambda m: ag_value(3, m))
-    phase(grad_two, 1)
-    pair_sum("w", 3)
-    run(step_up, "w", 3)
-    phase(grad_second, 1)
+
+    paired(
+        grad_two,
+        grad_second,
+        1,
+        (
+            steps((pair_sum, "w", 3), (one, up, "w", 3, 0)),
+            steps((one, up, "w", 3, 1), (one, mid, "w", 3, 0)),
+        ),
+    )
     taps_grad(1)
-    phase(grad_one, 1, lambda: run(step_mid, "w", 3))
-    pair_sum("k", 1)
-    run(step_up, "k", 1)
-    run(step_down, "w", 3)
-    phase(grad_first, 1)
-    run(step_last, "w", 3)
-    one(step_mid, "k", 1, 0)
-    phase(conv_grad, 1, lambda: one(step_mid, "k", 1, 1))
-    outs.append(put_out(3, sc.gp.at[0], gpre_ref.at[...]))
+    paired(
+        grad_one,
+        grad_first,
+        1,
+        (
+            steps(
+                (pair_sum, "k", 1),
+                (one, up, "k", 1, 0),
+                (one, mid, "w", 3, 1),
+                (one, down, "w", 3, 0),
+            ),
+            steps(
+                (one, up, "k", 1, 1),
+                (one, down, "w", 3, 1),
+                (one, last, "w", 3, 0),
+                (one, mid, "k", 1, 0),
+            ),
+        ),
+    )
+
+    def fold(layer, m):
+        conv_grad(1, m)
+        if m == 1:
+            outs.append(put_out(3, sc.gp.at[0], gpre_ref.at[...]))
+
+    paired(
+        fold,
+        grad_out_norm,
+        0,
+        (
+            steps(
+                (one, up, "k", 1, 2),
+                (one, last, "w", 3, 1),
+                (one, mid, "k", 1, 1),
+                (one, down, "k", 1, 0),
+            ),
+            steps(
+                (one, up, "k", 1, 3),
+                (one, mid, "k", 1, 2),
+                (one, down, "k", 1, 1),
+                (one, last, "k", 1, 0),
+            ),
+        ),
+    )
     wide_grad(2, lambda m: sc.s1[m], lambda m: ag_value(5, m))
-    one(step_mid, "k", 1, 2)
-    one(step_down, "k", 1, 0)
-    one(step_down, "k", 1, 1)
-
-    def early_zero():
-        one(step_mid, "k", 1, 3)
-        one(step_down, "k", 1, 2)
-        pair_sum("w", 2)
-        run(step_up, "w", 2)
-
-    phase(grad_out_norm, 0, early_zero)
     wide_grad(1, lambda m: sc.gt[m], lambda m: ag_value(2, m))
-    one(step_last, "k", 1, 0)
-    one(step_last, "k", 1, 1)
-    def early_two():
-        one(step_down, "k", 1, 3)
-        run(step_mid, "w", 2)
-
-    phase(grad_two, 0, early_two)
-    pair_sum("w", 1)
-    run(step_up, "w", 1)
-    one(step_last, "k", 1, 2)
-    one(step_last, "k", 1, 3)
-    phase(grad_second, 0, lambda: run(step_down, "w", 2))
+    paired(
+        grad_two,
+        grad_second,
+        0,
+        (
+            steps(
+                (pair_sum, "w", 2),
+                (one, up, "w", 2, 0),
+                (one, mid, "k", 1, 3),
+                (one, down, "k", 1, 2),
+                (one, last, "k", 1, 1),
+            ),
+            steps(
+                (one, up, "w", 2, 1),
+                (pair_sum, "w", 1),
+                (one, mid, "w", 2, 0),
+                (one, down, "k", 1, 3),
+                (one, last, "k", 1, 2),
+            ),
+        ),
+    )
     taps_grad(0)
-
-    def early_one():
-        run(step_last, "w", 2)
-        run(step_mid, "w", 1)
-        pair_sum("k", 0)
-        one(step_up, "k", 0, 0)
-
-    phase(grad_one, 0, early_one)
-    for part in range(1, 5):
-        one(step_up, "k", 0, part)
-    run(step_down, "w", 1)
-    phase(grad_first, 0)
+    paired(
+        grad_one,
+        grad_first,
+        0,
+        (
+            steps(
+                (pair_sum, "k", 0),
+                (one, up, "k", 0, 0),
+                (one, mid, "w", 2, 1),
+                (one, down, "w", 2, 0),
+                (one, last, "k", 1, 3),
+            ),
+            steps(
+                (one, up, "k", 0, 1),
+                (one, up, "k", 0, 2),
+                (one, up, "k", 0, 3),
+                (one, mid, "k", 0, 0),
+                (one, down, "w", 2, 1),
+                (one, last, "w", 2, 0),
+            ),
+        ),
+    )
     gains_start()
-    one(step_mid, "k", 0, 0)
-    run(step_last, "w", 1)
-    one(step_mid, "k", 0, 1)
-    one(step_down, "k", 0, 0)
+    one(mid, "k", 0, 1)
+    one(down, "k", 0, 0)
+    one(last, "w", 2, 1)
     conv_grad(0, 0)
-    one(step_mid, "k", 0, 2)
-    one(step_down, "k", 0, 1)
-    one(step_last, "k", 0, 0)
-    run(step_out, "k", 1)
+    one(up, "w", 1, 0)
+    one(mid, "k", 0, 2)
+    one(down, "k", 0, 1)
+    one(last, "k", 0, 0)
+    run(out, "k", 1)
     conv_grad(0, 1)
     wide_grad(0, lambda m: x_ref[m], lambda m: ag_value(4, m))
-    one(step_mid, "k", 0, 3)
-    one(step_down, "k", 0, 2)
-    one(step_last, "k", 0, 1)
-    one(step_out, "k", 0, 0)
+    one(mid, "k", 0, 3)
+    one(down, "k", 0, 2)
+    one(last, "k", 0, 1)
+    one(out, "k", 0, 0)
     outs.append(put_out(4, sc.cv.at[...], conv_ref.at[...]))
-    one(step_mid, "k", 0, 4)
     pair_sum("w", 0)
-    run(step_up, "w", 0)
-    one(step_down, "k", 0, 3)
-    one(step_last, "k", 0, 2)
-    one(step_out, "k", 0, 1)
-    run(step_out, "w", 3)
-    one(step_down, "k", 0, 4)
-    one(step_mid, "w", 0, 0)
-    one(step_last, "k", 0, 3)
-    one(step_out, "k", 0, 2)
-    one(step_mid, "w", 0, 1)
-    one(step_last, "k", 0, 4)
-    one(step_down, "w", 0, 0)
-    one(step_mid, "w", 0, 2)
-    one(step_out, "k", 0, 3)
-    one(step_down, "w", 0, 1)
-    one(step_mid, "w", 0, 3)
-    one(step_last, "w", 0, 0)
-    one(step_out, "k", 0, 4)
-    one(step_down, "w", 0, 2)
-    one(step_last, "w", 0, 1)
-    one(step_out, "w", 0, 0)
-    run(step_out, "w", 2)
-    one(step_down, "w", 0, 3)
-    one(step_last, "w", 0, 2)
-    one(step_out, "w", 0, 1)
-    one(step_last, "w", 0, 3)
-    run(step_out, "w", 1)
-    one(step_out, "w", 0, 2)
-    one(step_out, "w", 0, 3)
+    run(up, "w", 0)
+    one(up, "w", 1, 1)
+    one(mid, "w", 1, 0)
+    one(down, "k", 0, 3)
+    one(last, "k", 0, 2)
+    one(out, "k", 0, 1)
+    run(out, "w", 3)
+    one(mid, "w", 0, 0)
+    one(last, "k", 0, 3)
+    one(out, "k", 0, 2)
+    one(mid, "w", 0, 1)
+    one(down, "w", 0, 0)
+    one(mid, "w", 0, 2)
+    one(down, "w", 1, 0)
+    one(out, "k", 0, 3)
+    one(down, "w", 0, 1)
+    one(mid, "w", 0, 3)
+    one(last, "w", 0, 0)
+    one(mid, "w", 1, 1)
+    one(down, "w", 0, 2)
+    one(last, "w", 0, 1)
+    one(last, "w", 1, 0)
+    one(out, "w", 0, 0)
+    one(down, "w", 0, 3)
+    one(last, "w", 0, 2)
+    one(out, "w", 0, 1)
+    one(down, "w", 1, 1)
+    one(last, "w", 0, 3)
+    run(out, "w", 2)
+    one(out, "w", 1, 0)
+    one(out, "w", 0, 2)
+    one(last, "w", 1, 1)
+    one(out, "w", 0, 3)
+    one(out, "w", 1, 1)
     gains_done()
     run(step_sibling, "w", 3)
     run(step_sibling, "k", 1)
@@ -1251,11 +1328,11 @@
     outs.append(put_out(1, sc.ok.at[...], gtaps_ref.at[...]))
     for s in (3, 2, 1):
         run(step_done, "w", s)
-    last = of("w", 0)
-    for group, part in enumerate((last[:-1], last[-1:]) if len(last) > 1 else (last,)):
+    final = of("w", 0)
+    for group, part in enumerate((final[:-1], final[-1:]) if len(final) > 1 else (final,)):
         first, count = part[0].r0, sum(it.nr for it in part)
         for it in part:
-            if it.i >= last[0].i + 2:
+            if it.i >= final[0].i + 2:
                 step_sibling(it)
         for it in part:
             step_done(it)

time: 212 us -> 200 us (0.943)
  Pallas kernels: 211 us -> 199 us
    pallas_call x1, Pallas kernels: 205 us -> 193 us  [local(): pl.pallas_call(functools.partial(kernel, list(scratch), n_dp), out_shape=...]
where the time goes in v4:
time: 200 us
  Pallas kernels  199 us (100%)
    pallas_call x1, Pallas kernels, local(): pl.pallas_call(functools.partial(kernel, list(scratch), n_dp), out_shape=...  193 us
    pallas_call x1, Pallas kernels, cast_all(): pl.pallas_call(cast_kernel, in_specs=[anywhere] * 7, out_specs=[anywhere]...  6.44 us

profile of v4, /device:TPU:0, one launch (start us, length us, event | category | flops | bytes accessed | tf_op | source)
XLA Modules:
  0.0 200.2 jit_solution(3270722069029946281)
XLA Ops:
  0.6 192.9 %layers.1 = (bf16[2,384,512]{2,1,0:T(8,128)(2,1)}, bf16[2,384,512]{2,1,0:T(8,128)(2,1)}, bf16[2,384,512]{2,1,0:T(8,128)(2,1)}, bf16[4,2,256,512]{3,2,1,0:T(8,128...) custom-call(bf16[2,384,512]{2,1,0:T(8,128)(2,1)} %refs_0_.1, ...), custom_call_target="tpu_custom_call" | custom-call | tf_op jit(solution)/shard_map/layers/pallas_call | solution.py:1463
  193.5 6.4 %casts.1 = (bf16[2,384,512]{2,1,0:T(8,128)(2,1)}, f32[2,384,512]{2,1,0:T(8,128)}, f32[2048,512]{1,0:T(8,128)}, f32[2304,512]{1,0:T(8,128)}, f32[1,2,512]{2,1,0:T(2,128)}, /*index=5*/f32[1,2,1024]{2,1,0:T(2,128)}) custom-call(bf16[2,384,512]{2,1,0:T(8,128)(2,1)} %get-tuple-element.19.mixed, bf16[2,384,512]{2,1,0:T(8,128)(2,1)} %get-tuple-element.20.gpre, ...), custom_call_target="tpu_custom_call" | custom-call | tf_op jit(solution)/shard_map/casts/pallas_call | solution.py:1420

commit v5 on v4

--- a/solution.py
+++ b/solution.py
@@ -14,11 +14,7 @@
 EPS = 1e-05
 LANES = 128
 N_PIPE = 4
-NEAR = [k for k in range(9) if k != 4]
-
-
-def slot_of(tap):
-    return tap if tap < 4 else tap - 1
+SIDES = (7, 6, 5, 2)
 
 
 def dot_nn(a, b):
@@ -79,7 +75,9 @@
         gm=full(4, 2, 128),
         go=full(4, 2, 2, 512),
         msk=full(2, rows, 128),
-        pm=half(2, 8, rows, rows),
+        beside=full(2, 2, rows, 128),
+        above=full(2, 4, 2, rows, 128),
+        yf=full(9, rows, 128),
         part=half(2, 2, 4, rows, 128),
         rsr=half(6, 2, 3, rows, 128),
         ag=half(6, 2, 4, rows, 128),
@@ -97,7 +95,6 @@
         cv=half(2, rows, 512),
         gt=half(2, rows, 512),
         gb=half(2, rows, 1152),
-        yb=half(8, rows, 128),
         tb=half(512, 2 * rows),
         dw=half(4, 2, 256, 512),
         prw=half(4, 256, 512),
@@ -116,6 +113,10 @@
         gsm=full(4, 4, 2, 128),
         gsw=full(2, 4, 2, 512),
         cnt=pltpu.SMEM((2, n_dp), F32),
+        xin=half(2, rows, 512),
+        cin=half(2, rows, 512),
+        gmo=full(1, 2, 512),
+        goo=full(1, 2, 1024),
         counts=pltpu.SMEM((2, 4, n_dp), jnp.int32),
         f_s=dma((2,)),
         f_r=dma((2, 4)),
@@ -124,7 +125,7 @@
         b_r=dma((2, 4)),
         n_s=dma((2,)),
         n_r=dma((2,)),
-        loc=dma((4,)),
+        loc=dma((7,)),
         ex_s=dma((2, 2)),
         ex_r=dma((2, 2)),
         st_s=dma((2, 2)),
@@ -141,15 +142,16 @@
         sib_r=dma((2, 5)),
         g_s=dma((2,)),
         g_r=dma((2,)),
-        out=dma((7,)),
+        out=dma((8,)),
     )
 
 
 def kernel(names, n, *refs):
-    (x_ref, cot_ref, wide_ref, taps_ref, nmid_ref, nout_ref, counts_hbm) = refs[:7]
+    (x_hbm, cot_hbm, wide_ref, taps_ref, nmid_ref, nout_ref, counts_hbm) = refs[:7]
     (mixed_ref, gpre_ref, conv_ref, gwide_ref, gtaps_ref, gmid_ref, gout_ref) = refs[7:14]
     sc = SimpleNamespace(**dict(zip(names, refs[14:])))
     counts_ref = sc.counts
+    x_ref, cot_ref = sc.xin, sc.cin
     rows = x_ref.shape[1]
     n_z, n_own = sizes(n)
     p = lax.axis_index("pipe")
@@ -211,6 +213,9 @@
     )
     own_c = pltpu.make_async_copy(counts_hbm, counts_ref, sc.loc.at[2])
     own_c.start()
+    own_x = pltpu.make_async_copy(x_hbm, sc.xin, sc.loc.at[4])
+    own_cot = pltpu.make_async_copy(cot_hbm, sc.cin, sc.loc.at[5])
+    own_x.start()
     own_w.start()
     own_k.start()
     own_n = pltpu.make_async_copy(
@@ -218,7 +223,10 @@
     )
     own_n.start()
     for e in range(2):
-        sc.go[p, e] = nout_ref[0, :, 512 * e : 512 * e + 512]
+        pltpu.make_async_copy(
+            nout_ref.at[0, :, pl.ds(512 * e, 512)], sc.go.at[p, e], sc.loc.at[6]
+        ).start()
+    own_cot.start()
 
     own_c.wait()
 
@@ -352,47 +360,41 @@
     finish.append(finish_norm)
 
     row_id = lax.broadcasted_iota(jnp.int32, (rows, LANES), 0).astype(F32)
-    lane_id = lax.broadcasted_iota(jnp.int32, (rows, LANES), 1).astype(F32)
 
     def build(m):
-        ends = []
+        ends = [jnp.float32(0.0)]
         total = jnp.int32(0)
-        for g, area in enumerate((49, 36, 25, 4)):
-            total = total + area * counts_ref[m, g, d]
+        for g, side in enumerate(SIDES):
+            total = total + side * side * counts_ref[m, g, d]
             ends.append(total.astype(F32))
-        sc.msk[m] = jnp.where(row_id < ends[3], 1.0, 0.0)
-
-        def pick(values):
-            out = values[4]
-            for g in (3, 2, 1, 0):
-                out = jnp.where(row_id < ends[g], values[g], out)
-            return out
-
-        zero = jnp.zeros((rows, LANES), F32)
-        side = pick([zero + 7.0, zero + 6.0, zero + 5.0, zero + 2.0, zero + 1.0])
-        begin = pick([zero, zero + ends[0], zero + ends[1], zero + ends[2], row_id])
-        one_over = pick(
-            [zero + 1.0 / 7.0, zero + 1.0 / 6.0, zero + 1.0 / 5.0, zero + 0.5, zero + 1.0]
-        )
-        within = row_id - begin
-        within = within - side * side * jnp.floor((within + 0.5) * one_over * one_over)
-        map_row = jnp.floor((within + 0.5) * one_over)
-        map_col = within - side * map_row
-        for k in NEAR:
-            du, dv = k // 3 - 1, k % 3 - 1
-            usable = row_id < ends[3]
-            if du == -1:
-                usable = usable & (map_row > 0.5)
-            if du == 1:
-                usable = usable & (map_row < side - 1.5)
-            if dv == -1:
-                usable = usable & (map_col > 0.5)
-            if dv == 1:
-                usable = usable & (map_col < side - 1.5)
-            target = jnp.where(usable, row_id + du * side + dv, -1000.0)
-            for t in range(rows // LANES):
-                hit = jnp.where(target == lane_id + float(LANES * t), 1.0, 0.0)
-                sc.pm[m, slot_of(k), :, LANES * t : LANES * (t + 1)] = hit.astype(BF16)
+        sc.msk[m] = jnp.where(row_id < ends[4], 1.0, 0.0)
+        left = jnp.zeros((rows, LANES), F32)
+        right = left
+        for g, side in enumerate(SIDES):
+            inside = (row_id >= ends[g]) & (row_id < ends[g + 1])
+            within = row_id - ends[g]
+            within = within - side * side * jnp.floor((within + 0.5) / (side * side))
+            map_row = jnp.floor((within + 0.5) / side)
+            map_col = within - side * map_row
+            left = jnp.where(inside & (map_col > 0.5), 1.0, left)
+            right = jnp.where(inside & (map_col < side - 1.5), 1.0, right)
+            sc.above[m, g, 0] = jnp.where(inside & (map_row > 0.5), 1.0, 0.0)
+            sc.above[m, g, 1] = jnp.where(inside & (map_row < side - 1.5), 1.0, 0.0)
+        sc.beside[m, 0] = left
+        sc.beside[m, 1] = right
+
+    def shifted(values, count):
+        return pltpu.roll(values, count % rows, 0)
+
+    def from_above(values, m):
+        return sum(
+            sc.above[m, g, 0] * shifted(values, side) for g, side in enumerate(SIDES)
+        )
+
+    def from_below(values, m):
+        return sum(
+            sc.above[m, g, 1] * shifted(values, -side) for g, side in enumerate(SIDES)
+        )
 
     for m in range(2):
         build(m)
@@ -465,7 +467,17 @@
         def go(k):
             remote(own, own, ss, rs, (p, lax.rem(d + k, n))).start()
 
-        each(n, 1, go)
+        if n > 8:
+            each(n, 1, go)
+            return
+        high = lax.div(2 * z, n_z)
+        for i in range(n_z - 1):
+            low_far = n_z - 1 - i - lax.div(z + i + 1, n_z)
+            high_far = i + lax.div(i - z + n_z, n_z)
+            far = high * high_far + (1 - high) * low_far
+            for e in range(2):
+                remote(own, own, ss, rs, (p, 2 * far + e)).start()
+        remote(own, own, ss, rs, sibling).start()
 
     def st_wait(wide, i, m):
         st_bytes(sc.st_r, wide, i, m)
@@ -580,20 +592,20 @@
     def second_part(layer, m):
         ag_wait(layer, m)
         h = ag_value(layer, m)
-        centre = None
         for j in range(5):
             width = 256 if j < 4 else 128
             y = dot_nn(h, taps_of(layer, [2 * j + e for e in range(width // LANES)]))
             for e in range(width // LANES):
-                tap = 2 * j + e
-                if tap == 4:
-                    centre = y[:, lanes(e)]
-                    sc.midv[2 * layer + 1, m] = centre
-                else:
-                    sc.yb[slot_of(tap)] = y[:, lanes(e)].astype(BF16)
-        total = sc.midv[2 * layer + 1, m]
-        for k in range(8):
-            total = total + dot_nn(sc.pm[m, k], sc.yb[k])
+                sc.yf[2 * j + e] = y[:, lanes(e)]
+
+        def across(k):
+            return (
+                sc.yf[k + 1]
+                + sc.beside[m, 0] * shifted(sc.yf[k], 1)
+                + sc.beside[m, 1] * shifted(sc.yf[k + 2], -1)
+            )
+
+        total = across(3) + from_above(across(0), m) + from_below(across(6), m)
         mid_moments(2 * layer + 1, m, total)
 
     def hidden_two(layer, m):
@@ -690,11 +702,12 @@
 
     def grad_second(layer, m):
         gs = mid_back(2 * layer + 1, m)
-        for k in range(9):
-            if k == 4:
-                sc.gb[m, :, lanes(k)] = gs
-            else:
-                sc.gb[m, :, lanes(k)] = dot_nn(sc.pm[m, slot_of(8 - k)], gs).astype(BF16)
+        own = gs.astype(F32)
+        for du, moved in ((0, own), (1, from_above(own, m)), (-1, from_below(own, m))):
+            k = 3 * (du + 1)
+            sc.gb[m, :, lanes(k + 1)] = moved.astype(BF16)
+            sc.gb[m, :, lanes(k + 2)] = (sc.beside[m, 0] * shifted(moved, 1)).astype(BF16)
+            sc.gb[m, :, lanes(k)] = (sc.beside[m, 1] * shifted(moved, -1)).astype(BF16)
         g = sc.gb[m]
         rs_send(
             4 + layer,
@@ -1062,10 +1075,12 @@
     def gains_done():
         gains_wait(sc.g_r)
         for q in range(4):
-            gmid_ref[0, :, lanes(q)] = sc.gsm[p, q]
+            sc.gmo[0, :, lanes(q)] = sc.gsm[p, q]
         layer = lax.div(p, 2)
         for e in range(2):
-            gout_ref[0, :, 512 * e : 512 * e + 512] = sc.gsw[layer, 2 * parity + e]
+            sc.goo[0, :, 512 * e : 512 * e + 512] = sc.gsw[layer, 2 * parity + e]
+        outs.append(put_out(0, sc.gmo.at[...], gmid_ref.at[...]))
+        outs.append(put_out(7, sc.goo.at[...], gout_ref.at[...]))
 
     def finish_gains():
         gains_wait(sc.g_s)
@@ -1104,9 +1119,12 @@
     spread_first(wide, 0)
     spread_second(wide, 0)
     ready(wide, 0)
+    own_x.wait()
     first_part(0, 0)
     first_part(0, 1)
     own_n.wait()
+    bytes_wait(sc.go.at[0], sc.loc.at[6])
+    own_cot.wait()
     norm_wait(sc.n_r)
     spread_first(taps, 0)
     spread_first(taps, 1)
@@ -1453,7 +1471,6 @@
     n_dp = group_counts.shape[1]
     micro, rows, width = block_input.shape
     scratch = scratch_list(n_dp, rows)
-    vmem = pl.BlockSpec(memory_space=pltpu.VMEM)
     anywhere = pl.BlockSpec(memory_space=pl.ANY)
 
     def shape(dims, dtype):
@@ -1471,8 +1488,8 @@
             shape(norm_mid.shape, F32),
             shape(norm_out.shape, F32),
         ],
-        in_specs=[vmem, vmem, anywhere, anywhere, vmem, vmem, anywhere],
-        out_specs=[anywhere] * 5 + [vmem] * 2,
+        in_specs=[anywhere] * 7,
+        out_specs=[anywhere] * 7,
         scratch_shapes=list(scratch.values()),
         compiler_params=pltpu.CompilerParams(
             collective_id=0, has_side_effects=True, vmem_limit_bytes=62 * 2**20

time: 200 us -> 196 us (0.980)
  Pallas kernels: 199 us -> 195 us
    pallas_call x1, Pallas kernels: 193 us -> 189 us  [local(): pl.pallas_call(functools.partial(kernel, list(scratch), n_dp), out_shape=...]
where the time goes in v5:
time: 196 us
  Pallas kernels  195 us (99%)
    pallas_call x1, Pallas kernels, local(): pl.pallas_call(functools.partial(kernel, list(scratch), n_dp), out_shape=...  189 us
    pallas_call x1, Pallas kernels, cast_all(): pl.pallas_call(cast_kernel, in_specs=[anywhere] * 7, out_specs=[anywhere]...  6.44 us

profile of v5, /device:TPU:0, one launch (start us, length us, event | category | flops | bytes accessed | tf_op | source)
XLA Modules:
  0.0 195.9 jit_solution(10935964962569579535)
XLA Ops:
  0.6 188.6 %layers.1 = (bf16[2,384,512]{2,1,0:T(8,128)(2,1)}, bf16[2,384,512]{2,1,0:T(8,128)(2,1)}, bf16[2,384,512]{2,1,0:T(8,128)(2,1)}, bf16[4,2,256,512]{3,2,1,0:T(8,128...) custom-call(bf16[2,384,512]{2,1,0:T(8,128)(2,1)} %refs_0_.1, ...), custom_call_target="tpu_custom_call" | custom-call | tf_op jit(solution)/shard_map/layers/pallas_call | solution.py:1480
  189.3 6.4 %casts.1 = (bf16[2,384,512]{2,1,0:T(8,128)(2,1)}, f32[2,384,512]{2,1,0:T(8,128)}, f32[2048,512]{1,0:T(8,128)}, f32[2304,512]{1,0:T(8,128)}, f32[1,2,512]{2,1,0:T(2,128)}, /*index=5*/f32[1,2,1024]{2,1,0:T(2,128)}) custom-call(bf16[2,384,512]{2,1,0:T(8,128)(2,1)} %get-tuple-element.19.mixed, bf16[2,384,512]{2,1,0:T(8,128)(2,1)} %get-tuple-element.20.gpre, ...), custom_call_target="tpu_custom_call" | custom-call | tf_op jit(solution)/shard_map/casts/pallas_call | solution.py:1438

commit v6 on v5

--- a/solution.py
+++ b/solution.py
@@ -40,10 +40,10 @@
     listed = []
     for kind, index, parts in (
         ("w", 3, [128, 128]),
-        ("k", 1, [576] * 4),
+        ("k", 1, [768] * 3),
         ("w", 2, [128, 128]),
         ("w", 1, [128, 128]),
-        ("k", 0, [576] * 4),
+        ("k", 0, [288, 288, 288, 288, 576, 576]),
         ("w", 0, [64] * 4),
     ):
         start = 0
@@ -73,13 +73,17 @@
         wt=half(4, 512, 512),
         k2=half(2, 18, 256, 128),
         gm=full(4, 2, 128),
+        gmf=full(4, 2, 512),
+        hf=half(2, 2, rows, 512),
+        gff=half(2, 2, rows, 512),
+        sml=full(2, 2, 4, 4, 128),
         go=full(4, 2, 2, 512),
         msk=full(2, rows, 128),
         beside=full(2, 2, rows, 128),
         above=full(2, 4, 2, rows, 128),
         yf=full(9, rows, 128),
         part=half(2, 2, 4, rows, 128),
-        rsr=half(6, 2, 3, rows, 128),
+        rsr=half(6 if line else 2, 2, 3, rows, 128),
         ag=half(6, 2, 4, rows, 128),
         stm=full(8, 2, n_dp, 2, 128),
         stw=full(4, 2, n_dp, 2, 512),
@@ -92,10 +96,10 @@
         s1=half(2, rows, 512),
         mix=half(2, rows, 512),
         gp=half(2, 2, rows, 512),
-        cv=half(2, rows, 512),
         gt=half(2, rows, 512),
         gb=half(2, rows, 1152),
         tb=half(512, 2 * rows),
+        ack=full(512, 1152),
         dw=half(4, 2, 256, 512),
         prw=half(4, 256, 512),
         zsw=half(4, 256, 512),
@@ -107,9 +111,9 @@
         fzk=half(2, 2304, 128),
         ok=half(2304, 512),
         zow=half(4, 256, 512) if line else half(4, n_z - 1, 256 // n_own, 512),
-        ziw=half(4, 128, 512),
+        ziw=half(4, 128, 512) if line else half(1, 16, 128),
         zok=half(2, 2304, 128) if line else half(2, n_z - 1, 2304 // n_own, 128),
-        zik=half(2, 1152, 128),
+        zik=half(2, 1152, 128) if line else half(1, 16, 128),
         gsm=full(4, 4, 2, 128),
         gsw=full(2, 4, 2, 512),
         cnt=pltpu.SMEM((2, n_dp), F32),
@@ -123,23 +127,28 @@
         z_r=dma((2, 4)),
         b_s=dma((2, 4)),
         b_r=dma((2, 4)),
-        n_s=dma((2,)),
-        n_r=dma((2,)),
-        loc=dma((7,)),
+        n_s=dma((3,)),
+        n_r=dma((3,)),
+        sm_s=dma((2, 2)),
+        sm_r=dma((2, 2)),
+        loc=dma((8,)),
         ex_s=dma((2, 2)),
         ex_r=dma((2, 2)),
         st_s=dma((2, 2)),
         st_r=dma((2, 2)),
         pw_s=dma((6,)),
         pw_r=dma((6,)),
-        it_s=dma((items,)),
+        it_s=dma((6,)),
         one_r=dma((items,)),
         mid_r=dma((items,)),
         inn_r=dma((items,)),
-        to_s=dma((items,)),
-        to_r=dma((2, 5)),
-        sib_s=dma((2, 5)),
-        sib_r=dma((2, 5)),
+        to_s=dma((6,)),
+        ga_s=dma((6 if n_z != 4 else 1,)),
+        sh_s=dma((4,)),
+        sh_r=dma((4,)),
+        to_r=dma((2, 6)),
+        sib_s=dma((2,)),
+        sib_r=dma((2, 6)),
         g_s=dma((2,)),
         g_r=dma((2,)),
         out=dma((8,)),
@@ -227,6 +236,8 @@
             nout_ref.at[0, :, pl.ds(512 * e, 512)], sc.go.at[p, e], sc.loc.at[6]
         ).start()
     own_cot.start()
+    own_g = pltpu.make_async_copy(nmid_ref.at[0], sc.gmf.at[p], sc.loc.at[7])
+    own_g.start()
 
     own_c.wait()
 
@@ -277,7 +288,8 @@
                 sc.n_s.at[0],
                 sc.n_r.at[0],
                 (q, d),
-            )
+            ),
+            remote(nmid_ref.at[0], sc.gmf.at[p], sc.n_s.at[2], sc.n_r.at[2], (q, d)),
         ]
         for e in range(2):
             listed.append(
@@ -294,6 +306,7 @@
     def norm_wait(sems):
         bytes_wait(sc.gm.at[pl.ds(0, 3)], sems.at[0])
         bytes_wait(sc.go.at[pl.ds(0, 3)], sems.at[1])
+        bytes_wait(sc.gmf.at[pl.ds(0, 3)], sems.at[2])
 
     def pass_z(kind, s):
         view = held(kind, s, quarter)
@@ -405,8 +418,11 @@
         ("rs", 3), ("rs", 5), ("ag", 5), ("rs", 2), ("rs", 4), ("ag", 4),
     ]
 
+    def rs_slot(rid):
+        return rid if sc.rsr.shape[0] == 6 else rs_par[rid]
+
     def three(kind, i, m):
-        return sc.rsr.at[i, m] if kind == "rs" else sc.ag.at[i, m, pl.ds(0, 3)]
+        return sc.rsr.at[rs_slot(i), m] if kind == "rs" else sc.ag.at[i, m, pl.ds(0, 3)]
 
     def exchange_wait(sems, kind, i, m):
         turn = exchange_order.index((kind, i))
@@ -422,7 +438,7 @@
         exchange_wait(sc.ex_r, "rs", rid, m)
         total = sc.part[par, m, p].astype(F32)
         for k in range(3):
-            total = total + sc.rsr[rid, m, k].astype(F32)
+            total = total + sc.rsr[rs_slot(rid), m, k].astype(F32)
         return total
 
     def ag_start(aid, m, value):
@@ -551,7 +567,7 @@
             sc.part[par, m, 2 * j + 1] = half[:, LANES:]
         for off in range(1, 4):
             q = pipe_at(off)
-            remote(sc.part.at[par, m, q], sc.rsr.at[rid, m, off - 1], ss, rs, (q, d)).start()
+            remote(sc.part.at[par, m, q], sc.rsr.at[rs_slot(rid), m, off - 1], ss, rs, (q, d)).start()
 
     def first_part(layer, m):
         s = stream(layer, m)
@@ -578,7 +594,12 @@
         return (sc.msk[m] * (u * sigmoid(u))).astype(BF16)
 
     def hidden_one(layer, m):
-        ag_start(layer, m, mid_hidden(2 * layer, m))
+        i = 2 * layer
+        mean, inv = combine(False, i, m)
+        sc.inv_mid[i, m] = inv
+        vhat = ((sc.midv[i, m] - mean) * inv).astype(BF16)
+        sc.midv[i, m] = vhat.astype(F32)
+        ag_start(layer, m, vhat)
 
     def taps_of(layer, taps):
         return jnp.concatenate(
@@ -591,7 +612,11 @@
 
     def second_part(layer, m):
         ag_wait(layer, m)
-        h = ag_value(layer, m)
+        for q in range(4):
+            gain, bias = sc.gmf[2 * layer, 0:1, lanes(q)], sc.gmf[2 * layer, 1:2, lanes(q)]
+            u = gain * sc.ag[layer, m, q].astype(F32) + bias
+            sc.hf[layer, m, :, lanes(q)] = (sc.msk[m] * (u * sigmoid(u))).astype(BF16)
+        h = sc.hf[layer, m]
         for j in range(5):
             width = 256 if j < 4 else 128
             y = dot_nn(h, taps_of(layer, [2 * j + e for e in range(width // LANES)]))
@@ -722,26 +747,58 @@
 
     def grad_one(layer, m):
         mid_grad(2 * layer, m, rs_sum(4 + layer, m, rs_par[4 + layer]))
+        ag_start(4 + layer, m, sc.dzm[m].astype(BF16))
+
+    def small_copy(layer, m, off):
+        own = sc.sml.at[layer, m, p]
+        return remote(own, own, sc.sm_s.at[layer, m], sc.sm_r.at[layer, m], (pipe_at(off), d))
 
     def grad_first(layer, m):
-        ag_start(4 + layer, m, mid_back(2 * layer, m))
+        i = 2 * layer
+        sums = back_sums(False, 4 + i, m)
+        if m == 0:
+            sc.gsm[i, p] = sums
+        else:
+            sc.gsm[i, p] = sc.gsm[i, p] + sums
+        scale = sc.gm[i, 0:1, :] * sc.inv_mid[i, m]
+        s1 = scale * (sums[0:1, :] / totals[m])
+        s0 = scale * (sums[1:2, :] / totals[m])
+        sc.sml[layer, m, p] = jnp.concatenate([scale, s0, s1, s1], 0)
+        for off in range(1, 4):
+            small_copy(layer, m, off).start()
+
+    def finish_small():
+        for layer in range(2):
+            for m in range(2):
+                bytes_wait(sc.sml.at[layer, m, pl.ds(0, 3)], sc.sm_s.at[layer, m])
+
+    finish.append(finish_small)
+
+    def slopes(m):
+        for i in range(4):
+            pre = sc.pre0[m, :, lanes(i)]
+            sig = sigmoid(pre)
+            sc.pre0[m, :, lanes(i)] = sc.msk[m] * (sig * (1.0 + pre * (1.0 - sig)))
 
     def conv_grad(layer, m):
         ag_wait(4 + layer, m)
-        g = ag_value(4 + layer, m)
-        mask = sc.msk[m]
+        bytes_wait(sc.sml.at[layer, m, pl.ds(0, 3)], sc.sm_r.at[layer, m])
+        for q in range(4):
+            scale, s0, s1 = (sc.sml[layer, m, q, k : k + 1, :] for k in range(3))
+            dz = sc.ag[4 + layer, m, q].astype(F32)
+            vhat = sc.ag[layer, m, q].astype(F32)
+            dv = sc.msk[m] * (scale * dz - s0 - s1 * vhat)
+            sc.gff[layer, m, :, lanes(q)] = dv.astype(BF16)
+        g = sc.gff[layer, m]
         for j in range(2):
             r = dot_nt(g, sc.wt[2 * layer, 256 * j : 256 * j + 256, :]).astype(BF16)
             if layer == 0:
-                sc.cv[m, :, 256 * j : 256 * j + 256] = r
+                sc.cin[m, :, 256 * j : 256 * j + 256] = r
                 continue
             for e in range(2):
                 i = 2 * j + e
-                pre = sc.pre0[m, :, lanes(i)]
-                sig = sigmoid(pre)
-                slope = sig * (1.0 + pre * (1.0 - sig))
                 up = sc.gp[1, m, :, lanes(i)].astype(F32) + r[:, lanes(e)].astype(F32)
-                grad = (up * mask * slope).astype(BF16)
+                grad = (up * sc.pre0[m, :, lanes(i)]).astype(BF16)
                 sc.gp[0, m, :, lanes(i)] = grad
                 sc.stw[2, m, d, :, lanes(i)] = local_sums(
                     grad.astype(F32), sc.widv[0, m, :, lanes(i)]
@@ -766,8 +823,40 @@
                 sc.dw[s, h, :, cols] = r.astype(BF16)
         pair_copy("w", s).start()
 
+    def wide_early():
+        turned([x_ref[0], x_ref[1]])
+        g = sc.gff[0, 0]
+        for j in range(2):
+            cols = slice(256 * j, 256 * j + 256)
+            sc.ack[:, cols] = dot_nn(sc.tb[:, :rows], g[:, cols])
+
+    def wide_late():
+        g = sc.gff[0, 1]
+        for j in range(2):
+            cols = slice(256 * j, 256 * j + 256)
+            for h in range(2):
+                part = slice(256 * h, 256 * h + 256)
+                r = sc.ack[part, cols] + dot_nn(sc.tb[part, rows:], g[:, cols])
+                sc.dw[0, h, :, cols] = r.astype(BF16)
+        pair_copy("w", 0).start()
+
+    def taps_early():
+        turned([sc.hf[0, 0], sc.hf[0, 1]])
+        for j in range(5):
+            cols = slice(256 * j, min(256 * j + 256, 1152))
+            sc.ack[:, cols] = dot_nn(sc.tb[:, :rows], sc.gb[0, :, cols])
+
+    def taps_late():
+        for j in range(5):
+            cols = slice(256 * j, min(256 * j + 256, 1152))
+            r = (sc.ack[:, cols] + dot_nn(sc.tb[:, rows:], sc.gb[1, :, cols])).astype(BF16)
+            for e in range(r.shape[1] // LANES):
+                tap = 2 * j + e
+                sc.dk[0, 512 * tap : 512 * tap + 512, :] = r[:, lanes(e)]
+        pair_copy("k", 0).start()
+
     def taps_grad(layer):
-        turned([ag_value(layer, 0), ag_value(layer, 1)])
+        turned([sc.hf[layer, 0], sc.hf[layer, 1]])
         for j in range(5):
             width = 256 if j < 4 else 128
             rhs = both(lambda m: sc.gb[m, :, 256 * j : 256 * j + width])
@@ -803,6 +892,9 @@
     line = n_z == 4
     inner = (z == 1) | (z == 2)
 
+    def tile_sem(it):
+        return it.t if it.kind == "w" else 4 + it.t
+
     def tile(it, name):
         return getattr(sc, name + it.kind)
 
@@ -818,7 +910,7 @@
         return remote(
             tile(it, "zs").at[it.t, rows_of],
             tile(it, "zo").at[it.t, rows_of],
-            sc.it_s.at[it.i],
+            sc.it_s.at[tile_sem(it)],
             sc.one_r.at[it.i],
             (p, 2 * (1 + lax.div(z, 3)) + c),
         )
@@ -827,7 +919,7 @@
         return remote(
             tile(it, "zs").at[it.t, part_rows(it, 2 - z)],
             tile(it, "zi").at[it.t, pl.ds(it.r0 // 2, it.nr // 2)],
-            sc.it_s.at[it.i],
+            sc.it_s.at[tile_sem(it)],
             sc.mid_r.at[it.i],
             (p, 2 * (3 - z) + c),
         )
@@ -835,13 +927,13 @@
     def inn_copy(it):
         view = tile(it, "fz").at[it.t, part_rows(it, z - 1)]
         return remote(
-            view, view, sc.it_s.at[it.i], sc.inn_r.at[it.i], (p, 2 * (3 - z) + c)
+            view, view, sc.it_s.at[tile_sem(it)], sc.inn_r.at[it.i], (p, 2 * (3 - z) + c)
         )
 
     def down_copy(it, e):
         view = tile(it, "fz").at[it.t, part_rows(it, z - 1 if e == 0 else 2 - z)]
         return remote(
-            view, view, sc.it_s.at[it.i], sc.one_r.at[it.i], (p, 2 * (3 * (z - 1)) + c)
+            view, view, sc.it_s.at[tile_sem(it)], sc.one_r.at[it.i], (p, 2 * (3 * (z - 1)) + c)
         )
 
     def direct_rows(it, j):
@@ -859,7 +951,7 @@
         return j, remote(
             tile(it, "zs").at[it.t, direct_rows(it, lax.rem(j, n_own))],
             tile(it, "zo").at[it.t, k - 1],
-            sc.it_s.at[it.i],
+            sc.it_s.at[tile_sem(it)],
             sc.one_r.at[it.i],
             (p, 2 * j + c),
         )
@@ -867,7 +959,7 @@
     def gather_copy(it, k):
         j = lax.rem(z + k, n_z)
         view = tile(it, "fz").at[it.t, direct_rows(it, lax.rem(z, n_own))]
-        return remote(view, view, sc.to_s.at[it.i], sc.mid_r.at[it.i], (p, 2 * j + c))
+        return remote(view, view, sc.ga_s.at[tile_sem(it)], sc.mid_r.at[it.i], (p, 2 * j + c))
 
     def add_rows(target, first, second):
         target[...] = (first[...].astype(F32) + second[...].astype(F32)).astype(BF16)
@@ -952,10 +1044,35 @@
         return remote(
             some(it, "fz", it.r0, it.nr),
             landing(it, p, c),
-            sc.to_s.at[it.i],
+            sc.to_s.at[tile_sem(it)],
             to_sem(it, sc.to_r),
             (owner_of(it), d),
         )
+
+    def shared(it):
+        return line and it.kind == "w" and it.t == 0
+
+    def in_charge(it):
+        outer = (z == 0) | (z == 3)
+        return outer if it.part % 2 == 0 else jnp.logical_not(outer)
+
+    def sends_out(it):
+        if shared(it):
+            return (p == 1) | ((p > 1) & in_charge(it))
+        return p != owner_of(it)
+
+    def passes_on(it):
+        if shared(it):
+            return (p == 0) & in_charge(it)
+        return p < 0
+
+    def pass_copy(it):
+        view = sc.ow.at[pl.ds(2, 2), c, pl.ds(it.r0, it.nr)]
+        return remote(view, view, sc.sh_s.at[it.part], sc.sh_r.at[it.part], z_pair)
+
+    def step_inner_out(it):
+        if line:
+            pl.when(inner)(lambda: deliver(it))
 
     def step_out(it):
         if line:
@@ -963,6 +1080,7 @@
             @pl.when((z == 0) | (z == 3))
             def _():
                 bytes_wait(some(it, "fz", it.r0, it.nr), sc.one_r.at[it.i])
+                deliver(it)
 
         else:
             count = it.nr // n_own
@@ -978,7 +1096,10 @@
                 def _():
                     bytes_wait(some(it, "fz", it.r0, count * n_own), sc.mid_r.at[it.i])
 
-        @pl.when(p != owner_of(it))
+            deliver(it)
+
+    def deliver(it):
+        @pl.when(sends_out(it))
         def _():
             to_copy(it).start()
 
@@ -996,7 +1117,7 @@
     def sibling_copy(it, q):
         view = landing(it, q, c)
         return remote(
-            view, view, to_sem(it, sc.sib_s), to_sem(it, sc.sib_r), sibling
+            view, view, sc.sib_s.at[0 if it.kind == "w" else 1], to_sem(it, sc.sib_r), sibling
         )
 
     def slices(it, count):
@@ -1010,7 +1131,32 @@
             for q in range(4):
                 sibling_copy(it, q).start()
 
-        pl.when(p == owner_of(it))(go)
+        if not shared(it):
+            pl.when(p == owner_of(it))(go)
+            return
+
+        @pl.when((p == 0) & in_charge(it))
+        def _():
+            bytes_wait(slices(it, 3), to_sem(it, sc.to_r))
+            pass_copy(it).start()
+            for q in range(4):
+                sibling_copy(it, q).start()
+
+        @pl.when((p == 0) & jnp.logical_not(in_charge(it)))
+        def _():
+            bytes_wait(slices(it, 1), to_sem(it, sc.to_r))
+            for q in range(2):
+                sibling_copy(it, q).start()
+
+    def step_rest(it):
+        if not shared(it):
+            return
+
+        @pl.when((p == 0) & jnp.logical_not(in_charge(it)))
+        def _():
+            bytes_wait(slices(it, 2), sc.sh_r.at[it.part])
+            for q in range(2, 4):
+                sibling_copy(it, q).start()
 
     def step_done(it):
         def go():
@@ -1018,41 +1164,49 @@
 
         pl.when(p == (it.t if it.kind == "w" else 2 * it.t + 1 - c))(go)
 
-    def twice(it):
-        if it.kind == "w":
-            return sc.dw.at[it.t, :, pl.ds(0, it.nr)]
-        return sc.dk.at[it.t, pl.ds(0, 2 * it.nr)]
-
     def finish_grads():
         for kind, t in [("w", s) for s in range(4)] + [("k", layer) for layer in range(2)]:
             pair_copy(kind, t).wait_send()
-        for it in items:
+            whole = next(it for it in items if it.kind == kind and it.t == t)
+            sends = sc.it_s.at[tile_sem(whole)]
+            half = tile(whole, "zs").at[t]
             if line:
 
                 @pl.when(inner)
-                def _(it=it):
-                    bytes_wait(twice(it), sc.it_s.at[it.i])
+                def _(kind=kind, t=t, sends=sends):
+                    bytes_wait((sc.dw if kind == "w" else sc.dk).at[t], sends)
 
                 @pl.when((z == 0) | (z == 3))
-                def _(it=it):
-                    up_copy(it).wait_send()
+                def _(half=half, sends=sends):
+                    bytes_wait(half, sends)
 
             else:
 
-                def sent(k, it=it):
+                def sent(k, it=whole):
                     j, copy = scatter_copy(it, k)
                     owner(j, lambda: copy.wait_send())
 
                 each(n_z, 1, sent)
-                owner(z, lambda: each(n_z, 1, lambda k: gather_copy(it, k).wait_send()))
-
-            @pl.when(p != owner_of(it))
+                owner(
+                    z,
+                    lambda it=whole: each(n_z, 1, lambda k: gather_copy(it, k).wait_send()),
+                )
+
+        for it in items:
+
+            @pl.when(sends_out(it))
             def _(it=it):
-                to_copy(it).wait_send()
-
-            @pl.when(p == owner_of(it))
+                bytes_wait(some(it, "fz", it.r0, it.nr), sc.to_s.at[tile_sem(it)])
+
+            @pl.when(passes_on(it))
             def _(it=it):
-                bytes_wait(slices(it, 4), to_sem(it, sc.sib_s))
+                bytes_wait(slices(it, 2), sc.sh_s.at[it.part])
+
+        bytes_wait(sc.ow.at[:, 0], sc.sib_s.at[0])
+
+        @pl.when(c == parity)
+        def _():
+            bytes_wait(sc.ok.at[...], sc.sib_s.at[1])
 
     finish.append(finish_grads)
 
@@ -1115,6 +1269,7 @@
         return go
 
     up, mid, down, last, out = step_up, step_mid, step_down, step_last, step_out
+    inside = step_inner_out
     wide, taps = 0, 1
     spread_first(wide, 0)
     spread_second(wide, 0)
@@ -1125,6 +1280,7 @@
     own_n.wait()
     bytes_wait(sc.go.at[0], sc.loc.at[6])
     own_cot.wait()
+    own_g.wait()
     norm_wait(sc.n_r)
     spread_first(taps, 0)
     spread_first(taps, 1)
@@ -1180,62 +1336,44 @@
     outs = [put_out(2, sc.mix.at[...], mixed_ref.at[...])]
     grad_out_norm(1, 1)
     wide_grad(3, lambda m: sc.gt[m], lambda m: ag_value(3, m))
-
     paired(
         grad_two,
         grad_second,
         1,
         (
-            steps((pair_sum, "w", 3), (one, up, "w", 3, 0)),
-            steps((one, up, "w", 3, 1), (one, mid, "w", 3, 0)),
+            steps((pair_sum, "w", 3), (one, up, "w", 3, 0), (slopes, 0)),
+            steps((one, up, "w", 3, 1), (slopes, 1), (one, mid, "w", 3, 0)),
         ),
     )
     taps_grad(1)
-    paired(
-        grad_one,
-        grad_first,
-        1,
-        (
-            steps(
-                (pair_sum, "k", 1),
-                (one, up, "k", 1, 0),
-                (one, mid, "w", 3, 1),
-                (one, down, "w", 3, 0),
-            ),
-            steps(
-                (one, up, "k", 1, 1),
-                (one, down, "w", 3, 1),
-                (one, last, "w", 3, 0),
-                (one, mid, "k", 1, 0),
-            ),
-        ),
-    )
-
-    def fold(layer, m):
-        conv_grad(1, m)
-        if m == 1:
-            outs.append(put_out(3, sc.gp.at[0], gpre_ref.at[...]))
-
-    paired(
-        fold,
-        grad_out_norm,
-        0,
-        (
-            steps(
-                (one, up, "k", 1, 2),
-                (one, last, "w", 3, 1),
-                (one, mid, "k", 1, 1),
-                (one, down, "k", 1, 0),
-            ),
-            steps(
-                (one, up, "k", 1, 3),
-                (one, mid, "k", 1, 2),
-                (one, down, "k", 1, 1),
-                (one, last, "k", 1, 0),
-            ),
-        ),
-    )
-    wide_grad(2, lambda m: sc.s1[m], lambda m: ag_value(5, m))
+    grad_one(1, 0)
+    steps(
+        (pair_sum, "k", 1),
+        (one, up, "k", 1, 0),
+        (one, mid, "w", 3, 1),
+        (one, down, "w", 3, 0),
+    )()
+    grad_first(1, 0)
+    grad_one(1, 1)
+    conv_grad(1, 0)
+    steps(
+        (one, up, "k", 1, 1),
+        (one, down, "w", 3, 1),
+        (one, last, "w", 3, 0),
+        (one, mid, "k", 1, 0),
+    )()
+    grad_first(1, 1)
+    grad_out_norm(0, 0)
+    conv_grad(1, 1)
+    outs.append(put_out(3, sc.gp.at[0], gpre_ref.at[...]))
+    steps(
+        (one, up, "k", 1, 2),
+        (one, last, "w", 3, 1),
+        (one, mid, "k", 1, 1),
+        (one, down, "k", 1, 0),
+        (wide_grad, 2, lambda m: sc.s1[m], lambda m: sc.gff[1, m]),
+    )()
+    grad_out_norm(0, 1)
     wide_grad(1, lambda m: sc.gt[m], lambda m: ag_value(2, m))
     paired(
         grad_two,
@@ -1243,100 +1381,127 @@
         0,
         (
             steps(
+                (pair_sum, "w", 1),
+                (one, up, "w", 1, 0),
+                (one, mid, "k", 1, 2),
+                (one, down, "k", 1, 1),
+                (one, last, "k", 1, 0),
+            ),
+            steps(
+                (one, up, "w", 1, 1),
                 (pair_sum, "w", 2),
-                (one, up, "w", 2, 0),
-                (one, mid, "k", 1, 3),
+                (one, mid, "w", 1, 0),
                 (one, down, "k", 1, 2),
                 (one, last, "k", 1, 1),
-            ),
-            steps(
-                (one, up, "w", 2, 1),
-                (pair_sum, "w", 1),
-                (one, mid, "w", 2, 0),
-                (one, down, "k", 1, 3),
-                (one, last, "k", 1, 2),
+                (taps_early,),
             ),
         ),
     )
-    taps_grad(0)
-    paired(
-        grad_one,
-        grad_first,
-        0,
-        (
-            steps(
-                (pair_sum, "k", 0),
-                (one, up, "k", 0, 0),
-                (one, mid, "w", 2, 1),
-                (one, down, "w", 2, 0),
-                (one, last, "k", 1, 3),
-            ),
-            steps(
-                (one, up, "k", 0, 1),
-                (one, up, "k", 0, 2),
-                (one, up, "k", 0, 3),
-                (one, mid, "k", 0, 0),
-                (one, down, "w", 2, 1),
-                (one, last, "w", 2, 0),
-            ),
-        ),
-    )
+    taps_late()
+    grad_one(0, 0)
+    steps(
+        (pair_sum, "k", 0),
+        (one, up, "k", 0, 0),
+        (one, up, "k", 0, 1),
+        (one, mid, "w", 1, 1),
+        (one, down, "w", 1, 0),
+        (one, last, "k", 1, 2),
+    )()
+    grad_first(0, 0)
+    grad_one(0, 1)
+    steps(
+        (one, up, "k", 0, 2),
+        (one, up, "k", 0, 3),
+        (one, up, "k", 0, 4),
+        (one, up, "k", 0, 5),
+        (one, mid, "k", 0, 0),
+        (one, mid, "k", 0, 1),
+        (one, down, "w", 1, 1),
+        (one, last, "w", 1, 0),
+    )()
+    one(down, "k", 0, 0)
+    one(mid, "k", 0, 2)
+    conv_grad(0, 0)
+    one(down, "k", 0, 1)
+    grad_first(0, 1)
     gains_start()
-    one(mid, "k", 0, 1)
-    one(down, "k", 0, 0)
-    one(last, "w", 2, 1)
-    conv_grad(0, 0)
-    one(up, "w", 1, 0)
-    one(mid, "k", 0, 2)
-    one(down, "k", 0, 1)
+    one(mid, "k", 0, 3)
     one(last, "k", 0, 0)
+    one(down, "k", 0, 2)
+    one(last, "w", 1, 1)
+    one(up, "w", 2, 0)
+    one(last, "k", 0, 1)
+    one(mid, "k", 0, 4)
+    one(down, "k", 0, 3)
+    run(inside, "k", 1)
     run(out, "k", 1)
+    wide_early()
     conv_grad(0, 1)
-    wide_grad(0, lambda m: x_ref[m], lambda m: ag_value(4, m))
-    one(mid, "k", 0, 3)
-    one(down, "k", 0, 2)
-    one(last, "k", 0, 1)
+    wide_late()
+    run(inside, "w", 1)
+    one(inside, "k", 0, 0)
+    one(inside, "k", 0, 1)
+    run(out, "w", 1)
     one(out, "k", 0, 0)
-    outs.append(put_out(4, sc.cv.at[...], conv_ref.at[...]))
+    one(out, "k", 0, 1)
+    one(last, "k", 0, 2)
+    one(inside, "k", 0, 2)
+    one(mid, "k", 0, 5)
+    one(down, "k", 0, 4)
+    one(last, "k", 0, 3)
+    one(inside, "k", 0, 3)
+    outs.append(put_out(4, sc.cin.at[...], conv_ref.at[...]))
     pair_sum("w", 0)
     run(up, "w", 0)
-    one(up, "w", 1, 1)
-    one(mid, "w", 1, 0)
-    one(down, "k", 0, 3)
-    one(last, "k", 0, 2)
-    one(out, "k", 0, 1)
+    one(up, "w", 2, 1)
+    one(out, "k", 0, 2)
+    one(down, "k", 0, 5)
+    one(last, "k", 0, 4)
+    one(inside, "k", 0, 4)
+    one(out, "k", 0, 3)
+    one(mid, "w", 0, 0)
+    one(mid, "w", 2, 0)
+    run(inside, "w", 3)
     run(out, "w", 3)
-    one(mid, "w", 0, 0)
-    one(last, "k", 0, 3)
-    one(out, "k", 0, 2)
     one(mid, "w", 0, 1)
+    one(last, "k", 0, 5)
+    one(inside, "k", 0, 5)
+    one(out, "k", 0, 4)
     one(down, "w", 0, 0)
     one(mid, "w", 0, 2)
-    one(down, "w", 1, 0)
-    one(out, "k", 0, 3)
     one(down, "w", 0, 1)
+    one(out, "k", 0, 5)
+    one(down, "w", 2, 0)
+    one(last, "w", 0, 0)
+    one(inside, "w", 0, 0)
     one(mid, "w", 0, 3)
-    one(last, "w", 0, 0)
-    one(mid, "w", 1, 1)
     one(down, "w", 0, 2)
     one(last, "w", 0, 1)
-    one(last, "w", 1, 0)
+    one(inside, "w", 0, 1)
     one(out, "w", 0, 0)
+    one(mid, "w", 2, 1)
+    one(last, "w", 2, 0)
+    one(inside, "w", 2, 0)
     one(down, "w", 0, 3)
     one(last, "w", 0, 2)
+    one(inside, "w", 0, 2)
     one(out, "w", 0, 1)
-    one(down, "w", 1, 1)
+    one(out, "w", 2, 0)
+    one(down, "w", 2, 1)
     one(last, "w", 0, 3)
-    run(out, "w", 2)
-    one(out, "w", 1, 0)
+    one(inside, "w", 0, 3)
     one(out, "w", 0, 2)
-    one(last, "w", 1, 1)
+    one(last, "w", 2, 1)
+    one(inside, "w", 2, 1)
+    for part in range(4):
+        one(step_sibling, "k", 0, part)
     one(out, "w", 0, 3)
-    one(out, "w", 1, 1)
+    one(step_sibling, "k", 0, 4)
+    one(step_sibling, "k", 0, 5)
+    one(out, "w", 2, 1)
+    run(step_sibling, "w", 3)
     gains_done()
-    run(step_sibling, "w", 3)
     run(step_sibling, "k", 1)
-    run(step_sibling, "k", 0)
     run(step_sibling, "w", 2)
     run(step_sibling, "w", 1)
     one(step_sibling, "w", 0, 0)
@@ -1347,11 +1512,12 @@
     for s in (3, 2, 1):
         run(step_done, "w", s)
     final = of("w", 0)
+    for it in final[2:]:
+        step_sibling(it)
+    for it in final:
+        step_rest(it)
     for group, part in enumerate((final[:-1], final[-1:]) if len(final) > 1 else (final,)):
         first, count = part[0].r0, sum(it.nr for it in part)
-        for it in part:
-            if it.i >= final[0].i + 2:
-                step_sibling(it)
         for it in part:
             step_done(it)
         part_rows_of = pl.ds(first, count)

time: 196 us -> 193 us (0.985)
  Pallas kernels: 195 us -> 191 us
    pallas_call x1, Pallas kernels: 189 us -> 184 us  [local(): pl.pallas_call(functools.partial(kernel, list(scratch), n_dp), out_shape=...]
where the time goes in v6:
time: 193 us; the launch traced here: 191 us
  Pallas kernels  191 us (99%)
    pallas_call x1, Pallas kernels, local(): pl.pallas_call(functools.partial(kernel, list(scratch), n_dp), out_shape=...  184 us
    pallas_call x1, Pallas kernels, cast_all(): pl.pallas_call(cast_kernel, in_specs=[anywhere] * 7, out_specs=[anywhere]...  6.44 us

profile of v6, /device:TPU:0, one launch (start us, length us, event | category | flops | bytes accessed | tf_op | source)
XLA Modules:
  0.0 191.4 jit_solution(17366985312174304407)
XLA Ops:
  0.6 184.2 %layers.1 = (bf16[2,384,512]{2,1,0:T(8,128)(2,1)}, bf16[2,384,512]{2,1,0:T(8,128)(2,1)}, bf16[2,384,512]{2,1,0:T(8,128)(2,1)}, bf16[4,2,256,512]{3,2,1,0:T(8,128...) custom-call(bf16[2,384,512]{2,1,0:T(8,128)(2,1)} %refs_0_.1, ...), custom_call_target="tpu_custom_call" | custom-call | tf_op jit(solution)/shard_map/layers/pallas_call | solution.py:1646
  184.8 6.4 %casts.1 = (bf16[2,384,512]{2,1,0:T(8,128)(2,1)}, f32[2,384,512]{2,1,0:T(8,128)}, f32[2048,512]{1,0:T(8,128)}, f32[2304,512]{1,0:T(8,128)}, f32[1,2,512]{2,1,0:T(2,128)}, /*index=5*/f32[1,2,1024]{2,1,0:T(2,128)}) custom-call(bf16[2,384,512]{2,1,0:T(8,128)(2,1)} %get-tuple-element.19.mixed, bf16[2,384,512]{2,1,0:T(8,128)(2,1)} %get-tuple-element.20.gpre, ...), custom_call_target="tpu_custom_call" | custom-call | tf_op jit(solution)/shard_map/casts/pallas_call | solution.py:1604

commit v7 on v6

--- a/solution.py
+++ b/solution.py
@@ -1433,11 +1433,11 @@
     one(last, "k", 0, 1)
     one(mid, "k", 0, 4)
     one(down, "k", 0, 3)
-    run(inside, "k", 1)
-    run(out, "k", 1)
     wide_early()
     conv_grad(0, 1)
     wide_late()
+    run(inside, "k", 1)
+    run(out, "k", 1)
     run(inside, "w", 1)
     one(inside, "k", 0, 0)
     one(inside, "k", 0, 1)
@@ -1533,8 +1533,8 @@
 
 
 def cast_pieces(rows):
-    pieces = [("taps", pl.ds(576 * i, 576)) for i in range(4)]
-    pieces += [("wide", pl.ds(512 * i, 512)) for i in range(4)]
+    pieces = [("taps", pl.ds(1152 * i, 1152)) for i in range(2)]
+    pieces += [("wide", pl.ds(1024 * i, 1024)) for i in range(2)]
     return pieces + [("stream", m) for m in range(2)]
 
 

time: 193 us -> 193 us (level)
  no operation moved by 1% of the time
where the time goes in v7:
time: 193 us; the launch traced here: 192 us
  Pallas kernels  191 us (99%)
    pallas_call x1, Pallas kernels, local(): pl.pallas_call(functools.partial(kernel, list(scratch), n_dp), out_shape=...  185 us
    pallas_call x1, Pallas kernels, cast_all(): pl.pallas_call(cast_kernel, in_specs=[anywhere] * 7, out_specs=[anywhere]...  5.84 us

profile of v7, /device:TPU:0, one launch (start us, length us, event | category | flops | bytes accessed | tf_op | source)
XLA Modules:
  0.0 191.6 jit_solution(12724315559278947149)
XLA Ops:
  0.6 185.0 %layers.1 = (bf16[2,384,512]{2,1,0:T(8,128)(2,1)}, bf16[2,384,512]{2,1,0:T(8,128)(2,1)}, bf16[2,384,512]{2,1,0:T(8,128)(2,1)}, bf16[4,2,256,512]{3,2,1,0:T(8,128...) custom-call(bf16[2,384,512]{2,1,0:T(8,128)(2,1)} %refs_0_.1, ...), custom_call_target="tpu_custom_call" | custom-call | tf_op jit(solution)/shard_map/layers/pallas_call | solution.py:1646
  185.6 5.8 %casts.1 = (bf16[2,384,512]{2,1,0:T(8,128)(2,1)}, f32[2,384,512]{2,1,0:T(8,128)}, f32[2048,512]{1,0:T(8,128)}, f32[2304,512]{1,0:T(8,128)}, f32[1,2,512]{2,1,0:T(2,128)}, /*index=5*/f32[1,2,1024]{2,1,0:T(2,128)}) custom-call(bf16[2,384,512]{2,1,0:T(8,128)(2,1)} %get-tuple-element.19.mixed, bf16[2,384,512]{2,1,0:T(8,128)(2,1)} %get-tuple-element.20.gpre, ...), custom_call_target="tpu_custom_call" | custom-call | tf_op jit(solution)/shard_map/casts/pallas_call | solution.py:1604

commit v8 on v7

--- a/solution.py
+++ b/solution.py
@@ -136,7 +136,7 @@
         ex_r=dma((2, 2)),
         st_s=dma((2, 2)),
         st_r=dma((2, 2)),
-        pw_s=dma((6,)),
+        pw_s=dma((2,)),
         pw_r=dma((6,)),
         it_s=dma((6,)),
         one_r=dma((items,)),
@@ -874,7 +874,7 @@
             src, dst, i = sc.dw.at[t, 1 - c], sc.prw.at[t], t
         else:
             src, dst, i = sc.dk.at[t, half_rows(1 - c)], sc.prk.at[t], 4 + t
-        return remote(src, dst, sc.pw_s.at[i], sc.pw_r.at[i], sibling)
+        return remote(src, dst, sc.pw_s.at[0 if kind == "w" else 1], sc.pw_r.at[i], sibling)
 
     def pair_sum(kind, t):
         pair_copy(kind, t).wait_recv()
@@ -1165,8 +1165,9 @@
         pl.when(p == (it.t if it.kind == "w" else 2 * it.t + 1 - c))(go)
 
     def finish_grads():
+        bytes_wait(sc.dw.at[:, 0], sc.pw_s.at[0])
+        bytes_wait(sc.dk.at[0], sc.pw_s.at[1])
         for kind, t in [("w", s) for s in range(4)] + [("k", layer) for layer in range(2)]:
-            pair_copy(kind, t).wait_send()
             whole = next(it for it in items if it.kind == kind and it.t == t)
             sends = sc.it_s.at[tile_sem(whole)]
             half = tile(whole, "zs").at[t]

time: 193 us -> 193 us (level)
  no operation moved by 1% of the time
where the time goes in v8:
time: 193 us; the launch traced here: 192 us
  Pallas kernels  191 us (99%)
    pallas_call x1, Pallas kernels, local(): pl.pallas_call(functools.partial(kernel, list(scratch), n_dp), out_shape=...  185 us
    pallas_call x1, Pallas kernels, cast_all(): pl.pallas_call(cast_kernel, in_specs=[anywhere] * 7, out_specs=[anywhere]...  5.84 us

profile of v8, /device:TPU:0, one launch (start us, length us, event | category | flops | bytes accessed | tf_op | source)
XLA Modules:
  0.0 191.6 jit_solution(5625887568948689116)
XLA Ops:
  0.6 184.9 %layers.1 = (bf16[2,384,512]{2,1,0:T(8,128)(2,1)}, bf16[2,384,512]{2,1,0:T(8,128)(2,1)}, bf16[2,384,512]{2,1,0:T(8,128)(2,1)}, bf16[4,2,256,512]{3,2,1,0:T(8,128...) custom-call(bf16[2,384,512]{2,1,0:T(8,128)(2,1)} %refs_0_.1, ...), custom_call_target="tpu_custom_call" | custom-call | tf_op jit(solution)/shard_map/layers/pallas_call | solution.py:1647
  185.6 5.8 %casts.1 = (bf16[2,384,512]{2,1,0:T(8,128)(2,1)}, f32[2,384,512]{2,1,0:T(8,128)}, f32[2048,512]{1,0:T(8,128)}, f32[2304,512]{1,0:T(8,128)}, f32[1,2,512]{2,1,0:T(2,128)}, /*index=5*/f32[1,2,1024]{2,1,0:T(2,128)}) custom-call(bf16[2,384,512]{2,1,0:T(8,128)(2,1)} %get-tuple-element.19.mixed, bf16[2,384,512]{2,1,0:T(8,128)(2,1)} %get-tuple-element.20.gpre, ...), custom_call_target="tpu_custom_call" | custom-call | tf_op jit(solution)/shard_map/casts/pallas_call | solution.py:1605
